TPU v7x, 256 devices: a whole 4x4x8 slice. The times are simulated.
256 devices in a mesh: row: 8 (over y, x_hi), col: 32 (over z, x_lo, core).
Axes of the slice: x: 4 (x_hi: 2, x_lo: 2; x = x_hi * 2 + x_lo), y: 4, z: 8, core: 2. Of those that a mesh axis runs over, the one named last changes fastest.
Arguments:
- scalar_field: float32 [256, 256, 2048], P('col', 'row'), may hold values from -1.2 to 1.2
- reaction: float32 [256, 256, 2048], P('col', 'row'), may hold values from 0.5 to 4
- x_faces: float32 [2048], replicated, may hold values from 0.5 to 4
- y_faces: float32 [256], replicated, may hold values from 0.5 to 4
- z_faces: float32 [256], replicated, may hold values from 0.5 to 4
- x_inverse: float32 [16, 128, 128], replicated, may hold values from 0 to 1, as said below
- y_inverse: float32 [2, 128, 128], replicated, may hold values from 0 to 1, as said below
- z_inverse: float32 [2, 128, 128], replicated, may hold values from 0 to 1, as said below
Outputs:
- advanced: float32 [256, 256, 2048], P('col', 'row')
Inputs may be any that keep to these rules, and one draw needn't show every extreme that they name: x_inverse[c] is, up to float32 rounding, the inverse of the block of rows and columns c * 128 to (c + 1) * 128 - 1 of the matrix I - 500 A_x along one x line. y_inverse[c] is, up to float32 rounding, the inverse of the block of rows and columns c * 128 to (c + 1) * 128 - 1 of the matrix I - 500 A_y along one y line. z_inverse[c] is, up to float32 rounding, the inverse of the block of rows and columns c * 128 to (c + 1) * 128 - 1 of the matrix I - 500 A_z along one z line.
All inputs are finite; a program needn't handle non-finite values.
Results may differ from a plain program's by a relative error of at most 0.0003.
Values sent between devices are 32-bit elements; how exact they have to be, the bound alone decides.
No kernel may reach another device: no remote copies, remote signals or barrier semaphores. Data moves between devices by JAX's collectives and lax.ppermute only.
A program may use at most 64 MiB of HBM per device.

v0:
```python
import jax
import jax.numpy as jnp
from jax import lax
from jax.sharding import PartitionSpec as P

implicit_weight = 0.5
time_step = 1000.0


def with_halo(shard, sides, width):
    for axis, dim in sides:
        size, length = (lax.axis_size(axis), shard.shape[dim])
        up = [(i, (i + 1) % size) for i in range(size - 1)]
        down = [(j, i) for i, j in up]
        last = lax.slice_in_dim(shard, length - width, length, axis=dim)
        leading = lax.slice_in_dim(shard, 0, width, axis=dim)
        before = lax.ppermute(last, axis, up)
        after = lax.ppermute(leading, axis, down)
        shard = jnp.concatenate([before, shard, after], axis=dim)
    return shard


def shift_lower(values, line_axis):
    length = values.shape[line_axis]
    first_slot = jnp.zeros_like(lax.slice_in_dim(values, 0, 1, axis=line_axis))
    return jnp.concatenate(
        [first_slot, lax.slice_in_dim(values, 0, length - 1, axis=line_axis)], axis=line_axis
    )


def shift_upper(values, line_axis):
    length = values.shape[line_axis]
    last_slot = jnp.zeros_like(lax.slice_in_dim(values, 0, 1, axis=line_axis))
    return jnp.concatenate(
        [lax.slice_in_dim(values, 1, length, axis=line_axis), last_slot], axis=line_axis
    )


def apply_line(values, face_values, line_axis):
    spread = [1, 1, 1]
    spread[line_axis] = values.shape[line_axis]
    face_here = face_values.reshape(spread)
    face_next = jnp.concatenate([face_values[1:], jnp.zeros((1,), face_values.dtype)]).reshape(
        spread
    )
    lower_value = shift_lower(values, line_axis)
    upper_value = shift_upper(values, line_axis)
    return face_next * (upper_value - values) - face_here * (values - lower_value)


def invert_small(matrix):
    order = matrix.shape[0]
    joined = jnp.concatenate([matrix, jnp.eye(order, dtype=matrix.dtype)], axis=1)

    def sweep(step_index, current):
        pivot_row = lax.dynamic_index_in_dim(current, step_index, 0, keepdims=False)
        pivot_row = pivot_row / lax.dynamic_index_in_dim(pivot_row, step_index, 0, keepdims=False)
        pivot_column = lax.dynamic_slice_in_dim(current, step_index, 1, 1)
        current = current - pivot_column * pivot_row[None, :]
        return lax.dynamic_update_index_in_dim(current, pivot_row, step_index, 0)

    joined = lax.fori_loop(0, order, sweep, joined)
    return joined[:, order:]


def reduced_inverse(inverse, coupling_before, coupling_after):
    groups, block_width = (inverse.shape[0], inverse.shape[1])
    order = 2 * groups
    group_index = jnp.arange(groups)
    lead_rows = 2 * group_index
    trail_rows = 2 * group_index + 1
    prev_cols = jnp.maximum(2 * group_index - 1, 0)
    next_cols = jnp.minimum(2 * group_index + 2, order - 1)
    coupled = jnp.zeros((order, order), inverse.dtype)
    coupled = coupled.at[lead_rows, prev_cols].add(coupling_before * inverse[:, 0, 0])
    coupled = coupled.at[lead_rows, next_cols].add(coupling_after * inverse[:, 0, block_width - 1])
    coupled = coupled.at[trail_rows, prev_cols].add(
        coupling_before * inverse[:, block_width - 1, 0]
    )
    coupled = coupled.at[trail_rows, next_cols].add(
        coupling_after * inverse[:, block_width - 1, block_width - 1]
    )
    return invert_small(jnp.eye(order, dtype=inverse.dtype) - coupled)


def line_solve(right_side, inverse, face_values, line_axis):
    groups, block_width = (inverse.shape[0], inverse.shape[1])
    dims_full = right_side.shape
    blocked = right_side.reshape(
        dims_full[:line_axis] + (groups, block_width) + dims_full[line_axis + 1 :]
    )
    others = ["u", "v"]
    source = "".join(others[:line_axis] + ["c", "j"] + others[line_axis:])
    target = "".join(others[:line_axis] + ["c", "i"] + others[line_axis:])
    inside = jnp.einsum(
        "cij," + source + "->" + target, inverse, blocked, precision=lax.Precision.HIGHEST
    )
    leading = lax.index_in_dim(inside, 0, line_axis + 1, keepdims=False)
    trailing = lax.index_in_dim(inside, block_width - 1, line_axis + 1, keepdims=False)
    coupling = implicit_weight * time_step * face_values[block_width::block_width]
    nothing = jnp.zeros((1,), face_values.dtype)
    coupling_before = jnp.concatenate([nothing, coupling])
    coupling_after = jnp.concatenate([coupling, nothing])
    reduced = reduced_inverse(inverse, coupling_before, coupling_after)
    interface = jnp.stack([leading, trailing], axis=line_axis + 1)
    interface = interface.reshape(
        dims_full[:line_axis] + (2 * groups,) + dims_full[line_axis + 1 :]
    )
    end_source = "".join(others[:line_axis] + ["j"] + others[line_axis:])
    end_target = "".join(others[:line_axis] + ["i"] + others[line_axis:])
    solved = jnp.einsum(
        "ij," + end_source + "->" + end_target, reduced, interface, precision=lax.Precision.HIGHEST
    )
    solved = solved.reshape(dims_full[:line_axis] + (groups, 2) + dims_full[line_axis + 1 :])
    first_values = lax.index_in_dim(solved, 0, line_axis + 1, keepdims=False)
    last_values = lax.index_in_dim(solved, 1, line_axis + 1, keepdims=False)
    prev_last = shift_lower(last_values, line_axis)
    next_first = shift_upper(first_values, line_axis)
    spike_shape = [1, 1, 1, 1]
    spike_shape[line_axis] = groups
    spike_shape[line_axis + 1] = block_width
    left_spike = (coupling_before[:, None] * inverse[:, :, 0]).reshape(spike_shape)
    right_spike = (coupling_after[:, None] * inverse[:, :, block_width - 1]).reshape(spike_shape)
    result = (
        inside
        + left_spike * jnp.expand_dims(prev_last, line_axis + 1)
        + right_spike * jnp.expand_dims(next_first, line_axis + 1)
    )
    return result.reshape(dims_full)


def body(scalar_field, reaction, x_faces, y_faces, z_faces, x_inverse, y_inverse, z_inverse):
    z_cells, y_cells, x_cells = scalar_field.shape
    padded = with_halo(scalar_field, (("row", 1), ("col", 0)), 1)
    nothing = jnp.zeros((1,), jnp.float32)
    y_padded = jnp.concatenate([y_faces, nothing])
    z_padded = jnp.concatenate([z_faces, nothing])
    y_start = lax.axis_index("row") * y_cells
    z_start = lax.axis_index("col") * z_cells
    y_here = lax.dynamic_slice_in_dim(y_padded, y_start, y_cells).reshape(1, y_cells, 1)
    y_next = lax.dynamic_slice_in_dim(y_padded, y_start + 1, y_cells).reshape(1, y_cells, 1)
    z_here = lax.dynamic_slice_in_dim(z_padded, z_start, z_cells).reshape(z_cells, 1, 1)
    z_next = lax.dynamic_slice_in_dim(z_padded, z_start + 1, z_cells).reshape(z_cells, 1, 1)
    y_term = y_next * (padded[1:-1, 2:, :] - scalar_field) - y_here * (
        scalar_field - padded[1:-1, :-2, :]
    )
    z_term = z_next * (padded[2:, 1:-1, :] - scalar_field) - z_here * (
        scalar_field - padded[:-2, 1:-1, :]
    )
    x_term = apply_line(scalar_field, x_faces, 2)
    source = reaction * scalar_field * (1.0 - scalar_field * scalar_field)
    change = time_step * (x_term + y_term + z_term + source)
    first_section = line_solve(change, x_inverse, x_faces, 2)
    section_y = lax.all_to_all(first_section, "row", split_axis=2, concat_axis=1, tiled=True)
    second_section = line_solve(section_y, y_inverse, y_faces, 1)
    section_z = lax.all_to_all(second_section, "col", split_axis=1, concat_axis=0, tiled=True)
    total_change = line_solve(section_z, z_inverse, z_faces, 0)
    returned = lax.all_to_all(
        lax.all_to_all(total_change, "col", split_axis=0, concat_axis=1, tiled=True),
        "row",
        split_axis=1,
        concat_axis=2,
        tiled=True,
    )
    return scalar_field + returned


def solution(mesh):
    in_specs = (P("col", "row", None), P("col", "row", None), P(), P(), P(), P(), P(), P())
    out_specs = P("col", "row", None)
    return jax.shard_map(body, mesh=mesh, in_specs=in_specs, out_specs=out_specs, check_vma=False)
```

profile of v0, /device:TPU:2, one launch (start us, length us, event | category | flops | bytes accessed | tf_op | source)
XLA Modules:
  0.0 384.9 jit_solution(6545499612655248361)
XLA Ops:
  0.0 1.9 fusion.73
  1.9 1.3 collective-permute-start
  3.2 6.7 %collective-permute-start.1 = (f32[8,1,2048]{2,1,0:T(1,128)}, f32[8,1,2048]{2,1,0:T(1,128)}, u32[]{:S(2)}, u32[]{:S(2)}) collective-permute-start(f32[8,1,2048]{2,1,0:T(1,128)} %get-tuple-element.193), channel_id=1, source_target_pairs={{0,32},{32,64},{64,96},{96,128},{128,160},{160,192},{192,224},{1,3... | collective-permute-start | bytes 196616 | tf_op jit(solution)/shard_map/ppermute | solution.py:17
  9.9 5.1 %fusion.72 = (f32[8,32,2047]{2,1,0:T(8,128)}, f32[8,32,2047]{2,1,0:T(8,128)}) fusion(f32[8,32,2048]{2,1,0:T(8,128)} %param.14), kind=kLoop, calls=%fused_computation.183 | loop fusion | bytes 8384512 | tf_op jit(solution)/shard_map/slice | solution.py:35
  15.7 1.6 fusion.74
  22.5 1.3 scatter_fusion
  23.9 1.4 scatter_fusion.1
  25.2 1.4 scatter_fusion.2
  26.6 1.4 scatter_fusion.3
  28.1 66.6 %while.39 = (s32[]{:T(128)}, f32[32,64]{1,0:T(8,128)S(1)}, s32[]{:T(128)}, s32[]{:T(128)}, s32[]{:T(128)}, /*index=5*/s32[]{:T(128)}) while((s32[]{:T(128)}, f32[32,64]{1,0:T(8,128)S(1)}, s32[]{:T(128)}, s32[]{:T(128)}, s32[]{:T(128)}, /*index=5*/s32[]{:T(128)}) %tuple.111), condition=%wide.region_5.6_spmd, body=%wide.region_4.5_spmd.sunk | while | flops 4228 | bytes 18697 | solution.py:62
  98.2 1.4 scatter_fusion.4
  99.6 1.3 fusion.61
  100.8 1.3 scatter_fusion.5
  103.4 1.2 broadcast_multiply_fusion.2
  106.5 1.7 pad_maximum_fusion.11
  108.1 1.9 collective-permute-start.2
  110.0 2.9 collective-permute-start.3
  113.7 1.6 copy.171
  115.3 1.6 copy.172
  117.5 3.2 collective-permute-done.3
  120.8 7.4 %fusion.28 = f32[8,32,16,128]{3,1,0,2:T(8,128)S(1)} fusion(f32[16,128,128]{2,1,0:T(8,128)S(1)} %copy-done.3, f32[8,32,2048]{2,1,0:T(8,128)S(1)} %copy-done, f32[1,34,2048]{2,1,0:T(8,128)} %collective-permute-done.3, f32[8,1,2048]{2,1,0:T(1,128)S(1)} %collective-permute-done, f32[8,1,2048]{2,1,0:T(1,128)} %collective-permute-done.1, ...), kind=kOutput, calls=%fused_computation.58 | convolution fusion | flops 821559296 | bytes 12237120 | tf_op jit(solution)/shard_map/cij,uvcj->uvci/dot_general | solution.py:95
  129.5 2.0 pad_maximum_fusion.8
  131.5 2.4 copy.129
  134.3 3.4 multiply_add_fusion.2
  137.7 6.3 %copy.165 = f32[8,32,16,128]{1,0,3,2:T(8,128)} copy(f32[8,32,16,128]{3,1,0,2:T(8,128)} %multiply_add_fusion.2) | data formatting | bytes 4194304 | tf_op jit(solution)/shard_map/reshape | solution.py:129
  144.0 8.6 %reshape.391 = f32[8,1,65536]{2,1,0:T(1,128)} reshape(f32[2048,8,32]{2,1,0:T(8,128)} %bitcast.134) | data formatting | bytes 4194304
  152.5 6.9 %all-to-all-start = ((f32[8,1,65536]{2,1,0:T(1,128)}), f32[8,1,65536]{2,1,0:T(1,128)}, u32[]{:S(2)}, u32[]{:S(2)}) async-start(f32[8,1,65536]{2,1,0:T(1,128)} %reshape.391), calls=%async_computation | async-start | bytes 4194304 | tf_op jit(solution)/shard_map/all_to_all | solution.py:154
  159.5 8.7 %while.40 = (s32[]{:T(128)}, f32[4,8]{1,0:T(4,128)S(1)}, s32[]{:T(128)}, s32[]{:T(128)}, s32[]{:T(128)}, /*index=5*/s32[]{:T(128)}) while((s32[]{:T(128)}, f32[4,8]{1,0:T(4,128)S(1)}, s32[]{:T(128)}, s32[]{:T(128)}, s32[]{:T(128)}, /*index=5*/s32[]{:T(128)}) %tuple.114), condition=%wide.region_11.12_spmd, body=%wide.region_10.11_spmd.sunk | while | flops 84 | bytes 665 | solution.py:62
  168.1 18.2 %all-to-all-done = f32[8,1,65536]{2,1,0:T(1,128)} async-done(((f32[8,1,65536]{2,1,0:T(1,128)}), f32[8,1,65536]{2,1,0:T(1,128)}, u32[]{:S(2)}, u32[]{:S(2)}) %all-to-all-start) | async-done | bytes 2097184 | tf_op jit(solution)/shard_map/all_to_all | solution.py:154
  186.8 8.5 %reduce.38 = f32[8,65536]{1,0:T(8,128)} reduce(f32[8,1,65536]{2,1,0:T(1,128)} %all-to-all-done, f32[]{:T(128)} %broadcast.1002), dimensions={1}, to_apply=%all_to_all.48.reduce_sub_computation | reduce | bytes 4194308 | tf_op jit(solution)/shard_map/all_to_all | solution.py:154
  195.3 7.6 %reshape.392 = f32[2048,8,32]{2,1,0:T(8,128)} reshape(f32[8,65536]{1,0:T(8,128)} %reduce.38) | data formatting | bytes 4194304
  202.9 6.4 %copy.138 = f32[8,8,32,256]{3,2,1,0:T(8,128)} copy(f32[8,8,32,256]{2,0,3,1:T(8,128)} %bitcast.135) | data formatting | bytes 4194304 | tf_op jit(solution)/shard_map/all_to_all | solution.py:154
  209.3 3.6 fusion.22
  212.9 1.3 copy-done.2
  214.7 2.1 multiply_add_fusion.1
  217.0 2.5 copy.145
  219.6 10.5 %all-to-all-start.1 = ((f32[8,256,256]{2,0,1:T(8,128)}), f32[8,256,256]{2,0,1:T(8,128)}, u32[]{:S(2)}, u32[]{:S(2)}) async-start(f32[8,256,256]{2,0,1:T(8,128)} %copy.145), calls=%async_computation.1 | async-start | bytes 4194304 | tf_op jit(solution)/shard_map/all_to_all | solution.py:156
  230.0 8.7 %while.41 = (s32[]{:T(128)}, f32[4,8]{1,0:T(4,128)S(1)}, s32[]{:T(128)}, s32[]{:T(128)}, s32[]{:T(128)}, /*index=5*/s32[]{:T(128)}) while((s32[]{:T(128)}, f32[4,8]{1,0:T(4,128)S(1)}, s32[]{:T(128)}, s32[]{:T(128)}, s32[]{:T(128)}, /*index=5*/s32[]{:T(128)}) %tuple.117), condition=%wide.region_17.18_spmd, body=%wide.region_16.17_spmd.sunk | while | flops 84 | bytes 665 | solution.py:62
  239.1 41.2 %all-to-all-done.1 = f32[8,256,256]{2,0,1:T(8,128)} async-done(((f32[8,256,256]{2,0,1:T(8,128)}), f32[8,256,256]{2,0,1:T(8,128)}, u32[]{:S(2)}, u32[]{:S(2)}) %all-to-all-start.1) | async-done | bytes 2097184 | tf_op jit(solution)/shard_map/all_to_all | solution.py:156
  280.3 2.5 copy.147
  282.8 2.6 fusion.25
  286.2 1.2 copy.153
  287.5 56.1 %all_to_all.66 = f32[256,8,256]{2,1,0:T(8,128)S(1)} all-to-all(f32[256,8,256]{2,1,0:T(8,128)S(1)} %bitcast.139), channel_id=1, replica_groups=mesh['row'=8,'col'=32] {'col'}, dimensions={0} | all-to-all | bytes 4194304 | tf_op jit(solution)/shard_map/all_to_all | solution.py:159
  343.8 1.2 copy.155
  345.0 31.1 %all_to_all.67 = f32[8,256,256]{2,0,1:T(8,128)S(1)} all-to-all(f32[8,256,256]{2,0,1:T(8,128)S(1)} %copy.155), channel_id=1, replica_groups=mesh['row'=8,'col'=32] {'row'}, dimensions={1} | all-to-all | bytes 4194304 | tf_op jit(solution)/shard_map/all_to_all | solution.py:158
  376.1 2.5 copy.157
  378.6 2.7 all_to_all.61
  381.4 3.2 add.391
  (353 shorter events, 99.8 us)
Async XLA Ops:
  1.9 104.5 %collective-permute-start = (f32[8,1,2048]{2,1,0:T(1,128)}, f32[8,1,2048]{2,1,0:T(1,128)S(1)}, u32[]{:S(2)}, u32[]{:S(2)}) collective-permute-start(f32[8,1,2048]{2,1,0:T(1,128)} %get-tuple-element.194), channel_id=1, source_target_pairs={{32,0},{64,32},{96,64},{128,96},{160,128},{192,160},{224,192},{33,... | collective-permute-start | bytes 196616 | tf_op jit(solution)/shard_map/ppermute | solution.py:18
  3.2 103.2 %collective-permute-start.1 = (f32[8,1,2048]{2,1,0:T(1,128)}, f32[8,1,2048]{2,1,0:T(1,128)}, u32[]{:S(2)}, u32[]{:S(2)}) collective-permute-start(f32[8,1,2048]{2,1,0:T(1,128)} %get-tuple-element.193), channel_id=1, source_target_pairs={{0,32},{32,64},{64,96},{96,128},{128,160},{160,192},{192,224},{1,3... | collective-permute-start | bytes 196616 | tf_op jit(solution)/shard_map/ppermute | solution.py:17
  9.9 5.1 %copy-start.6 = (f32[2048]{0:T(1024)S(1)}, f32[2048]{0:T(1024)}, u32[]{:S(2)}) copy-start(f32[2048]{0:T(1024)} %param.16) | copy-start | bytes 24580
  9.9 5.3 %copy-start.3 = (f32[16,128,128]{2,1,0:T(8,128)S(1)}, f32[16,128,128]{2,1,0:T(8,128)}, u32[]{:S(2)}) copy-start(f32[16,128,128]{2,1,0:T(8,128)} %param.19) | copy-start | bytes 3145732
  15.7 1.8 copy-start.4
  15.7 2.7 copy-start.12
  15.7 3.2 copy-start.13
  23.9 70.8 %copy-start.5 = (f32[2,128,128]{2,1,0:T(8,128)S(1)}, f32[2,128,128]{2,1,0:T(8,128)}, u32[]{:S(2)}) copy-start(f32[2,128,128]{2,1,0:T(8,128)} %param.21) | copy-start | bytes 393220
  98.2 8.3 %copy-start = (f32[8,32,2048]{2,1,0:T(8,128)S(1)}, f32[8,32,2048]{2,1,0:T(8,128)}, u32[]{:S(2)}) copy-start(f32[8,32,2048]{2,1,0:T(8,128)} %param.14) | copy-start | bytes 6291460
  106.4 10.4 %copy-start.9 = (f32[16]{0:T(128)S(1)}, f32[16]{0:T(128)}, u32[]{:S(2)}) copy-start(f32[16]{0:T(128)} %get-tuple-element.209) | copy-start | bytes 196
  108.1 9.4 %collective-permute-start.2 = (f32[1,34,2048]{2,1,0:T(8,128)}, f32[1,34,2048]{2,1,0:T(8,128)}, u32[]{:S(2)}, u32[]{:S(2)}) collective-permute-start(f32[1,34,2048]{2,1,0:T(8,128)} %get-tuple-element.183), channel_id=1, source_target_pairs={{1,0},{2,1},{3,2},{4,3},{5,4},{6,5},{7,6},{8,7},{9,8},{10,9},{11,1... | collective-permute-start | bytes 835592 | tf_op jit(solution)/shard_map/ppermute | solution.py:18
  110.0 10.7 %collective-permute-start.3 = (f32[1,34,2048]{2,1,0:T(8,128)}, f32[1,34,2048]{2,1,0:T(8,128)}, u32[]{:S(2)}, u32[]{:S(2)}) collective-permute-start(f32[1,34,2048]{2,1,0:T(8,128)} %get-tuple-element.184), channel_id=1, source_target_pairs={{0,1},{1,2},{2,3},{3,4},{4,5},{5,6},{6,7},{7,8},{8,9},{9,10},{10,1... | collective-permute-start | bytes 835592 | tf_op jit(solution)/shard_map/ppermute | solution.py:17
  128.2 1.3 copy-start.1
  152.5 33.8 %all-to-all-start = ((f32[8,1,65536]{2,1,0:T(1,128)}), f32[8,1,65536]{2,1,0:T(1,128)}, u32[]{:S(2)}, u32[]{:S(2)}) async-start(f32[8,1,65536]{2,1,0:T(1,128)} %reshape.391), calls=%async_computation | async-start | bytes 4194304 | tf_op jit(solution)/shard_map/all_to_all | solution.py:154
  209.3 5.4 %copy-start.7 = (f32[2,128]{1,0:T(2,128)S(1)}, f32[2,128]{1,0:T(2,128)}, u32[]{:S(2)}) copy-start(f32[2,128]{1,0:T(2,128)} %broadcast_multiply_fusion.2) | copy-start | bytes 3076
  209.3 5.4 %copy-start.8 = (f32[2,128]{1,0:T(2,128)S(1)}, f32[2,128]{1,0:T(2,128)}, u32[]{:S(2)}) copy-start(f32[2,128]{1,0:T(2,128)} %broadcast_multiply_fusion.3) | copy-start | bytes 3076
  212.9 1.3 copy-start.2
  219.6 19.4 %copy-start.11 = (f32[2]{0:T(128)S(1)}, f32[2]{0:T(128)}, u32[]{:S(2)}) copy-start(f32[2]{0:T(128)} %get-tuple-element.219) | copy-start | bytes 28
  219.6 19.5 %copy-start.10 = (f32[2]{0:T(128)S(1)}, f32[2]{0:T(128)}, u32[]{:S(2)}) copy-start(f32[2]{0:T(128)} %get-tuple-element.217) | copy-start | bytes 28
  219.6 60.8 %all-to-all-start.1 = ((f32[8,256,256]{2,0,1:T(8,128)}), f32[8,256,256]{2,0,1:T(8,128)}, u32[]{:S(2)}, u32[]{:S(2)}) async-start(f32[8,256,256]{2,0,1:T(8,128)} %copy.145), calls=%async_computation.1 | async-start | bytes 4194304 | tf_op jit(solution)/shard_map/all_to_all | solution.py:156
where the time goes:
time: 392 us; the launch traced here: 385 us
  local copies, waits for them, and re-layouts  96.2 us (25%)
  other arithmetic  91.3 us (23%)
  blocking collectives  87.2 us (22%)
  waiting for transfers between devices  62.6 us (16%)
  starting transfers between devices  30.1 us (8%)
  matrix products  14.3 us (4%)
    all_to_all x1, blocking collectives, body(): lax.all_to_all(total_change, 'col', split_axis=0, concat_axis=1, tiled=True)  56.1 us
    all_to_all x1, waiting for transfers between devices, body(): lax.all_to_all(second_section, 'col', split_axis=1, concat_axis=0, tiled=...  41.2 us
    all_to_all x1, blocking collectives, body(): lax.all_to_all(lax.all_to_all(total_change, 'col', split_axis=0, concat_a...  31.1 us
    dynamic_slice x40, local copies, waits for them, and re-layouts, sweep(): lax.dynamic_index_in_dim(pivot_row, step_index, 0, keepdims=False)  23.8 us
    mul x40, other arithmetic, sweep(): current = current - pivot_column * pivot_row[None, :]  23.7 us
    div x40, other arithmetic, sweep(): pivot_row / lax.dynamic_index_in_dim(pivot_row, step_index, 0, keepdims=F...  23.7 us
    unnamed x38, local copies, waits for them, and re-layouts  21.2 us
    all_to_all x1, waiting for transfers between devices, body(): lax.all_to_all(first_section, 'row', split_axis=2, concat_axis=1, tiled=T...  18.2 us
  transfers between devices with their start and end apart: 6, of which 3 were waited for; matrix products, arithmetic and copies ran while one was open for 30% of the time, Pallas kernels for 0%

commit v1 on v0

v1 whole, which is shorter than its diff:
```python
import functools

import jax
import jax.numpy as jnp
from jax import lax
from jax.experimental import pallas as pl
from jax.experimental.pallas import tpu as pltpu
from jax.sharding import PartitionSpec as P

F32 = jnp.float32
half_step = 500.0
time_step = 1000.0
LANES = 128


def dot(left, right):
    return lax.dot_general(
        left,
        right,
        (((1,), (0,)), ((), ())),
        precision=lax.Precision.HIGHEST,
        preferred_element_type=F32,
    )


def dot_t(left, right):
    return lax.dot_general(
        left,
        right,
        (((1,), (1,)), ((), ())),
        precision=lax.Precision.HIGHEST,
        preferred_element_type=F32,
    )


def iota(shape, dim):
    return lax.broadcasted_iota(jnp.int32, shape, dim)


def joint(g_ref, faces_ref):
    b = half_step * faces_ref[0:1, 128:129]
    g0 = g_ref[0, 127:128, 127:128]
    g1 = g_ref[1, 0:1, 0:1]
    den = 1.0 - b * b * g0 * g1
    return b * b * g1 / den, b * b * g0 / den, b / den


def line_block(g_ref, faces_ref, start, size):
    alpha0, alpha1, _ = joint(g_ref, faces_ref)
    group = start // 128
    offset = start - group * 128
    rows = g_ref[group, pl.ds(pl.multiple_of(offset, size), size), :]
    low = group == 0
    edge_row = jnp.where(low, g_ref[0, 127:128, :], g_ref[1, 0:1, :])
    edge_col = jnp.where(low, rows[:, 127:128], rows[:, 0:1])
    alpha = jnp.where(low, alpha0, alpha1)
    block = rows + (alpha * edge_col) * edge_row
    return pltpu.roll(block, lax.rem(128 - offset, 128), 1)


def element(g_ref, joined, i, j):
    alpha0, alpha1, beta = joined
    gi, gj = i // 128, j // 128
    li, lj = i % 128, j % 128
    ei, ej = (0 if gi else 127), (0 if gj else 127)
    across = g_ref[gi, li : li + 1, ei : ei + 1] * g_ref[gj, ej : ej + 1, lj : lj + 1]
    if gi == gj:
        alpha = alpha1 if gi else alpha0
        return g_ref[gi, li : li + 1, lj : lj + 1] + alpha * across
    return beta * across


def call(kernel, out_shape, flops, nbytes, name, **kw):
    return pl.pallas_call(
        kernel,
        out_shape=out_shape,
        name=name,
        compiler_params=pltpu.CompilerParams(vmem_limit_bytes=48 * 1024 * 1024),
        cost_estimate=pl.CostEstimate(flops=flops, bytes_accessed=nbytes, transcendentals=0),
        **kw,
    )


def explicit_kernel(u_ref, r_ref, xf_ref, gy_ref, yf_ref, a_ref, buf_ref, w_ref):
    z = pl.program_id(0)
    cells = u_ref.shape[1]
    width = u_ref.shape[2]

    @pl.when(z == 0)
    def _():
        block = line_block(gy_ref, yf_ref, lax.axis_index("row") * cells, cells)
        last = block[:, cells - 1 : cells] / block[cells - 1 : cells, cells - 1 : cells]
        first = block[:, 0:1] / block[0:1, 0:1]
        w_ref[0] = jnp.broadcast_to(last, (cells, LANES))
        w_ref[1] = jnp.broadcast_to(first, (cells, LANES))

    u = u_ref[0]
    here = xf_ref[...]
    lane = iota((1, width), 1)
    after = jnp.where(lane == width - 1, 0.0, pltpu.roll(here, width - 1, 1))
    lower = jnp.where(iota((cells, width), 1) == 0, 0.0, pltpu.roll(u, 1, 1))
    upper = pltpu.roll(u, width - 1, 1)
    x_term = after * (upper - u) - here * (u - lower)
    a = time_step * (x_term + r_ref[0] * u * (1.0 - u * u)) + 4.0 * u
    a_ref[0] = a
    dests, span = buf_ref.shape[0], buf_ref.shape[2]
    for d in range(dests):
        for k in range(2):
            w = w_ref[k, :, 0:1]
            for f, field in enumerate((a, u)):
                part = field[:, d * span : (d + 1) * span]
                row = jnp.sum(w * part, axis=0, keepdims=True)
                buf_ref[d, pl.ds(z + 16 * k + 8 * f, 1), :] = row


def coef_kernel(gy_ref, yf_ref, gz_ref, zf_ref, yc_ref, zc_ref):
    for g_ref, f_ref, out_ref, count in ((gy_ref, yf_ref, yc_ref, 8), (gz_ref, zf_ref, zc_ref, 16)):
        joined = joint(g_ref, f_ref)
        size = 256 // count
        m = functools.partial(element, g_ref, joined)
        out_ref[...] = jnp.zeros_like(out_ref)
        for c in range(count):
            b, e = c * size, c * size + size - 1
            if c > 0:
                ee = m(e, e - size) / m(e, e)
                be = m(b, b - 1)
                out_ref[c : c + 1, :] = jnp.broadcast_to(ee, (1, LANES))
                out_ref[count + c : count + c + 1, :] = jnp.broadcast_to(be, (1, LANES))
            if c < count - 1:
                bb = m(b, b + size) / m(b, b)
                eb = m(e, e + 1)
                out_ref[2 * count + c : 2 * count + c + 1, :] = jnp.broadcast_to(bb, (1, LANES))
                out_ref[3 * count + c : 3 * count + c + 1, :] = jnp.broadcast_to(eb, (1, LANES))


def scan_kernel(in_ref, c_ref, out_ref):
    count, rows, span = in_ref.shape
    half = rows // 2

    def coef(k):
        return c_ref[k : k + 1, 0:1]

    zero = jnp.zeros((half, span), F32)
    out_ref[0, :half, :] = zero
    out_ref[count - 1, half:, :] = zero
    below = above = None
    for s in range(count - 1):
        own = in_ref[s, :half, :]
        below = own if s == 0 else own + coef(s) * below
        out_ref[s + 1, :half, :] = coef(count + s + 1) * below
        t = count - 1 - s
        own = in_ref[t, half:, :]
        above = own if s == 0 else own + coef(2 * count + t) * above
        out_ref[t - 1, half:, :] = coef(3 * count + t - 1) * above


def local_kernel(a_ref, u_ref, gy_ref, yf_ref, gz_ref, zf_ref, l_ref, zp_ref, k_ref):
    planes, cells = a_ref.shape[0], a_ref.shape[1]
    local = planes * cells

    @pl.when(pl.program_id(0) == 0)
    def _():
        dy = line_block(gy_ref, yf_ref, lax.axis_index("row") * cells, cells)
        dz = line_block(gz_ref, zf_ref, lax.axis_index("col") * planes, planes)
        spread_y = (iota((LANES, local), 0) == iota((LANES, local), 1) % cells).astype(F32)
        spread_z = (iota((LANES, local), 0) == iota((LANES, local), 1) // cells).astype(F32)
        dy_tiled = dot(dy, spread_y)
        unit = (iota((cells, local), 0) == iota((cells, local), 1) % cells).astype(F32)
        last = dz[planes - 1 : planes, :] / dz[planes - 1 : planes, planes - 1 : planes]
        first = dz[0:1, :] / dz[0:1, 0:1]
        rows = jnp.concatenate([dz, last, first, jnp.zeros((6, LANES), F32)], axis=0)
        wide = dot(rows, spread_z)
        plane = iota((1, local), 1) // cells
        for k in range(planes + 2):
            row = wide[k : k + 1, :]
            k_ref[k * cells : (k + 1) * cells, :local] = dy_tiled * row
            other = unit * row
            if k < planes:
                other = other + jnp.where(plane == k, dy_tiled, 0.0)
            k_ref[k * cells : (k + 1) * cells, local:] = -2.0 * other

    span = a_ref.shape[2]
    both = jnp.concatenate(
        [a_ref[...].reshape(local, span), u_ref[...].reshape(local, span)], axis=0
    )
    out = dot(k_ref[...], both)
    l_ref[...] = out[:local, :]
    zp_ref[...] = out[local:, :]


def reduced_kernel(g_ref, xf_ref, et_ref, b_ref):
    groups, width = g_ref.shape[0], g_ref.shape[1]
    order = 2 * groups
    shape = (order, LANES)
    row, col = iota(shape, 0), iota(shape, 1)
    current = ((row == col) | (row + order == col)).astype(F32)
    couple = [half_step * xf_ref[0:1, width * c : width * c + 1] for c in range(1, groups)]
    et_ref[...] = jnp.zeros_like(et_ref)
    for c in range(groups):
        span = slice(c * width, (c + 1) * width)
        first_row, last_row = g_ref[c, 0:1, :], g_ref[c, width - 1 : width, :]
        et_ref[2 * c : 2 * c + 1, span] = first_row
        et_ref[2 * c + 1 : 2 * c + 2, span] = last_row
        if c > 0:
            at = row == 2 * c - 1
            b = couple[c - 1]
            current = current - jnp.where(at & (col == 2 * c), b * first_row[:, 0:1], 0.0)
            current = current - jnp.where(at & (col == 2 * c + 1), b * last_row[:, 0:1], 0.0)
        if c < groups - 1:
            at = row == 2 * c + 2
            b = couple[c]
            current = current - jnp.where(
                at & (col == 2 * c), b * first_row[:, width - 1 : width], 0.0
            )
            current = current - jnp.where(
                at & (col == 2 * c + 1), b * last_row[:, width - 1 : width], 0.0
            )
    for s in range(order):
        pivot = current[s : s + 1, :] / current[s : s + 1, s : s + 1]
        current = jnp.where(row == s, pivot, current - current[:, s : s + 1] * pivot)
    for c in range(groups):
        span = slice(c * width, (c + 1) * width)
        add = jnp.zeros((order, width), F32)
        if c > 0:
            k = order + 2 * c - 1
            add = add + current[:, k : k + 1] * (couple[c - 1] * g_ref[c, 0:1, :])
        if c < groups - 1:
            k = order + 2 * c + 2
            add = add + current[:, k : k + 1] * (couple[c] * g_ref[c, width - 1 : width, :])
        b_ref[:, span] = add


def x_solve(rows_ref, g_ref, et_ref, b_ref, store):
    groups, width = g_ref.shape[0], g_ref.shape[1]
    ends = dot_t(rows_ref[...], et_ref[...])
    for c in range(groups):
        span = slice(c * width, (c + 1) * width)
        store(span, dot_t(rows_ref[:, span], g_ref[c]) + dot(ends, b_ref[:, span]))


def section_kernel(
    y_ref, zp_ref, gy_ref, yf_ref, gz_ref, zf_ref, keep_ref, send_ref, all_ref
):
    blocks, rows, span = y_ref.shape
    cells = zp_ref.shape[0] // 2
    planes = rows // 4
    mine = lax.axis_index("col") % 2
    dy = line_block(gy_ref, yf_ref, lax.axis_index("row") * cells, cells)
    dz = line_block(gz_ref, zf_ref, lax.axis_index("col") * planes, planes)
    from_last = dy[:, cells - 1 : cells] / dy[cells - 1 : cells, cells - 1 : cells]
    from_first = dy[:, 0:1] / dy[0:1, 0:1]
    last = dz[:, planes - 1 : planes] / dz[planes - 1 : planes, planes - 1 : planes]
    first = dz[:, 0:1] / dz[0:1, 0:1]
    for s in range(blocks):
        at = slice(s * span, (s + 1) * span)
        below = y_ref[s, 0:planes, :]
        above = y_ref[s, 2 * planes : 3 * planes, :]
        for k, w in enumerate((last, first)):
            lo = jnp.sum(w * below, axis=0, keepdims=True)
            hi = jnp.sum(w * above, axis=0, keepdims=True)
            own = slice(k * cells, (k + 1) * cells)
            all_ref[own, at] = zp_ref[own, at] + from_first * lo + from_last * hi
    half = cells // 2
    for k in range(2):
        at = slice(k * half, (k + 1) * half)
        kept = pl.multiple_of(k * cells + mine * half, half)
        sent = pl.multiple_of(k * cells + (1 - mine) * half, half)
        keep_ref[at, :] = all_ref[pl.ds(kept, half), :]
        send_ref[at, :] = all_ref[pl.ds(sent, half), :]


def chip_pair(keep_ref, recv_ref, rows, lanes):
    lower_core = lax.axis_index("col") % 2 == 0
    kept, got = keep_ref[rows, lanes], recv_ref[rows, lanes]
    return jnp.where(lower_core, kept, got), jnp.where(lower_core, got, kept)


def pack_kernel(planes, keep_ref, recv_ref, gz_ref, zf_ref, buf_ref):
    chip = 2 * planes
    block = line_block(gz_ref, zf_ref, lax.axis_index("col") // 2 * chip, chip)
    e0, e1 = planes - 1, chip - 1
    up = block[e1 : e1 + 1, e0 : e0 + 1] / block[e1 : e1 + 1, e1 : e1 + 1]
    down = block[0:1, planes : planes + 1] / block[0:1, 0:1]
    dests, rows, span = buf_ref.shape
    half = rows // 2
    for d in range(dests):
        lanes = slice(d * span, (d + 1) * span)
        p0, p1 = chip_pair(keep_ref, recv_ref, slice(0, half), lanes)
        buf_ref[d, :half, :] = p1 + up * p0
        q0, q1 = chip_pair(keep_ref, recv_ref, slice(half, rows), lanes)
        buf_ref[d, half:, :] = q0 + down * q1


def unpack_kernel(planes, back_ref, keep_ref, recv_ref, gz_ref, zf_ref, own_ref, sib_ref):
    chip = 2 * planes
    block = line_block(gz_ref, zf_ref, lax.axis_index("col") // 2 * chip, chip)
    e0, b1, e1 = planes - 1, planes, chip - 1
    up = block[b1 : b1 + 1, 0:1] / block[0:1, 0:1]
    down = block[e0 : e0 + 1, e1 : e1 + 1] / block[e1 : e1 + 1, e1 : e1 + 1]
    cross = block[b1 : b1 + 1, e0 : e0 + 1]
    lower_core = lax.axis_index("col") % 2 == 0
    dests, rows, span = back_ref.shape
    half = rows // 2
    for d in range(dests):
        lanes = slice(d * span, (d + 1) * span)
        p0, _ = chip_pair(keep_ref, recv_ref, slice(0, half), lanes)
        _, q1 = chip_pair(keep_ref, recv_ref, slice(half, rows), lanes)
        below0 = back_ref[d, :half, :]
        below1 = up * below0 + cross * p0
        above1 = back_ref[d, half:, :]
        above0 = down * above1 + cross * q1
        own_ref[:half, lanes] = jnp.where(lower_core, below0, below1)
        own_ref[half:, lanes] = jnp.where(lower_core, above0, above1)
        sib_ref[:half, lanes] = jnp.where(lower_core, below1, below0)
        sib_ref[half:, lanes] = jnp.where(lower_core, above1, above0)


def inner_kernel(
    l_ref, y_ref, u_ref, gy_ref, yf_ref, gz_ref, zf_ref, gx_ref, et_ref, b_ref, out_ref, rows_ref
):
    blocks, rows, span = y_ref.shape
    planes = rows // 4
    cells = u_ref.shape[1]
    local = planes * cells
    dy = line_block(gy_ref, yf_ref, lax.axis_index("row") * cells, cells)
    dz = line_block(gz_ref, zf_ref, lax.axis_index("col") * planes, planes)
    from_last = dy[:, cells - 1 : cells] / dy[cells - 1 : cells, cells - 1 : cells]
    from_first = dy[:, 0:1] / dy[0:1, 0:1]
    lane = iota((1, LANES), 1)
    parts = []
    for z in range(planes):
        row = jnp.where(lane < planes, dz[z : z + 1, :], jnp.where(lane == planes + z, -2.0, 0.0))
        parts.append(from_first * row + from_last * pltpu.roll(row, 2 * planes, 1))
    mix = jnp.concatenate(parts, axis=0)[:, :rows]
    for s in range(blocks):
        at = slice(s * span, (s + 1) * span)
        rows_ref[:, at] = l_ref[:, at] + dot(mix, y_ref[s])

    def store(at, value):
        for z in range(planes):
            out_ref[z, :, at] = u_ref[z, :, at] + value[z * cells : (z + 1) * cells, :]

    x_solve(rows_ref, gx_ref, et_ref, b_ref, store)


def final_kernel(
    s_ref, own_ref, got_ref, gz_ref, zf_ref, gx_ref, et_ref, b_ref, out_ref, x_ref, sx_ref, c_ref
):
    z = pl.program_id(0)
    planes = c_ref.shape[1]
    cells = s_ref.shape[1]
    half = cells // 2

    @pl.when(z == 0)
    def _():
        mine = lax.axis_index("col") % 2
        for k in range(2):
            at = slice(k * half, (k + 1) * half)
            own = pl.multiple_of(k * cells + mine * half, half)
            other = pl.multiple_of(k * cells + (1 - mine) * half, half)
            x_ref[pl.ds(own, half), :] = own_ref[at, :]
            x_ref[pl.ds(other, half), :] = got_ref[at, :]
        dz = line_block(gz_ref, zf_ref, lax.axis_index("col") * planes, planes)
        first = dz[:, 0:1] / dz[0:1, 0:1]
        last = dz[:, planes - 1 : planes] / dz[planes - 1 : planes, planes - 1 : planes]
        c_ref[0] = jnp.broadcast_to(first, (planes, LANES))
        c_ref[1] = jnp.broadcast_to(last, (planes, LANES))

        def store(at, value):
            sx_ref[:, at] = value

        x_solve(x_ref, gx_ref, et_ref, b_ref, store)

    low = c_ref[0, pl.ds(z, 1), :][:, 0:1]
    high = c_ref[1, pl.ds(z, 1), :][:, 0:1]
    out_ref[0] = s_ref[0] + low * sx_ref[:cells, :] + high * sx_ref[cells:, :]


def body(scalar_field, reaction, x_faces, y_faces, z_faces, x_inverse, y_inverse, z_inverse):
    planes, cells, width = scalar_field.shape
    local = planes * cells
    rows = lax.axis_size("row")
    chips = lax.axis_size("col") // 2
    xf, yf, zf = x_faces[None, :], y_faces[None, :], z_faces[None, :]
    sds = lambda *s: jax.ShapeDtypeStruct(s, F32)
    whole = lambda *s: pl.BlockSpec(s, lambda i: (0,) * len(s))
    plane = pl.BlockSpec((1, cells, width), lambda i: (i, 0, 0))
    gspec, fspec = whole(2, 128, 128), whole(1, 256)

    a, y_buf = call(
        explicit_kernel,
        (sds(planes, cells, width), sds(rows, 4 * planes, width // rows)),
        20 * local * width,
        12 * local * width,
        "explicit",
        grid=(planes,),
        in_specs=[plane, plane, whole(1, width), gspec, fspec],
        out_specs=(plane, whole(rows, 4 * planes, width // rows)),
        scratch_shapes=[pltpu.VMEM((2, cells, LANES), F32)],
    )(scalar_field, reaction, xf, y_inverse, yf)
    y_in = lax.all_to_all(y_buf, "row", 0, 0, tiled=True)

    y_coef, z_coef = call(coef_kernel, (sds(32, LANES), sds(64, LANES)), 10**8, 10**6, "coefs")(
        y_inverse, yf, z_inverse, zf
    )
    end_rows, end_adds = call(
        reduced_kernel, (sds(32, width), sds(32, width)), 10**9, 2 * 10**6, "reduced"
    )(x_inverse, xf)
    span = 512
    chunk = pl.BlockSpec((planes, cells, span), lambda i: (0, 0, i))
    inside, z_part = call(
        local_kernel,
        (sds(local, width), sds(2 * cells, width)),
        12 * 320 * 512 * width,
        14 * local * width,
        "local",
        grid=(width // span,),
        in_specs=[chunk, chunk, gspec, fspec, gspec, fspec],
        out_specs=(
            pl.BlockSpec((local, span), lambda i: (0, i)),
            pl.BlockSpec((2 * cells, span), lambda i: (0, i)),
        ),
        scratch_shapes=[pltpu.VMEM((local + 2 * cells, 2 * local), F32)],
    )(a, scalar_field, y_inverse, yf, z_inverse, zf)

    y_out = call(scan_kernel, sds(*y_in.shape), 10**6, 10**6, "scan_y")(y_in, y_coef)
    y_back = lax.all_to_all(y_out, "row", 0, 0, tiled=True)

    keep, send = call(
        section_kernel,
        (sds(cells, width), sds(cells, width)),
        10**7,
        10**6,
        "section",
        scratch_shapes=[pltpu.VMEM((2 * cells, width), F32)],
    )(y_back, z_part, y_inverse, yf, z_inverse, zf)
    pairs = [(i, i ^ 1) for i in range(2 * chips)]
    recv = lax.ppermute(send, "col", pairs)
    z_buf = call(
        functools.partial(pack_kernel, planes), sds(chips, cells, width // chips), 10**6, 10**6, "pack"
    )(keep, recv, z_inverse, zf)
    groups = [list(range(k, 2 * chips, 2)) for k in range(2)]
    z_in = lax.all_to_all(z_buf, "col", 0, 0, axis_index_groups=groups, tiled=True)

    partial_out = call(
        inner_kernel,
        sds(planes, cells, width),
        12 * local * width * 200,
        16 * local * width,
        "inner",
        scratch_shapes=[pltpu.VMEM((local, width), F32)],
    )(
        inside, y_back, scalar_field, y_inverse, yf, z_inverse, zf, x_inverse, end_rows, end_adds
    )

    z_out = call(scan_kernel, sds(*z_in.shape), 10**6, 10**6, "scan_z")(z_in, z_coef)
    z_back = lax.all_to_all(z_out, "col", 0, 0, axis_index_groups=groups, tiled=True)
    own, sib = call(
        functools.partial(unpack_kernel, planes),
        (sds(cells, width), sds(cells, width)),
        10**6,
        10**6,
        "unpack",
    )(z_back, keep, recv, z_inverse, zf)
    got = lax.ppermute(sib, "col", pairs)
    return call(
        final_kernel,
        sds(planes, cells, width),
        12 * local * width,
        8 * local * width,
        "final",
        grid=(planes,),
        in_specs=[
            plane,
            whole(cells, width),
            whole(cells, width),
            gspec,
            fspec,
            whole(*x_inverse.shape),
            whole(32, width),
            whole(32, width),
        ],
        out_specs=plane,
        scratch_shapes=[
            pltpu.VMEM((2 * cells, width), F32),
            pltpu.VMEM((2 * cells, width), F32),
            pltpu.VMEM((2, planes, LANES), F32),
        ],
    )(partial_out, own, got, z_inverse, zf, x_inverse, end_rows, end_adds)


def solution(mesh):
    in_specs = (P("col", "row", None), P("col", "row", None), P(), P(), P(), P(), P(), P())
    out_specs = P("col", "row", None)
    return jax.shard_map(body, mesh=mesh, in_specs=in_specs, out_specs=out_specs, check_vma=False)
```

time: 392 us -> 103 us (0.26)
  the two profiles are of different devices: /device:TPU:2 before, /device:TPU:1 now
where the time goes in v1:
time: 103 us
  Pallas kernels  44.1 us (43%)
  blocking collectives  32.4 us (31%)
  starting transfers between devices  17.4 us (17%)
  local copies, waits for them, and re-layouts  5.2 us (5%)
  waiting for transfers between devices  3.45 us (3%)
    all_to_all x1, blocking collectives, body(): lax.all_to_all(z_buf, 'col', 0, 0, axis_index_groups=groups, tiled=True)  19.1 us
    all_to_all x1, blocking collectives, body(): lax.all_to_all(z_out, 'col', 0, 0, axis_index_groups=groups, tiled=True)  13.3 us
    pallas_call x1, Pallas kernels, body(): call(inner_kernel, sds(planes, cells, width), 12 * local * width * 200, 1...  12.5 us
    all_to_all x1, starting transfers between devices, body(): y_in = lax.all_to_all(y_buf, 'row', 0, 0, tiled=True)  7.48 us
    pallas_call x1, Pallas kernels, body(): call(final_kernel, sds(planes, cells, width), 12 * local * width, 8 * loc...  7.03 us
    pallas_call x1, Pallas kernels, body(): call(local_kernel, (sds(local, width), sds(2 * cells, width)), 12 * 320 *...  6.86 us
    pallas_call x1, Pallas kernels, body(): call(explicit_kernel, (sds(planes, cells, width), sds(rows, 4 * planes, w...  6.82 us
    pallas_call x1, Pallas kernels, body(): call(coef_kernel, (sds(32, LANES), sds(64, LANES)), 10 ** 8, 10 ** 6, 'co...  5.32 us
  transfers between devices with their start and end apart: 4, of which 2 were waited for; matrix products, arithmetic and copies ran while one was open for 0% of the time, Pallas kernels for 27%

profile of v1, /device:TPU:1, one launch (start us, length us, event | category | flops | bytes accessed | tf_op | source)
XLA Modules:
  0.0 102.6 jit_solution(4516544468084105793)
XLA Ops:
  0.0 0.0 copy-start
  0.0 1.6 %copy-done = f32[8,32,2048]{2,1,0:T(8,128)S(1)} copy-done((f32[8,32,2048]{2,1,0:T(8,128)S(1)}, f32[8,32,2048]{2,1,0:T(8,128)}, u32[]{:S(2)}) %copy-start) | copy-done | bytes 2097176
  1.6 0.0 copy-start.4
  1.6 0.9 copy-done.4
  2.5 0.0 copy-start.7
  2.5 0.7 copy-done.7
  3.2 0.0 copy-start.9
  3.2 0.7 copy-done.9
  3.9 0.0 copy-start.2
  3.9 0.0 copy-start.5
  3.9 0.0 copy-start.6
  3.9 0.0 copy-start.8
  3.9 6.8 %explicit.1 = (f32[8,32,2048]{2,1,0:T(8,128)S(1)}, f32[8,32,256]{2,1,0:T(8,128)}) custom-call(f32[8,32,2048]{2,1,0:T(8,128)S(1)} %copy-done, f32[8,32,2048]{2,1,0:T(8,128)} %r_ref.1, f32[1,2048]{1,0:T(1,128)S(1)} %bitcast.15, f32[2,128,128]{2,1,0:T(8,128)S(1)} %copy-done.4, f32[1,256]{1,0:T(1,128)S(1)} %bitcast.10), custom_call_target="tpu_custom_call" | custom-call | flops 10485760 | bytes 6291456 | tf_op jit(solution)/shard_map/explicit/pallas_call | solution.py:390
  10.7 7.5 %all-to-all-start = ((f32[8,32,256]{2,1,0:T(8,128)}), f32[8,32,256]{2,1,0:T(8,128)S(1)}, u32[]{:S(2)}, u32[]{:S(2)}) async-start(f32[8,32,256]{2,1,0:T(8,128)} %get-tuple-element.19), calls=%async_computation | async-start | bytes 524288 | tf_op jit(solution)/shard_map/all_to_all | solution.py:401
  18.2 0.0 copy-done.2
  18.2 0.0 copy-done.5
  18.2 0.0 copy-done.6
  18.2 0.0 copy-done.8
  18.2 5.3 %coefs.1 = (f32[32,128]{1,0:T(8,128)S(1)}, f32[64,128]{1,0:T(8,128)S(1)}) custom-call(f32[2,128,128]{2,1,0:T(8,128)S(1)} %copy-done.5, f32[1,256]{1,0:T(1,128)S(1)} %bitcast.11, f32[2,128,128]{2,1,0:T(8,128)S(1)} %copy-done.2, f32[1,256]{1,0:T(1,128)S(1)} %bitcast.3), custom_call_target="tpu_custom_call" | custom-call | flops 100000000 | bytes 1000000 | tf_op jit(solution)/shard_map/coefs/pallas_call | solution.py:403
  23.5 2.3 %all-to-all-done.in_ref = f32[8,32,256]{2,1,0:T(8,128)S(1)} async-done(((f32[8,32,256]{2,1,0:T(8,128)}), f32[8,32,256]{2,1,0:T(8,128)S(1)}, u32[]{:S(2)}, u32[]{:S(2)}) %all-to-all-start) | async-done | bytes 262176 | tf_op jit(solution)/shard_map/all_to_all | solution.py:401
  25.8 0.8 scan_y.1
  26.6 4.4 %all-to-all-start.1 = ((f32[8,32,256]{2,1,0:T(8,128)}), f32[8,32,256]{2,1,0:T(8,128)S(1)}, u32[]{:S(2)}, u32[]{:S(2)}) async-start(f32[8,32,256]{2,1,0:T(8,128)} %scan_y.1), calls=%async_computation.1 | async-start | bytes 524288 | tf_op jit(solution)/shard_map/all_to_all | solution.py:427
  31.0 6.9 %local.1 = (f32[256,2048]{1,0:T(8,128)S(1)}, f32[64,2048]{1,0:T(8,128)S(1)}) custom-call(f32[8,32,2048]{2,1,0:T(8,128)S(1)} %get-tuple-element.17.a_ref, f32[8,32,2048]{2,1,0:T(8,128)} %u_ref.5, f32[2,128,128]{2,1,0:T(8,128)S(1)} %copy-done.5, f32[1,256]{1,0:T(1,128)S(1)} %bitcast.12, f32[2,128,128]{2,1,0:T(8,128)S(1)} %copy-done.2, f32[1,256]{1,0:T(1,128)S(1)} %bitcast.4), custom_call_target="tpu_custom_call" | custom-call | flops 4026531840 | bytes 7340032 | tf_op jit(solution)/shard_map/local/pallas_call | solution.py:411
  37.8 0.0 copy-start.3
  37.8 1.3 %copy-done.3 = f32[256,2048]{1,0:T(8,128)} copy-done((f32[256,2048]{1,0:T(8,128)}, f32[256,2048]{1,0:T(8,128)S(1)}, u32[]{:S(2)}) %copy-start.3) | copy-done | bytes 2097176
  39.1 0.0 all-to-all-done.1.y_ref
  39.1 0.0 copy-start.1
  39.1 0.0 copy-start.10
  39.2 0.6 section.1
  39.7 2.2 %collective-permute-start = (f32[32,2048]{1,0:T(8,128)S(1)}, f32[32,2048]{1,0:T(8,128)S(1)}, u32[]{:S(2)}, u32[]{:S(2)}) collective-permute-start(f32[32,2048]{1,0:T(8,128)S(1)} %get-tuple-element.25), channel_id=1, source_target_pairs={{0,1},{1,0},{2,3},{3,2},{4,5},{5,4},{6,7},{7,6},{8,9},{9,8},{10,11... | collective-permute-start | bytes 786440 | tf_op jit(solution)/shard_map/ppermute | solution.py:438
  41.9 1.2 %collective-permute-done.recv_ref = f32[32,2048]{1,0:T(8,128)S(1)} collective-permute-done((f32[32,2048]{1,0:T(8,128)S(1)}, f32[32,2048]{1,0:T(8,128)S(1)}, u32[]{:S(2)}, u32[]{:S(2)}) %collective-permute-start) | collective-permute-done | bytes 262176 | tf_op jit(solution)/shard_map/ppermute | solution.py:438
  43.1 0.5 pack.1
  43.6 19.1 %all_to_all.20.in_ref = f32[16,32,128]{2,1,0:T(8,128)S(1)} all-to-all(f32[16,32,128]{2,1,0:T(8,128)S(1)} %pack.1), channel_id=1, replica_groups={{0,2,4,6,8,10,12,14,16,18,20,22,24,26,28,30},{1,3,5,7,9,11,13,15,17,19,..., dimensions={0} | all-to-all | bytes 524288 | tf_op jit(solution)/shard_map/all_to_all | solution.py:443
  62.7 0.1 scan_z.1
  62.8 13.3 %all_to_all.21.back_ref = f32[16,32,128]{2,1,0:T(8,128)S(1)} all-to-all(f32[16,32,128]{2,1,0:T(8,128)S(1)} %scan_z.1), channel_id=1, replica_groups={{0,2,4,6,8,10,12,14,16,18,20,22,24,26,28,30},{1,3,5,7,9,11,13,15,17,19,..., dimensions={0} | all-to-all | bytes 524288 | tf_op jit(solution)/shard_map/all_to_all | solution.py:457
  76.0 0.5 unpack.1
  76.5 3.4 %collective-permute-start.1 = (f32[32,2048]{1,0:T(8,128)S(1)}, f32[32,2048]{1,0:T(8,128)S(1)}, u32[]{:S(2)}, u32[]{:S(2)}) collective-permute-start(f32[32,2048]{1,0:T(8,128)S(1)} %get-tuple-element.28), channel_id=1, source_target_pairs={{0,1},{1,0},{2,3},{3,2},{4,5},{5,4},{6,7},{7,6},{8,9},{9,8},{10,11... | collective-permute-start | bytes 786440 | tf_op jit(solution)/shard_map/ppermute | solution.py:465
  79.8 0.0 copy-done.1
  79.8 0.0 copy-done.10
  79.9 3.2 %reduced.1 = (f32[32,2048]{1,0:T(8,128)S(1)}, f32[32,2048]{1,0:T(8,128)S(1)}) custom-call(f32[16,128,128]{2,1,0:T(8,128)S(1)} %copy-done.1, f32[1,2048]{1,0:T(1,128)S(1)} %bitcast.16), custom_call_target="tpu_custom_call" | custom-call | flops 1000000000 | bytes 2000000 | tf_op jit(solution)/shard_map/reduced/pallas_call | solution.py:406
  83.0 12.5 %inner.1.s_ref = f32[8,32,2048]{2,1,0:T(8,128)S(1)} custom-call(f32[256,2048]{1,0:T(8,128)} %copy-done.3, f32[8,32,256]{2,1,0:T(8,128)S(1)} %all-to-all-done.1.y_ref, f32[8,32,2048]{2,1,0:T(8,128)} %u_ref.5, f32[2,128,128]{2,1,0:T(8,128)S(1)} %copy-done.5, f32[1,256]{1,0:T(1,128)S(1)} %bitcast.14, f32[2,128,128]{2,1,0:T(8,128)S(1)} %copy-done.2, ...), custom_call_target="tpu_custom_call" | custom-call | flops 1258291200 | bytes 8388608 | tf_op jit(solution)/shard_map/inner/pallas_call | solution.py:445
  95.6 0.0 collective-permute-done.1.got_ref
  95.6 7.0 %final.1 = f32[8,32,2048]{2,1,0:T(8,128)} custom-call(f32[8,32,2048]{2,1,0:T(8,128)S(1)} %inner.1.s_ref, f32[32,2048]{1,0:T(8,128)S(1)} %get-tuple-element.27.own_ref, f32[32,2048]{1,0:T(8,128)S(1)} %collective-permute-done.1.got_ref, f32[2,128,128]{2,1,0:T(8,128)S(1)} %copy-done.2, f32[1,256]{1,0:T(1,128)S(1)} %bitcast.9, f32[16,128,128]{2,1,0:T(8,128)S(1)} %copy-done.1, ...), custom_call_target="tpu_custom_call" | custom-call | flops 6291456 | bytes 4194304 | tf_op jit(solution)/shard_map/final/pallas_call | solution.py:466
Async XLA Ops:
  0.0 1.6 %copy-start = (f32[8,32,2048]{2,1,0:T(8,128)S(1)}, f32[8,32,2048]{2,1,0:T(8,128)}, u32[]{:S(2)}) copy-start(f32[8,32,2048]{2,1,0:T(8,128)} %u_ref.5) | copy-start | bytes 6291460
  1.6 0.9 copy-start.4
  2.5 0.7 copy-start.7
  3.2 0.7 copy-start.9
  3.9 14.3 %copy-start.2 = (f32[2,128,128]{2,1,0:T(8,128)S(1)}, f32[2,128,128]{2,1,0:T(8,128)}, u32[]{:S(2)}) copy-start(f32[2,128,128]{2,1,0:T(8,128)} %gz_ref.13) | copy-start | bytes 393220
  3.9 14.3 %copy-start.5 = (f32[2,128,128]{2,1,0:T(8,128)S(1)}, f32[2,128,128]{2,1,0:T(8,128)}, u32[]{:S(2)}) copy-start(f32[2,128,128]{2,1,0:T(8,128)} %gy_ref.9) | copy-start | bytes 393220
  3.9 14.3 %copy-start.6 = (f32[256]{0:T(256)S(1)}, f32[256]{0:T(256)}, u32[]{:S(2)}) copy-start(f32[256]{0:T(256)} %param.12) | copy-start | bytes 3076
  3.9 14.3 %copy-start.8 = (f32[256]{0:T(256)S(1)}, f32[256]{0:T(256)}, u32[]{:S(2)}) copy-start(f32[256]{0:T(256)} %param.11) | copy-start | bytes 3076
  10.7 15.1 %all-to-all-start = ((f32[8,32,256]{2,1,0:T(8,128)}), f32[8,32,256]{2,1,0:T(8,128)S(1)}, u32[]{:S(2)}, u32[]{:S(2)}) async-start(f32[8,32,256]{2,1,0:T(8,128)} %get-tuple-element.19), calls=%async_computation | async-start | bytes 524288 | tf_op jit(solution)/shard_map/all_to_all | solution.py:401
  26.6 12.6 %all-to-all-start.1 = ((f32[8,32,256]{2,1,0:T(8,128)}), f32[8,32,256]{2,1,0:T(8,128)S(1)}, u32[]{:S(2)}, u32[]{:S(2)}) async-start(f32[8,32,256]{2,1,0:T(8,128)} %scan_y.1), calls=%async_computation.1 | async-start | bytes 524288 | tf_op jit(solution)/shard_map/all_to_all | solution.py:427
  37.8 1.3 %copy-start.3 = (f32[256,2048]{1,0:T(8,128)}, f32[256,2048]{1,0:T(8,128)S(1)}, u32[]{:S(2)}) copy-start(f32[256,2048]{1,0:T(8,128)S(1)} %get-tuple-element.18.l_ref) | copy-start | bytes 6291460
  39.1 40.7 %copy-start.1 = (f32[16,128,128]{2,1,0:T(8,128)S(1)}, f32[16,128,128]{2,1,0:T(8,128)}, u32[]{:S(2)}) copy-start(f32[16,128,128]{2,1,0:T(8,128)} %gx_ref.3) | copy-start | bytes 3145732
  39.1 40.7 %copy-start.10 = (f32[2048]{0:T(1024)S(1)}, f32[2048]{0:T(1024)}, u32[]{:S(2)}) copy-start(f32[2048]{0:T(1024)} %param.10) | copy-start | bytes 24580
  39.7 3.4 %collective-permute-start = (f32[32,2048]{1,0:T(8,128)S(1)}, f32[32,2048]{1,0:T(8,128)S(1)}, u32[]{:S(2)}, u32[]{:S(2)}) collective-permute-start(f32[32,2048]{1,0:T(8,128)S(1)} %get-tuple-element.25), channel_id=1, source_target_pairs={{0,1},{1,0},{2,3},{3,2},{4,5},{5,4},{6,7},{7,6},{8,9},{9,8},{10,11... | collective-permute-start | bytes 786440 | tf_op jit(solution)/shard_map/ppermute | solution.py:438
  76.5 19.1 %collective-permute-start.1 = (f32[32,2048]{1,0:T(8,128)S(1)}, f32[32,2048]{1,0:T(8,128)S(1)}, u32[]{:S(2)}, u32[]{:S(2)}) collective-permute-start(f32[32,2048]{1,0:T(8,128)S(1)} %get-tuple-element.28), channel_id=1, source_target_pairs={{0,1},{1,0},{2,3},{3,2},{4,5},{5,4},{6,7},{7,6},{8,9},{9,8},{10,11... | collective-permute-start | bytes 786440 | tf_op jit(solution)/shard_map/ppermute | solution.py:465

commit v2 on v1

v2 whole, which is shorter than its diff:
```python
import functools

import jax
import jax.numpy as jnp
from jax import lax
from jax.experimental import pallas as pl
from jax.experimental.pallas import tpu as pltpu
from jax.sharding import Mesh
from jax.sharding import PartitionSpec as P

F32 = jnp.float32
BF16 = jnp.bfloat16
half_step = 500.0
time_step = 1000.0
LANES = 128


def dot(left, right):
    return lax.dot_general(
        left,
        right,
        (((1,), (0,)), ((), ())),
        precision=lax.Precision.HIGHEST,
        preferred_element_type=F32,
    )


def halves(value):
    high = value.astype(BF16)
    return high, (value - high.astype(F32)).astype(BF16)


def iota(shape, dim):
    return lax.broadcasted_iota(jnp.int32, shape, dim)


def joint(g_ref, faces_ref):
    b = half_step * faces_ref[0:1, 128:129]
    g0 = g_ref[0, 127:128, 127:128]
    g1 = g_ref[1, 0:1, 0:1]
    den = 1.0 - b * b * g0 * g1
    return b * b * g1 / den, b * b * g0 / den, b / den


def line_block(g_ref, faces_ref, start, size):
    alpha0, alpha1, _ = joint(g_ref, faces_ref)
    group = start // 128
    offset = start - group * 128
    rows = g_ref[group, pl.ds(pl.multiple_of(offset, size), size), :]
    low = group == 0
    edge_row = jnp.where(low, g_ref[0, 127:128, :], g_ref[1, 0:1, :])
    edge_col = jnp.where(low, rows[:, 127:128], rows[:, 0:1])
    alpha = jnp.where(low, alpha0, alpha1)
    block = rows + (alpha * edge_col) * edge_row
    return pltpu.roll(block, lax.rem(128 - offset, 128), 1)


def element(g_ref, joined, i, j):
    alpha0, alpha1, beta = joined
    gi, gj = i // 128, j // 128
    li, lj = i % 128, j % 128
    ei, ej = (0 if gi else 127), (0 if gj else 127)
    across = g_ref[gi, li : li + 1, ei : ei + 1] * g_ref[gj, ej : ej + 1, lj : lj + 1]
    if gi == gj:
        alpha = alpha1 if gi else alpha0
        return g_ref[gi, li : li + 1, lj : lj + 1] + alpha * across
    return beta * across


MIB = 1024 * 1024


def call(kernel, out_shape, flops, nbytes, name, room=20, **kw):
    return pl.pallas_call(
        kernel,
        out_shape=out_shape,
        name=name,
        compiler_params=pltpu.CompilerParams(vmem_limit_bytes=int(room * MIB)),
        cost_estimate=pl.CostEstimate(flops=flops, bytes_accessed=nbytes, transcendentals=0),
        **kw,
    )


def call_after(earlier, kernel, out_shape, flops, nbytes, name, *args, **kw):
    count, extra = len(args), len(earlier)

    def ordered(*refs):
        kernel(*refs[:count], *refs[count + extra :])

    specs = [pl.BlockSpec(memory_space=pltpu.VMEM)] * count + [pl.BlockSpec(memory_space=pltpu.HBM)] * extra
    return call(ordered, out_shape, flops, nbytes, name, in_specs=specs, **kw)(*args, *earlier)


def explicit_kernel(
    u_hbm, r_hbm, xf_hbm, gy_hbm, yf_hbm, a_hbm, buf_ref,
    u_ref, r_ref, a_ref, xf_ref, gy_ref, yf_ref, f_ref, u_sem, r_sem, a_sem, s_sem
):
    planes, cells, width = u_ref.shape
    small = [
        pltpu.make_async_copy(gy_hbm, gy_ref, s_sem.at[0]),
        pltpu.make_async_copy(yf_hbm, yf_ref, s_sem.at[1]),
        pltpu.make_async_copy(xf_hbm, xf_ref, s_sem.at[2]),
    ]
    for copy in small:
        copy.start()

    def fetch(z):
        return (
            pltpu.make_async_copy(u_hbm.at[z], u_ref.at[z], u_sem.at[z]),
            pltpu.make_async_copy(r_hbm.at[z], r_ref.at[z], r_sem.at[z]),
        )

    def give(z):
        return pltpu.make_async_copy(a_ref.at[z], a_hbm.at[z], a_sem.at[z])

    for z in range(planes):
        for copy in fetch(z):
            copy.start()
    for copy in small:
        copy.wait()

    block = line_block(gy_ref, yf_ref, lax.axis_index("row") * cells, cells)
    last = block[:, cells - 1 : cells] / block[cells - 1 : cells, cells - 1 : cells]
    first = block[:, 0:1] / block[0:1, 0:1]
    w = [jnp.broadcast_to(v, (cells, LANES)) for v in (last, first)]
    here = time_step * xf_ref[...]
    lane = iota((1, width), 1)
    after = jnp.where(lane == width - 1, 0.0, pltpu.roll(here, width - 1, 1))
    f_ref[0:1, :] = after
    f_ref[1:2, :] = jnp.where(lane == 0, 0.0, here)
    f_ref[2:3, :] = 4.0 - (after + here)

    span = buf_ref.shape[2]
    count = width // LANES
    lane = iota((cells, LANES), 1)

    def plane(z, carry):
        for copy in fetch(z):
            copy.wait()

        def column(c):
            here = u_ref[z, :, c * LANES : (c + 1) * LANES]
            return here, pltpu.roll(here, 1, 1), pltpu.roll(here, LANES - 1, 1)

        sums = {}
        before = jnp.zeros((cells, LANES), F32)
        now = column(0)
        for c in range(count):
            then = column(c + 1) if c + 1 < count else (None, None, before)
            u = now[0]
            lower = jnp.where(lane == 0, before, now[1])
            upper = jnp.where(lane == LANES - 1, then[2], now[2])
            at = slice(c * LANES, (c + 1) * LANES)
            rate = r_ref[z, :, at] * (time_step - time_step * (u * u)) + f_ref[2:3, at]
            a = f_ref[0:1, at] * upper + f_ref[1:2, at] * lower + rate * u
            a_ref[z, :, at] = a
            for k in range(2):
                for f, field in enumerate((a, u)):
                    row = jnp.sum(w[k] * field, axis=0, keepdims=True)
                    sums.setdefault((k, f), []).append(row)
            if (c + 1) * LANES % span == 0:
                for (k, f), pieces in sums.items():
                    row = jnp.concatenate(pieces, axis=1)
                    buf_ref[c * LANES // span, pl.ds(z + 16 * k + 8 * f, 1), :] = row
                sums = {}
            before, now = now[1], then
        give(z).start()
        return carry

    lax.fori_loop(0, planes, plane, 0)
    for z in range(planes):
        give(z).wait()


def coef_kernel(gy_ref, yf_ref, gz_ref, zf_ref, yc_ref, zc_ref):
    for g_ref, f_ref, out_ref, count in ((gy_ref, yf_ref, yc_ref, 8), (gz_ref, zf_ref, zc_ref, 16)):
        joined = joint(g_ref, f_ref)
        size = 256 // count
        m = functools.partial(element, g_ref, joined)
        out_ref[...] = jnp.zeros_like(out_ref)
        for c in range(count):
            b, e = c * size, c * size + size - 1
            if c > 0:
                ee = m(e, e - size) / m(e, e)
                be = m(b, b - 1)
                out_ref[c : c + 1, :] = jnp.broadcast_to(ee, (1, LANES))
                out_ref[count + c : count + c + 1, :] = jnp.broadcast_to(be, (1, LANES))
            if c < count - 1:
                bb = m(b, b + size) / m(b, b)
                eb = m(e, e + 1)
                out_ref[2 * count + c : 2 * count + c + 1, :] = jnp.broadcast_to(bb, (1, LANES))
                out_ref[3 * count + c : 3 * count + c + 1, :] = jnp.broadcast_to(eb, (1, LANES))


def scan_kernel(in_ref, c_ref, out_ref):
    count, rows, span = in_ref.shape
    half = rows // 2

    def coef(k):
        return c_ref[k : k + 1, 0:1]

    zero = jnp.zeros((half, span), F32)
    out_ref[0, :half, :] = zero
    out_ref[count - 1, half:, :] = zero
    below = above = None
    for s in range(count - 1):
        own = in_ref[s, :half, :]
        below = own if s == 0 else own + coef(s) * below
        out_ref[s + 1, :half, :] = coef(count + s + 1) * below
        t = count - 1 - s
        own = in_ref[t, half:, :]
        above = own if s == 0 else own + coef(2 * count + t) * above
        out_ref[t - 1, half:, :] = coef(3 * count + t - 1) * above


def local_kernel(
    a_hbm, u_hbm, gy_ref, yf_ref, gz_ref, zf_ref, l_hbm, zp_ref,
    k_ref, a_ref, u_ref, l_ref, a_sem, u_sem, l_sem
):
    chunks, planes, cells, span = u_ref.shape

    def fetch(k):
        lanes = pl.ds(pl.multiple_of(k * span, span), span)
        return (
            pltpu.make_async_copy(a_hbm.at[:, lanes], a_ref.at[k], a_sem.at[k]),
            pltpu.make_async_copy(u_hbm.at[:, :, lanes], u_ref.at[k], u_sem.at[k]),
        )

    def give(k):
        lanes = pl.ds(pl.multiple_of(k * span, span), span)
        return pltpu.make_async_copy(l_ref.at[k], l_hbm.at[:, lanes], l_sem.at[k])

    for k in range(chunks):
        for copy in fetch(k):
            copy.start()
    count = k_ref.shape[0] // 2
    local = planes * cells

    dy = line_block(gy_ref, yf_ref, lax.axis_index("row") * cells, cells)
    dz = line_block(gz_ref, zf_ref, lax.axis_index(("chip", "core")) * planes, planes)
    spread_y = (iota((LANES, local), 0) == iota((LANES, local), 1) % cells).astype(F32)
    spread_z = (iota((LANES, local), 0) == iota((LANES, local), 1) // cells).astype(F32)
    dy_tiled = dot(dy, spread_y)
    unit = (iota((cells, local), 0) == iota((cells, local), 1) % cells).astype(F32)
    last = dz[planes - 1 : planes, :] / dz[planes - 1 : planes, planes - 1 : planes]
    first = dz[0:1, :] / dz[0:1, 0:1]
    rows = jnp.concatenate([dz, last, first, jnp.zeros((6, LANES), F32)], axis=0)
    wide = dot(rows, spread_z)
    plane = iota((1, local), 1) // cells

    def unit_part(k, row):
        other = unit * row
        return other + jnp.where(plane == k, dy_tiled, 0.0) if k < planes else other

    for k in range(planes + 2):
        row = wide[k : k + 1, :]
        own, rest = k * cells, count + k * cells
        for lanes, value in ((0, dy_tiled * row), (local, -2.0 * unit_part(k, row))):
            high, low = halves(value)
            k_ref[own : own + cells, lanes : lanes + local] = high
            k_ref[rest : rest + cells, lanes : lanes + local] = low

    def chunk(k, carry):
        for copy in fetch(k):
            copy.wait()
        both = jnp.concatenate(
            [a_ref[k], u_ref[k].reshape(local, span)], axis=0
        )
        high, low = halves(both)
        wide = jnp.dot(k_ref[...], high, preferred_element_type=F32)
        out = wide[:count] + wide[count:]
        out = out + jnp.dot(k_ref[:count], low, preferred_element_type=F32)
        l_ref[k] = out[:local, :]
        zp_ref[:, pl.ds(pl.multiple_of(k * span, span), span)] = out[local:, :]
        give(k).start()
        return carry

    lax.fori_loop(0, chunks, chunk, 0)
    for k in range(chunks):
        give(k).wait()


def reduced_kernel(g_ref, xf_ref, wh_ref, wl_ref, bh_ref, bl_ref, mark_ref):
    groups, width = g_ref.shape[0], g_ref.shape[1]
    order = 2 * groups
    shape = (order, LANES)
    row, col = iota(shape, 0), iota(shape, 1)
    current = ((row == col) | (row + order == col)).astype(F32)
    mark_ref[...] = jnp.zeros_like(mark_ref)
    couple = [half_step * xf_ref[0:1, width * c : width * c + 1] for c in range(1, groups)]
    lane = iota((width, LANES), 1)
    for c in range(groups):
        block = g_ref[c]
        ends = jnp.where(
            lane == 2 * c,
            block[:, 0:1],
            jnp.where(lane == 2 * c + 1, block[:, width - 1 : width], 0.0),
        )
        wh_ref[c, :, :width], wl_ref[c, :, :width] = halves(block)
        wh_ref[c, :, width:], wl_ref[c, :, width:] = halves(ends)
        first_row, last_row = g_ref[c, 0:1, :], g_ref[c, width - 1 : width, :]
        if c > 0:
            at = row == 2 * c - 1
            b = couple[c - 1]
            current = current - jnp.where(at & (col == 2 * c), b * first_row[:, 0:1], 0.0)
            current = current - jnp.where(at & (col == 2 * c + 1), b * last_row[:, 0:1], 0.0)
        if c < groups - 1:
            at = row == 2 * c + 2
            b = couple[c]
            current = current - jnp.where(
                at & (col == 2 * c), b * first_row[:, width - 1 : width], 0.0
            )
            current = current - jnp.where(
                at & (col == 2 * c + 1), b * last_row[:, width - 1 : width], 0.0
            )
    for s in range(order):
        pivot = current[s : s + 1, :] / current[s : s + 1, s : s + 1]
        current = jnp.where(row == s, pivot, current - current[:, s : s + 1] * pivot)
    for c in range(groups):
        span = slice(c * width, (c + 1) * width)
        add = jnp.zeros((order, width), F32)
        if c > 0:
            k = order + 2 * c - 1
            add = add + current[:, k : k + 1] * (couple[c - 1] * g_ref[c, 0:1, :])
        if c < groups - 1:
            k = order + 2 * c + 2
            add = add + current[:, k : k + 1] * (couple[c] * g_ref[c, width - 1 : width, :])
        bh_ref[:, span], bl_ref[:, span] = halves(add)


def dot_halves(both, high, left, right):
    count = high.shape[0]
    wide = jnp.dot(both, left, preferred_element_type=F32)
    return wide[:count] + wide[count:] + jnp.dot(high, right, preferred_element_type=F32)


def x_solve(rows_ref, wh_ref, wl_ref, bh_ref, bl_ref, out_ref, store):
    groups, width = wh_ref.shape[0], wh_ref.shape[1]
    ends = jnp.zeros((rows_ref.shape[0], LANES), F32)
    for c in range(groups):
        at = slice(c * width, (c + 1) * width)
        high, low = halves(rows_ref[:, at])
        wide = dot_halves(jnp.concatenate([high, low], axis=0), high, wh_ref[c], wl_ref[c])
        out_ref[:, at] = wide[:, :width]
        ends = ends + wide[:, width:]
    order = bh_ref.shape[0]
    high, low = halves(ends[:, :order])
    both = jnp.concatenate([high, low], axis=0)
    for c in range(groups // 2):
        at = slice(2 * c * width, 2 * (c + 1) * width)
        store(at, out_ref[:, at] + dot_halves(both, high, bh_ref[:, at], bl_ref[:, at]))


def section_kernel(
    y_ref, zp_ref, gy_ref, yf_ref, gz_ref, zf_ref, keep_ref, send_ref, all_ref
):
    blocks, rows, span = y_ref.shape
    cells = zp_ref.shape[0] // 2
    planes = rows // 4
    mine = lax.axis_index("core")
    dy = line_block(gy_ref, yf_ref, lax.axis_index("row") * cells, cells)
    dz = line_block(gz_ref, zf_ref, lax.axis_index(("chip", "core")) * planes, planes)
    from_last = dy[:, cells - 1 : cells] / dy[cells - 1 : cells, cells - 1 : cells]
    from_first = dy[:, 0:1] / dy[0:1, 0:1]
    last = dz[:, planes - 1 : planes] / dz[planes - 1 : planes, planes - 1 : planes]
    first = dz[:, 0:1] / dz[0:1, 0:1]
    for s in range(blocks):
        at = slice(s * span, (s + 1) * span)
        below = y_ref[s, 0:planes, :]
        above = y_ref[s, 2 * planes : 3 * planes, :]
        for k, w in enumerate((last, first)):
            lo = jnp.sum(w * below, axis=0, keepdims=True)
            hi = jnp.sum(w * above, axis=0, keepdims=True)
            own = slice(k * cells, (k + 1) * cells)
            all_ref[own, at] = zp_ref[own, at] + from_first * lo + from_last * hi
    half = cells // 2
    for k in range(2):
        at = slice(k * half, (k + 1) * half)
        kept = pl.multiple_of(k * cells + mine * half, half)
        sent = pl.multiple_of(k * cells + (1 - mine) * half, half)
        keep_ref[at, :] = all_ref[pl.ds(kept, half), :]
        send_ref[at, :] = all_ref[pl.ds(sent, half), :]


def chip_pair(keep_ref, recv_ref, rows, lanes):
    lower_core = lax.axis_index("core") == 0
    kept, got = keep_ref[rows, lanes], recv_ref[rows, lanes]
    return jnp.where(lower_core, kept, got), jnp.where(lower_core, got, kept)


def pack_kernel(planes, keep_ref, recv_ref, gz_ref, zf_ref, buf_ref, near_ref):
    chip = 2 * planes
    block = line_block(gz_ref, zf_ref, lax.axis_index("chip") * chip, chip)
    e0, e1 = planes - 1, chip - 1
    up = block[e1 : e1 + 1, e0 : e0 + 1] / block[e1 : e1 + 1, e1 : e1 + 1]
    down = block[0:1, planes : planes + 1] / block[0:1, 0:1]
    cross = block[planes : planes + 1, e0 : e0 + 1]
    dests, rows, span = buf_ref.shape
    half = rows // 2
    for d in range(dests):
        lanes = slice(d * span, (d + 1) * span)
        p0, p1 = chip_pair(keep_ref, recv_ref, slice(0, half), lanes)
        buf_ref[d, :half, :] = p1 + up * p0
        near_ref[:half, lanes] = cross * p0
        q0, q1 = chip_pair(keep_ref, recv_ref, slice(half, rows), lanes)
        buf_ref[d, half:, :] = q0 + down * q1
        near_ref[half:, lanes] = cross * q1


def unpack_kernel(planes, back_ref, near_ref, gz_ref, zf_ref, own_ref, sib_ref):
    chip = 2 * planes
    block = line_block(gz_ref, zf_ref, lax.axis_index("chip") * chip, chip)
    e0, b1, e1 = planes - 1, planes, chip - 1
    up = block[b1 : b1 + 1, 0:1] / block[0:1, 0:1]
    down = block[e0 : e0 + 1, e1 : e1 + 1] / block[e1 : e1 + 1, e1 : e1 + 1]
    lower_core = lax.axis_index("core") == 0
    dests, rows, span = back_ref.shape
    half = rows // 2
    for d in range(dests):
        lanes = slice(d * span, (d + 1) * span)
        below0 = back_ref[d, :half, :]
        below1 = up * below0 + near_ref[:half, lanes]
        above1 = back_ref[d, half:, :]
        above0 = down * above1 + near_ref[half:, lanes]
        own_ref[:half, lanes] = jnp.where(lower_core, below0, below1)
        own_ref[half:, lanes] = jnp.where(lower_core, above0, above1)
        sib_ref[:half, lanes] = jnp.where(lower_core, below1, below0)
        sib_ref[half:, lanes] = jnp.where(lower_core, above1, above0)


def inner_kernel(
    l_ref, y_ref, u_ref, gy_ref, yf_ref, gz_ref, zf_ref, wh_ref, wl_ref, bh_ref, bl_ref,
    out_ref, mark_ref, rows_ref, part_ref
):
    mark_ref[...] = jnp.zeros_like(mark_ref)
    blocks, rows, span = y_ref.shape
    planes = rows // 4
    cells = u_ref.shape[1]
    local = planes * cells
    dy = line_block(gy_ref, yf_ref, lax.axis_index("row") * cells, cells)
    dz = line_block(gz_ref, zf_ref, lax.axis_index(("chip", "core")) * planes, planes)
    from_last = dy[:, cells - 1 : cells] / dy[cells - 1 : cells, cells - 1 : cells]
    from_first = dy[:, 0:1] / dy[0:1, 0:1]
    lane = iota((1, LANES), 1)
    parts = []
    for z in range(planes):
        row = jnp.where(lane < planes, dz[z : z + 1, :], jnp.where(lane == planes + z, -2.0, 0.0))
        parts.append(from_first * row + from_last * pltpu.roll(row, 2 * planes, 1))
    mix = jnp.concatenate(parts, axis=0)[:, :rows]
    for s in range(blocks):
        at = slice(s * span, (s + 1) * span)
        rows_ref[:, at] = l_ref[:, at] + dot(mix, y_ref[s])

    def store(at, value):
        for z in range(planes):
            out_ref[z, :, at] = u_ref[z, :, at] + value[z * cells : (z + 1) * cells, :]

    x_solve(rows_ref, wh_ref, wl_ref, bh_ref, bl_ref, part_ref, store)


def final_kernel(
    s_hbm, own_ref, got_ref, gz_ref, zf_ref, wh_ref, wl_ref, bh_ref, bl_ref,
    out_hbm, x_ref, sx_ref, f_ref, in_sem, out_sem
):
    planes, cells = f_ref.shape[0], f_ref.shape[1]
    half = cells // 2

    def fetch(z):
        return pltpu.make_async_copy(s_hbm.at[z], f_ref.at[z], in_sem.at[z])

    def give(z):
        return pltpu.make_async_copy(f_ref.at[z], out_hbm.at[z], out_sem.at[z])

    for z in range(planes):
        fetch(z).start()
    mine = lax.axis_index("core")
    for k in range(2):
        at = slice(k * half, (k + 1) * half)
        own = pl.multiple_of(k * cells + mine * half, half)
        other = pl.multiple_of(k * cells + (1 - mine) * half, half)
        x_ref[pl.ds(own, half), :] = own_ref[at, :]
        x_ref[pl.ds(other, half), :] = got_ref[at, :]
    dz = line_block(gz_ref, zf_ref, lax.axis_index(("chip", "core")) * planes, planes)
    first = dz[:, 0:1] / dz[0:1, 0:1]
    last = dz[:, planes - 1 : planes] / dz[planes - 1 : planes, planes - 1 : planes]

    def store(at, value):
        sx_ref[:, at] = value

    x_solve(x_ref, wh_ref, wl_ref, bh_ref, bl_ref, sx_ref, store)
    for z in range(planes):
        low, high = first[z : z + 1, :], last[z : z + 1, :]
        fetch(z).wait()
        f_ref[z] = f_ref[z] + low * sx_ref[:cells, :] + high * sx_ref[cells:, :]
        give(z).start()
    for z in range(planes):
        give(z).wait()


def body(scalar_field, reaction, x_faces, y_faces, z_faces, x_inverse, y_inverse, z_inverse):
    planes, cells, width = scalar_field.shape
    local = planes * cells
    rows = lax.axis_size("row")
    chips = lax.axis_size("chip")
    xf, yf, zf = x_faces[None, :], y_faces[None, :], z_faces[None, :]
    sds = lambda *s: jax.ShapeDtypeStruct(s, F32)
    held = lambda *s: pltpu.VMEM(s, F32)

    far = pl.BlockSpec(memory_space=pltpu.HBM)
    near_by = pl.BlockSpec(memory_space=pltpu.VMEM)
    field = pltpu.VMEM((planes, cells, width), F32)
    a, y_buf = call(
        explicit_kernel,
        (sds(planes, cells, width), sds(rows, 4 * planes, width // rows)),
        20 * local * width,
        12 * local * width,
        "explicit",
        in_specs=[far] * 5,
        out_specs=(far, near_by),
        scratch_shapes=[
            field,
            field,
            field,
            pltpu.VMEM((1, width), F32),
            pltpu.VMEM((2, 128, 128), F32),
            pltpu.VMEM((1, 256), F32),
            pltpu.VMEM((8, width), F32),
            pltpu.SemaphoreType.DMA((planes,)),
            pltpu.SemaphoreType.DMA((planes,)),
            pltpu.SemaphoreType.DMA((planes,)),
            pltpu.SemaphoreType.DMA((3,)),
        ],
        room=60,
    )(scalar_field, reaction, xf, y_inverse, yf)
    y_in = lax.all_to_all(y_buf, "row", 0, 0, tiled=True)

    y_coef, z_coef = call(coef_kernel, (sds(32, LANES), sds(64, LANES)), 10**8, 10**6, "coefs")(
        y_inverse, yf, z_inverse, zf
    )
    half = lambda *s: jax.ShapeDtypeStruct(s, BF16)
    *weights, x_made = call(
        reduced_kernel,
        (
            half(16, 128, 256),
            half(16, 128, 256),
            half(32, width),
            half(32, width),
            held(8, LANES),
        ),
        10**9,
        2 * 10**6,
        "reduced",
        room=60,
    )(x_inverse, xf)
    chunks = 4
    field_chunks = pltpu.VMEM((chunks, planes, cells, width // chunks), F32)
    inside, z_part = call(
        local_kernel,
        (sds(local, width), held(2 * cells, width)),
        6 * 320 * 512 * width,
        14 * local * width,
        "local",
        in_specs=[far, far] + [near_by] * 4,
        out_specs=(far, near_by),
        scratch_shapes=[
            pltpu.VMEM((2 * (local + 2 * cells), 2 * local), BF16),
            pltpu.VMEM((chunks, local, width // chunks), F32),
            field_chunks,
            pltpu.VMEM((chunks, local, width // chunks), F32),
            pltpu.SemaphoreType.DMA((chunks,)),
            pltpu.SemaphoreType.DMA((chunks,)),
            pltpu.SemaphoreType.DMA((chunks,)),
        ],
        input_output_aliases={0: 0},
        room=61.5,
    )(a.reshape(local, width), scalar_field, y_inverse, yf, z_inverse, zf)

    y_out = call(scan_kernel, sds(*y_in.shape), 10**6, 10**6, "scan_y")(y_in, y_coef)
    y_back = lax.all_to_all(y_out, "row", 0, 0, tiled=True)

    keep, send = call(
        section_kernel,
        (sds(cells, width), sds(cells, width)),
        10**7,
        10**6,
        "section",
        scratch_shapes=[pltpu.VMEM((2 * cells, width), F32)],
    )(y_back, z_part, y_inverse, yf, z_inverse, zf)
    pairs = [(0, 1), (1, 0)]
    recv = lax.ppermute(send, "core", pairs)
    z_buf, near = call(
        functools.partial(pack_kernel, planes),
        (sds(chips, cells, width // chips), sds(cells, width)),
        10**6,
        10**6,
        "pack",
    )(keep, recv, z_inverse, zf)
    z_in = lax.all_to_all(z_buf, "chip", 0, 0, tiled=True)

    z_out = call_after(
        (x_made,), scan_kernel, sds(*z_in.shape), 10**6, 10**6, "scan_z", z_in, z_coef
    )
    z_back = lax.all_to_all(z_out, "chip", 0, 0, tiled=True)
    partial_out, inner_made = call(
        inner_kernel,
        (sds(planes, cells, width), held(8, LANES)),
        12 * local * width * 200,
        16 * local * width,
        "inner",
        scratch_shapes=[pltpu.VMEM((local, width), F32), pltpu.VMEM((local, width), F32)],
        room=60,
    )(inside, y_back, scalar_field, y_inverse, yf, z_inverse, zf, *weights)
    own, sib = call_after(
        (inner_made,),
        functools.partial(unpack_kernel, planes),
        (sds(cells, width), sds(cells, width)),
        10**6,
        10**6,
        "unpack",
        z_back,
        near,
        z_inverse,
        zf,
    )
    got = lax.ppermute(sib, "core", pairs)
    return call(
        final_kernel,
        sds(planes, cells, width),
        12 * local * width,
        8 * local * width,
        "final",
        in_specs=[far] + [near_by] * 8,
        out_specs=far,
        scratch_shapes=[
            pltpu.VMEM((2 * cells, width), F32),
            pltpu.VMEM((2 * cells, width), F32),
            field,
            pltpu.SemaphoreType.DMA((planes,)),
            pltpu.SemaphoreType.DMA((planes,)),
        ],
        input_output_aliases={0: 0},
    )(partial_out, own, got, z_inverse, zf, *weights)


def solution(mesh):
    rows, columns = mesh.shape["row"], mesh.shape["col"]
    split = Mesh(mesh.devices.reshape(rows, columns // 2, 2), ("row", "chip", "core"))
    field = P(("chip", "core"), "row", None)
    in_specs = (field, field, P(), P(), P(), P(), P(), P())
    return jax.shard_map(body, mesh=split, in_specs=in_specs, out_specs=field, check_vma=False)
```

time: 103 us -> 82.1 us (0.80)
  blocking collectives: 32.4 us -> 0 us
  starting transfers between devices: 17.4 us -> 30 us
  waiting for transfers between devices: 3.45 us -> 12.2 us
  local copies, waits for them, and re-layouts: 5.2 us -> 0.07 us
  Pallas kernels: 44.1 us -> 39.1 us
    all_to_all x2 -> x0, blocking collectives: 32.4 us -> none  [the longest x1 19.1 us: body(): lax.all_to_all(z_buf, 'col', 0, 0, axis_index_groups=groups, tiled=True)]
    all_to_all x0 -> x2, starting transfers between devices: none -> 11.8 us  [the longest x1 8.32 us: body(): z_in = lax.all_to_all(z_buf, 'chip', 0, 0, tiled=True)]
    all_to_all x0 -> x2, waiting for transfers between devices: none -> 5.92 us  [the longest x1 5.5 us: body(): z_in = lax.all_to_all(z_buf, 'chip', 0, 0, tiled=True)]
    unnamed x22 -> x30, local copies, waits for them, and re-layouts: 5.2 us -> 0.07 us
    pallas_call x1, Pallas kernels: 7.03 us -> 3.63 us  [body(): call(final_kernel, sds(planes, cells, width), 12 * local * width, 8 * loc...]
    all_to_all x1, waiting for transfers between devices: 0.01 us -> 1.71 us  [body(): y_back = lax.all_to_all(y_out, 'row', 0, 0, tiled=True)]
    ppermute x2, waiting for transfers between devices: 1.16 us -> 2.32 us  [the longest x1 1.16 us: body(): recv = lax.ppermute(send, 'core', pairs)]
  transfers between devices with their start and end apart: 4 -> 6, of which waited for: 2 -> 6; matrix products, arithmetic and copies ran while one was open for 0% -> 0% of each run, Pallas kernels for 27% -> 32%
where the time goes in v2:
time: 82.1 us; the launch traced here: 81.6 us
  Pallas kernels  39.1 us (48%)
  starting transfers between devices  30 us (37%)
  waiting for transfers between devices  12.2 us (15%)
    pallas_call x1, Pallas kernels, body(): call(inner_kernel, (sds(planes, cells, width), held(8, LANES)), 12 * loca...  9.16 us
    all_to_all x1, starting transfers between devices, body(): z_in = lax.all_to_all(z_buf, 'chip', 0, 0, tiled=True)  8.32 us
    all_to_all x1, starting transfers between devices, body(): y_in = lax.all_to_all(y_buf, 'row', 0, 0, tiled=True)  7.49 us
    pallas_call x1, Pallas kernels, body(): call(local_kernel, (sds(local, width), held(2 * cells, width)), 6 * 320 *...  5.88 us
    pallas_call x1, Pallas kernels, body(): call(explicit_kernel, (sds(planes, cells, width), sds(rows, 4 * planes, w...  5.87 us
    all_to_all x1, waiting for transfers between devices, body(): z_in = lax.all_to_all(z_buf, 'chip', 0, 0, tiled=True)  5.5 us
    pallas_call x1, Pallas kernels, body(): call(reduced_kernel, (half(16, 128, 256), half(16, 128, 256), half(32, wi...  5.48 us
    pallas_call x1, Pallas kernels, body(): call(coef_kernel, (sds(32, LANES), sds(64, LANES)), 10 ** 8, 10 ** 6, 'co...  5.32 us
  transfers between devices with their start and end apart: 6, of which 6 were waited for; matrix products, arithmetic and copies ran while one was open for 0% of the time, Pallas kernels for 32%

profile of v2, /device:TPU:1, one launch (start us, length us, event | category | flops | bytes accessed | tf_op | source)
XLA Modules:
  0.0 81.6 jit_solution(14436167256489717792)
XLA Ops:
  0.0 0.0 copy-start.13
  0.0 5.9 %explicit.1 = (f32[8,32,2048]{2,1,0:T(8,128)}, f32[8,32,256]{2,1,0:T(8,128)}) custom-call(f32[8,32,2048]{2,1,0:T(8,128)} %u_ref.1, f32[8,32,2048]{2,1,0:T(8,128)} %r_hbm.1, f32[1,2048]{1,0:T(1,128)} %bitcast.17, f32[2,128,128]{2,1,0:T(8,128)} %gy_ref.7, f32[1,256]{1,0:T(1,128)} %bitcast.11), custom_call_target="tpu_custom_call" | custom-call | flops 10485760 | bytes 6291456 | tf_op jit(solution)/shard_map/explicit/pallas_call | solution.py:512
  5.9 7.5 %all-to-all-start = ((f32[8,32,256]{2,1,0:T(8,128)}), f32[8,32,256]{2,1,0:T(8,128)S(1)}, u32[]{:S(2)}, u32[]{:S(2)}) async-start(f32[8,32,256]{2,1,0:T(8,128)} %get-tuple-element.26), calls=%async_computation | async-start | bytes 524288 | tf_op jit(solution)/shard_map/all_to_all | solution.py:535
  13.4 0.0 copy-done.2
  13.4 0.0 copy-done.6
  13.4 0.0 copy-done.10
  13.4 0.0 copy-done.13
  13.4 5.3 %coefs.1 = (f32[32,128]{1,0:T(8,128)S(1)}, f32[64,128]{1,0:T(8,128)S(1)}) custom-call(f32[2,128,128]{2,1,0:T(8,128)S(1)} %copy-done.6, f32[1,256]{1,0:T(1,128)S(1)} %bitcast.14, f32[2,128,128]{2,1,0:T(8,128)S(1)} %copy-done.2, f32[1,256]{1,0:T(1,128)S(1)} %bitcast.6), custom_call_target="tpu_custom_call" | custom-call | flops 100000000 | bytes 1000000 | tf_op jit(solution)/shard_map/coefs/pallas_call | solution.py:537
  18.7 2.3 %all-to-all-done.in_ref = f32[8,32,256]{2,1,0:T(8,128)S(1)} async-done(((f32[8,32,256]{2,1,0:T(8,128)}), f32[8,32,256]{2,1,0:T(8,128)S(1)}, u32[]{:S(2)}, u32[]{:S(2)}) %all-to-all-start) | async-done | bytes 262176 | tf_op jit(solution)/shard_map/all_to_all | solution.py:535
  21.0 0.8 scan_y.1
  21.8 4.4 %all-to-all-start.1 = ((f32[8,32,256]{2,1,0:T(8,128)}), f32[8,32,256]{2,1,0:T(8,128)S(1)}, u32[]{:S(2)}, u32[]{:S(2)}) async-start(f32[8,32,256]{2,1,0:T(8,128)} %scan_y.1), calls=%async_computation.1 | async-start | bytes 524288 | tf_op jit(solution)/shard_map/all_to_all | solution.py:579
  26.2 0.0 copy-start.7
  26.2 0.0 copy-start.11
  26.2 0.0 copy-start.14
  26.2 5.9 %local.1 = (f32[256,2048]{1,0:T(8,128)}, f32[64,2048]{1,0:T(8,128)S(1)}) custom-call(f32[256,2048]{1,0:T(8,128)} %bitcast.16, f32[8,32,2048]{2,1,0:T(8,128)} %u_ref.1, f32[2,128,128]{2,1,0:T(8,128)} %gy_ref.7, f32[1,256]{1,0:T(1,128)} %bitcast.12, f32[2,128,128]{2,1,0:T(8,128)} %gz_ref.11, f32[1,256]{1,0:T(1,128)} %bitcast.4), custom_call_target="tpu_custom_call", output_to_operand_aliasing={{0}: (0, {})} | custom-call | flops 2013265920 | bytes 7340032 | tf_op jit(solution)/shard_map/local/pallas_call | solution.py:557
  32.1 1.7 %all-to-all-done.1.y_ref = f32[8,32,256]{2,1,0:T(8,128)S(1)} async-done(((f32[8,32,256]{2,1,0:T(8,128)}), f32[8,32,256]{2,1,0:T(8,128)S(1)}, u32[]{:S(2)}, u32[]{:S(2)}) %all-to-all-start.1) | async-done | bytes 262176 | tf_op jit(solution)/shard_map/all_to_all | solution.py:579
  33.8 0.0 copy-done.3
  33.8 0.0 copy-done.7
  33.8 0.0 copy-done.11
  33.8 0.0 copy-done.14
  33.8 0.6 section.1
  34.4 2.8 %collective-permute-start = (f32[32,2048]{1,0:T(8,128)S(1)}, f32[32,2048]{1,0:T(8,128)S(1)}, u32[]{:S(2)}, u32[]{:S(2)}) collective-permute-start(f32[32,2048]{1,0:T(8,128)S(1)} %get-tuple-element.35), channel_id=1, source_target_pairs={{0,1},{1,0},{2,3},{3,2},{4,5},{5,4},{6,7},{7,6},{8,9},{9,8},{10,11... | collective-permute-start | bytes 786440 | tf_op jit(solution)/shard_map/ppermute | solution.py:590
  37.2 1.2 %collective-permute-done.recv_ref = f32[32,2048]{1,0:T(8,128)S(1)} collective-permute-done((f32[32,2048]{1,0:T(8,128)S(1)}, f32[32,2048]{1,0:T(8,128)S(1)}, u32[]{:S(2)}, u32[]{:S(2)}) %collective-permute-start) | collective-permute-done | bytes 262176 | tf_op jit(solution)/shard_map/ppermute | solution.py:590
  38.3 1.2 %pack.1 = (f32[16,32,128]{2,1,0:T(8,128)}, f32[32,2048]{1,0:T(8,128)S(1)}) custom-call(f32[32,2048]{1,0:T(8,128)S(1)} %get-tuple-element.34.keep_ref, f32[32,2048]{1,0:T(8,128)S(1)} %collective-permute-done.recv_ref, f32[2,128,128]{2,1,0:T(8,128)S(1)} %copy-done.3, f32[1,256]{1,0:T(1,128)S(1)} %bitcast.8), custom_call_target="tpu_custom_call" | custom-call | flops 1000000 | bytes 1000000 | tf_op jit(solution)/shard_map/pack/pallas_call | solution.py:591
  39.5 8.3 %all-to-all-start.2 = ((f32[16,32,128]{2,1,0:T(8,128)}), f32[16,32,128]{2,1,0:T(8,128)S(1)}, u32[]{:S(2)}, u32[]{:S(2)}) async-start(f32[16,32,128]{2,1,0:T(8,128)} %get-tuple-element.36), calls=%async_computation.2 | async-start | bytes 524288 | tf_op jit(solution)/shard_map/all_to_all | solution.py:598
  47.9 5.5 %reduced.1 = (bf16[16,128,256]{2,1,0:T(8,128)(2,1)}, bf16[16,128,256]{2,1,0:T(8,128)(2,1)}, bf16[32,2048]{1,0:T(8,128)(2,1)}, bf16[32,2048]{1,0:T(8,128)(2,1)}, f32[8,128]{1,0:T(8,128)S(1)}) custom-call(f32[16,128,128]{2,1,0:T(8,128)} %g_ref.1, f32[1,2048]{1,0:T(1,128)} %bitcast.18), custom_call_target="tpu_custom_call" | custom-call | flops 1000000000 | bytes 2000000 | tf_op jit(solution)/shard_map/reduced/pallas_call | solution.py:541
  53.3 0.0 copy-done.5
  53.3 5.5 %all-to-all-done.2.refs_0_ = f32[16,32,128]{2,1,0:T(8,128)S(1)} async-done(((f32[16,32,128]{2,1,0:T(8,128)}), f32[16,32,128]{2,1,0:T(8,128)S(1)}, u32[]{:S(2)}, u32[]{:S(2)}) %all-to-all-start.2) | async-done | bytes 262176 | tf_op jit(solution)/shard_map/all_to_all | solution.py:598
  58.8 0.8 scan_z.1
  59.6 3.5 %all-to-all-start.3 = ((f32[16,32,128]{2,1,0:T(8,128)}), f32[16,32,128]{2,1,0:T(8,128)S(1)}, u32[]{:S(2)}, u32[]{:S(2)}) async-start(f32[16,32,128]{2,1,0:T(8,128)} %scan_z.1), calls=%async_computation.3 | async-start | bytes 524288 | tf_op jit(solution)/shard_map/all_to_all | solution.py:603
  63.2 0.0 copy-start.4
  63.2 0.0 copy-start.12
  63.2 0.0 copy-start
  63.2 0.0 copy-start.1
  63.2 0.0 copy-start.8
  63.2 0.0 copy-start.9
  63.2 9.2 %inner.1 = (f32[8,32,2048]{2,1,0:T(8,128)}, f32[8,128]{1,0:T(8,128)S(1)}) custom-call(f32[256,2048]{1,0:T(8,128)} %get-tuple-element.25.l_ref, f32[8,32,256]{2,1,0:T(8,128)} %copy-done.5, f32[8,32,2048]{2,1,0:T(8,128)} %u_ref.1, f32[2,128,128]{2,1,0:T(8,128)} %gy_ref.7, f32[1,256]{1,0:T(1,128)} %bitcast.13, f32[2,128,128]{2,1,0:T(8,128)} %gz_ref.11, ...), custom_call_target="tpu_custom_call" | custom-call | flops 1258291200 | bytes 8388608 | tf_op jit(solution)/shard_map/inner/pallas_call | solution.py:604
  72.4 0.4 all-to-all-done.3.refs_0_
  72.8 0.0 copy-done.4
  72.8 0.0 copy-done.12
  72.8 0.4 unpack.1
  73.3 3.5 %collective-permute-start.1 = (f32[32,2048]{1,0:T(8,128)S(1)}, f32[32,2048]{1,0:T(8,128)S(1)}, u32[]{:S(2)}, u32[]{:S(2)}) collective-permute-start(f32[32,2048]{1,0:T(8,128)S(1)} %get-tuple-element.42), channel_id=1, source_target_pairs={{0,1},{1,0},{2,3},{3,2},{4,5},{5,4},{6,7},{7,6},{8,9},{9,8},{10,11... | collective-permute-start | bytes 786440 | tf_op jit(solution)/shard_map/ppermute | solution.py:625
  76.8 1.2 %collective-permute-done.1.got_ref = f32[32,2048]{1,0:T(8,128)S(1)} collective-permute-done((f32[32,2048]{1,0:T(8,128)S(1)}, f32[32,2048]{1,0:T(8,128)S(1)}, u32[]{:S(2)}, u32[]{:S(2)}) %collective-permute-start.1) | collective-permute-done | bytes 262176 | tf_op jit(solution)/shard_map/ppermute | solution.py:625
  77.9 0.0 copy-done
  77.9 0.0 copy-done.1
  77.9 0.0 copy-done.8
  77.9 0.0 copy-done.9
  77.9 3.6 %final.1 = f32[8,32,2048]{2,1,0:T(8,128)} custom-call(f32[8,32,2048]{2,1,0:T(8,128)} %get-tuple-element.32.s_hbm, f32[32,2048]{1,0:T(8,128)S(1)} %get-tuple-element.41.own_ref, f32[32,2048]{1,0:T(8,128)S(1)} %collective-permute-done.1.got_ref, f32[2,128,128]{2,1,0:T(8,128)S(1)} %copy-done.4, f32[1,256]{1,0:T(1,128)S(1)} %bitcast.10, ...), custom_call_target="tpu_custom_call", output_to_operand_aliasing={{}: (0, {})} | custom-call | flops 6291456 | bytes 4194304 | tf_op jit(solution)/shard_map/final/pallas_call | solution.py:626
  (5 shorter events, 0.0 us)
Async XLA Ops:
  0.0 13.4 %copy-start.2 = (f32[2,128,128]{2,1,0:T(8,128)S(1)}, f32[2,128,128]{2,1,0:T(8,128)}, u32[]{:S(2)}) copy-start(f32[2,128,128]{2,1,0:T(8,128)} %gz_ref.11) | copy-start | bytes 393220
  0.0 13.4 %copy-start.6 = (f32[2,128,128]{2,1,0:T(8,128)S(1)}, f32[2,128,128]{2,1,0:T(8,128)}, u32[]{:S(2)}) copy-start(f32[2,128,128]{2,1,0:T(8,128)} %gy_ref.7) | copy-start | bytes 393220
  0.0 13.4 %copy-start.10 = (f32[256]{0:T(256)S(1)}, f32[256]{0:T(256)}, u32[]{:S(2)}) copy-start(f32[256]{0:T(256)} %param.12) | copy-start | bytes 3076
  0.0 13.4 %copy-start.13 = (f32[256]{0:T(256)S(1)}, f32[256]{0:T(256)}, u32[]{:S(2)}) copy-start(f32[256]{0:T(256)} %param.11) | copy-start | bytes 3076
  5.9 15.1 %all-to-all-start = ((f32[8,32,256]{2,1,0:T(8,128)}), f32[8,32,256]{2,1,0:T(8,128)S(1)}, u32[]{:S(2)}, u32[]{:S(2)}) async-start(f32[8,32,256]{2,1,0:T(8,128)} %get-tuple-element.26), calls=%async_computation | async-start | bytes 524288 | tf_op jit(solution)/shard_map/all_to_all | solution.py:535
  21.8 12.0 %all-to-all-start.1 = ((f32[8,32,256]{2,1,0:T(8,128)}), f32[8,32,256]{2,1,0:T(8,128)S(1)}, u32[]{:S(2)}, u32[]{:S(2)}) async-start(f32[8,32,256]{2,1,0:T(8,128)} %scan_y.1), calls=%async_computation.1 | async-start | bytes 524288 | tf_op jit(solution)/shard_map/all_to_all | solution.py:579
  26.2 7.6 %copy-start.3 = (f32[2,128,128]{2,1,0:T(8,128)S(1)}, f32[2,128,128]{2,1,0:T(8,128)}, u32[]{:S(2)}) copy-start(f32[2,128,128]{2,1,0:T(8,128)} %gz_ref.11) | copy-start | bytes 393220
  26.2 7.6 %copy-start.7 = (f32[2,128,128]{2,1,0:T(8,128)S(1)}, f32[2,128,128]{2,1,0:T(8,128)}, u32[]{:S(2)}) copy-start(f32[2,128,128]{2,1,0:T(8,128)} %gy_ref.7) | copy-start | bytes 393220
  26.2 7.6 %copy-start.11 = (f32[256]{0:T(256)S(1)}, f32[256]{0:T(256)}, u32[]{:S(2)}) copy-start(f32[256]{0:T(256)} %param.12) | copy-start | bytes 3076
  26.2 7.6 %copy-start.14 = (f32[256]{0:T(256)S(1)}, f32[256]{0:T(256)}, u32[]{:S(2)}) copy-start(f32[256]{0:T(256)} %param.11) | copy-start | bytes 3076
  33.8 19.5 %copy-start.5 = (f32[8,32,256]{2,1,0:T(8,128)}, f32[8,32,256]{2,1,0:T(8,128)S(1)}, u32[]{:S(2)}) copy-start(f32[8,32,256]{2,1,0:T(8,128)S(1)} %all-to-all-done.1.y_ref) | copy-start | bytes 786436
  34.4 3.9 %collective-permute-start = (f32[32,2048]{1,0:T(8,128)S(1)}, f32[32,2048]{1,0:T(8,128)S(1)}, u32[]{:S(2)}, u32[]{:S(2)}) collective-permute-start(f32[32,2048]{1,0:T(8,128)S(1)} %get-tuple-element.35), channel_id=1, source_target_pairs={{0,1},{1,0},{2,3},{3,2},{4,5},{5,4},{6,7},{7,6},{8,9},{9,8},{10,11... | collective-permute-start | bytes 786440 | tf_op jit(solution)/shard_map/ppermute | solution.py:590
  39.5 19.3 %all-to-all-start.2 = ((f32[16,32,128]{2,1,0:T(8,128)}), f32[16,32,128]{2,1,0:T(8,128)S(1)}, u32[]{:S(2)}, u32[]{:S(2)}) async-start(f32[16,32,128]{2,1,0:T(8,128)} %get-tuple-element.36), calls=%async_computation.2 | async-start | bytes 524288 | tf_op jit(solution)/shard_map/all_to_all | solution.py:598
  59.6 13.2 %all-to-all-start.3 = ((f32[16,32,128]{2,1,0:T(8,128)}), f32[16,32,128]{2,1,0:T(8,128)S(1)}, u32[]{:S(2)}, u32[]{:S(2)}) async-start(f32[16,32,128]{2,1,0:T(8,128)} %scan_z.1), calls=%async_computation.3 | async-start | bytes 524288 | tf_op jit(solution)/shard_map/all_to_all | solution.py:603
  63.2 9.6 %copy-start.4 = (f32[2,128,128]{2,1,0:T(8,128)S(1)}, f32[2,128,128]{2,1,0:T(8,128)}, u32[]{:S(2)}) copy-start(f32[2,128,128]{2,1,0:T(8,128)} %gz_ref.11) | copy-start | bytes 393220
  63.2 9.6 %copy-start.12 = (f32[256]{0:T(256)S(1)}, f32[256]{0:T(256)}, u32[]{:S(2)}) copy-start(f32[256]{0:T(256)} %param.12) | copy-start | bytes 3076
  63.2 14.7 %copy-start = (bf16[16,128,256]{2,1,0:T(8,128)(2,1)S(1)}, bf16[16,128,256]{2,1,0:T(8,128)(2,1)}, u32[]{:S(2)}) copy-start(bf16[16,128,256]{2,1,0:T(8,128)(2,1)} %get-tuple-element.28.wh_ref) | copy-start | bytes 3145732
  63.2 14.7 %copy-start.1 = (bf16[16,128,256]{2,1,0:T(8,128)(2,1)S(1)}, bf16[16,128,256]{2,1,0:T(8,128)(2,1)}, u32[]{:S(2)}) copy-start(bf16[16,128,256]{2,1,0:T(8,128)(2,1)} %get-tuple-element.29.wl_ref) | copy-start | bytes 3145732
  63.2 14.7 %copy-start.8 = (bf16[32,2048]{1,0:T(8,128)(2,1)S(1)}, bf16[32,2048]{1,0:T(8,128)(2,1)}, u32[]{:S(2)}) copy-start(bf16[32,2048]{1,0:T(8,128)(2,1)} %get-tuple-element.30.bh_ref) | copy-start | bytes 393220
  63.2 14.7 %copy-start.9 = (bf16[32,2048]{1,0:T(8,128)(2,1)S(1)}, bf16[32,2048]{1,0:T(8,128)(2,1)}, u32[]{:S(2)}) copy-start(bf16[32,2048]{1,0:T(8,128)(2,1)} %get-tuple-element.31.bl_ref) | copy-start | bytes 393220
  73.3 4.7 %collective-permute-start.1 = (f32[32,2048]{1,0:T(8,128)S(1)}, f32[32,2048]{1,0:T(8,128)S(1)}, u32[]{:S(2)}, u32[]{:S(2)}) collective-permute-start(f32[32,2048]{1,0:T(8,128)S(1)} %get-tuple-element.42), channel_id=1, source_target_pairs={{0,1},{1,0},{2,3},{3,2},{4,5},{5,4},{6,7},{7,6},{8,9},{9,8},{10,11... | collective-permute-start | bytes 786440 | tf_op jit(solution)/shard_map/ppermute | solution.py:625

commit v3 on v2

--- a/solution.py
+++ b/solution.py
@@ -92,8 +92,8 @@
 
 
 def explicit_kernel(
-    u_hbm, r_hbm, xf_hbm, gy_hbm, yf_hbm, a_hbm, buf_ref,
-    u_ref, r_ref, a_ref, xf_ref, gy_ref, yf_ref, f_ref, u_sem, r_sem, a_sem, s_sem
+    u_hbm, r_hbm, xf_hbm, gy_hbm, yf_hbm, a_hbm, ends_ref,
+    buf_ref, u_ref, r_ref, a_ref, xf_ref, gy_ref, yf_ref, f_ref, u_sem, r_sem, a_sem, s_sem
 ):
     planes, cells, width = u_ref.shape
     small = [
@@ -168,28 +168,68 @@
         return carry
 
     lax.fori_loop(0, planes, plane, 0)
+    for d in range(width // span):
+        ends_ref[:, d * span : (d + 1) * span] = buf_ref[d]
     for z in range(planes):
         give(z).wait()
 
 
-def coef_kernel(gy_ref, yf_ref, gz_ref, zf_ref, yc_ref, zc_ref):
-    for g_ref, f_ref, out_ref, count in ((gy_ref, yf_ref, yc_ref, 8), (gz_ref, zf_ref, zc_ref, 16)):
-        joined = joint(g_ref, f_ref)
-        size = 256 // count
-        m = functools.partial(element, g_ref, joined)
-        out_ref[...] = jnp.zeros_like(out_ref)
-        for c in range(count):
-            b, e = c * size, c * size + size - 1
-            if c > 0:
-                ee = m(e, e - size) / m(e, e)
-                be = m(b, b - 1)
-                out_ref[c : c + 1, :] = jnp.broadcast_to(ee, (1, LANES))
-                out_ref[count + c : count + c + 1, :] = jnp.broadcast_to(be, (1, LANES))
-            if c < count - 1:
-                bb = m(b, b + size) / m(b, b)
-                eb = m(e, e + 1)
-                out_ref[2 * count + c : 2 * count + c + 1, :] = jnp.broadcast_to(bb, (1, LANES))
-                out_ref[3 * count + c : 3 * count + c + 1, :] = jnp.broadcast_to(eb, (1, LANES))
+def coef_kernel(count, g_ref, f_ref, out_ref):
+    joined = joint(g_ref, f_ref)
+    size = 256 // count
+    m = functools.partial(element, g_ref, joined)
+    out_ref[...] = jnp.zeros_like(out_ref)
+    for c in range(count):
+        b, e = c * size, c * size + size - 1
+        if c > 0:
+            ee = m(e, e - size) / m(e, e)
+            be = m(b, b - 1)
+            out_ref[c : c + 1, :] = jnp.broadcast_to(ee, (1, LANES))
+            out_ref[count + c : count + c + 1, :] = jnp.broadcast_to(be, (1, LANES))
+        if c < count - 1:
+            bb = m(b, b + size) / m(b, b)
+            eb = m(e, e + 1)
+            out_ref[2 * count + c : 2 * count + c + 1, :] = jnp.broadcast_to(bb, (1, LANES))
+            out_ref[3 * count + c : 3 * count + c + 1, :] = jnp.broadcast_to(eb, (1, LANES))
+
+
+def line_rows(g_ref, faces_ref, start, size):
+    alpha0, alpha1, beta = joint(g_ref, faces_ref)
+    group = start // 128
+    offset = start - group * 128
+    rows = g_ref[group, pl.ds(pl.multiple_of(offset, size), size), :]
+    low = group == 0
+    edge = jnp.where(low, rows[:, 127:128], rows[:, 0:1])
+    end0, end1 = g_ref[0, 127:128, :], g_ref[1, 0:1, :]
+    left = jnp.where(low, rows + (alpha0 * edge) * end0, (beta * edge) * end0)
+    right = jnp.where(low, (beta * edge) * end1, rows + (alpha1 * edge) * end1)
+    return left, right
+
+
+def pair_kernel(cells, rings, mine_ref, got_ref, gy_ref, yf_ref, *out_refs):
+    *send_refs, near_ref = out_refs
+    r = lax.axis_index("row")
+    pair = r // 2
+    lower = r % 2 == 0
+    block = line_block(gy_ref, yf_ref, pair * (2 * cells), 2 * cells)
+    e0, b1, e1 = cells - 1, cells, 2 * cells - 1
+    up = block[e1 : e1 + 1, e0 : e0 + 1] / block[e1 : e1 + 1, e1 : e1 + 1]
+    down = block[0:1, b1 : b1 + 1] / block[0:1, 0:1]
+    cross = block[b1 : b1 + 1, e0 : e0 + 1]
+    half = mine_ref.shape[0] // 2
+    span = 512
+    for s in range(mine_ref.shape[1] // span):
+        at = slice(s * span, (s + 1) * span)
+        p, p_got = mine_ref[:half, at], got_ref[:half, at]
+        q, q_got = mine_ref[half:, at], got_ref[half:, at]
+        p0, p1 = jnp.where(lower, p, p_got), jnp.where(lower, p_got, p)
+        q0, q1 = jnp.where(lower, q, q_got), jnp.where(lower, q_got, q)
+        below = p1 + up * p0
+        above = q0 + down * q1
+        for k, send_ref in enumerate(send_refs):
+            send_ref[:, at] = jnp.where(pair + k + 1 < rings, below, above)
+        near_ref[:half, at] = jnp.where(lower, 0.0, cross * p0)
+        near_ref[half:, at] = jnp.where(lower, cross * q1, 0.0)
 
 
 def scan_kernel(in_ref, c_ref, out_ref):
@@ -352,27 +392,47 @@
 
 
 def section_kernel(
-    y_ref, zp_ref, gy_ref, yf_ref, gz_ref, zf_ref, keep_ref, send_ref, all_ref
+    near_ref, r1_ref, r2_ref, r3_ref, zp_ref, gy_ref, yf_ref, gz_ref, zf_ref,
+    keep_ref, send_ref, rows_ref, all_ref
 ):
-    blocks, rows, span = y_ref.shape
+    rows, width = near_ref.shape
     cells = zp_ref.shape[0] // 2
     planes = rows // 4
     mine = lax.axis_index("core")
-    dy = line_block(gy_ref, yf_ref, lax.axis_index("row") * cells, cells)
+    r = lax.axis_index("row")
+    pair = r // 2
+    dy = line_block(gy_ref, yf_ref, r * cells, cells)
     dz = line_block(gz_ref, zf_ref, lax.axis_index(("chip", "core")) * planes, planes)
     from_last = dy[:, cells - 1 : cells] / dy[cells - 1 : cells, cells - 1 : cells]
     from_first = dy[:, 0:1] / dy[0:1, 0:1]
     last = dz[:, planes - 1 : planes] / dz[planes - 1 : planes, planes - 1 : planes]
     first = dz[:, 0:1] / dz[0:1, 0:1]
-    for s in range(blocks):
+    full = line_rows(gy_ref, yf_ref, r * cells, cells)
+    step = 2 * cells
+    below, above = [], []
+    for k in range(1, 4):
+        lo = hi = jnp.zeros((1, 1), F32)
+        for t in range(4):
+            b, e = t * step % 128, t * step % 128 + step - 1
+            part = full[t * step // 128]
+            lo = jnp.where(pair - k == t, part[0:1, e : e + 1], lo)
+            hi = jnp.where(pair - k + 4 == t, part[cells - 1 : cells, b : b + 1], hi)
+        below.append(lo)
+        above.append(hi)
+    half = rows // 2
+    span = 256
+    for s in range(width // span):
         at = slice(s * span, (s + 1) * span)
-        below = y_ref[s, 0:planes, :]
-        above = y_ref[s, 2 * planes : 3 * planes, :]
+        got = [ref[:, at] for ref in (r1_ref, r2_ref, r3_ref)]
+        lo = near_ref[:half, at] + sum(c * g for c, g in zip(below, got))
+        hi = near_ref[half:, at] + sum(c * g for c, g in zip(above, got))
+        rows_ref[:half, at] = lo
+        rows_ref[half:, at] = hi
         for k, w in enumerate((last, first)):
-            lo = jnp.sum(w * below, axis=0, keepdims=True)
-            hi = jnp.sum(w * above, axis=0, keepdims=True)
+            low = jnp.sum(w * lo[:planes], axis=0, keepdims=True)
+            high = jnp.sum(w * hi[:planes], axis=0, keepdims=True)
             own = slice(k * cells, (k + 1) * cells)
-            all_ref[own, at] = zp_ref[own, at] + from_first * lo + from_last * hi
+            all_ref[own, at] = zp_ref[own, at] + from_first * low + from_last * high
     half = cells // 2
     for k in range(2):
         at = slice(k * half, (k + 1) * half)
@@ -433,7 +493,7 @@
     out_ref, mark_ref, rows_ref, part_ref
 ):
     mark_ref[...] = jnp.zeros_like(mark_ref)
-    blocks, rows, span = y_ref.shape
+    rows, width = y_ref.shape
     planes = rows // 4
     cells = u_ref.shape[1]
     local = planes * cells
@@ -447,9 +507,10 @@
         row = jnp.where(lane < planes, dz[z : z + 1, :], jnp.where(lane == planes + z, -2.0, 0.0))
         parts.append(from_first * row + from_last * pltpu.roll(row, 2 * planes, 1))
     mix = jnp.concatenate(parts, axis=0)[:, :rows]
-    for s in range(blocks):
+    span = 256
+    for s in range(width // span):
         at = slice(s * span, (s + 1) * span)
-        rows_ref[:, at] = l_ref[:, at] + dot(mix, y_ref[s])
+        rows_ref[:, at] = l_ref[:, at] + dot(mix, y_ref[:, at])
 
     def store(at, value):
         for z in range(planes):
@@ -509,15 +570,16 @@
     far = pl.BlockSpec(memory_space=pltpu.HBM)
     near_by = pl.BlockSpec(memory_space=pltpu.VMEM)
     field = pltpu.VMEM((planes, cells, width), F32)
-    a, y_buf = call(
+    a, ends = call(
         explicit_kernel,
-        (sds(planes, cells, width), sds(rows, 4 * planes, width // rows)),
+        (sds(planes, cells, width), held(4 * planes, width)),
         20 * local * width,
         12 * local * width,
         "explicit",
         in_specs=[far] * 5,
         out_specs=(far, near_by),
         scratch_shapes=[
+            pltpu.VMEM((8, 4 * planes, width // 8), F32),
             field,
             field,
             field,
@@ -532,11 +594,11 @@
         ],
         room=60,
     )(scalar_field, reaction, xf, y_inverse, yf)
-    y_in = lax.all_to_all(y_buf, "row", 0, 0, tiled=True)
-
-    y_coef, z_coef = call(coef_kernel, (sds(32, LANES), sds(64, LANES)), 10**8, 10**6, "coefs")(
-        y_inverse, yf, z_inverse, zf
-    )
+    got_ends = lax.ppermute(ends, "row", [(i, i ^ 1) for i in range(rows)])
+
+    z_coef = call(
+        functools.partial(coef_kernel, chips), held(4 * chips, LANES), 10**8, 10**6, "coefs"
+    )(z_inverse, zf)
     half = lambda *s: jax.ShapeDtypeStruct(s, BF16)
     *weights, x_made = call(
         reduced_kernel,
@@ -575,17 +637,31 @@
         room=61.5,
     )(a.reshape(local, width), scalar_field, y_inverse, yf, z_inverse, zf)
 
-    y_out = call(scan_kernel, sds(*y_in.shape), 10**6, 10**6, "scan_y")(y_in, y_coef)
-    y_back = lax.all_to_all(y_out, "row", 0, 0, tiled=True)
-
-    keep, send = call(
+    *sums, near_y = call_after(
+        (z_coef,),
+        functools.partial(pair_kernel, cells, rows // 2),
+        tuple(sds(2 * planes, width) for _ in range(3)) + (sds(4 * planes, width),),
+        10**6,
+        10**6,
+        "pair",
+        ends,
+        got_ends,
+        y_inverse,
+        yf,
+    )
+    got_sums = [
+        lax.ppermute(total, "row", [(i, (i + 2 * k + 2) % rows) for i in range(rows)])
+        for k, total in enumerate(sums)
+    ]
+
+    keep, send, y_rows = call(
         section_kernel,
-        (sds(cells, width), sds(cells, width)),
+        (sds(cells, width), sds(cells, width), sds(4 * planes, width)),
         10**7,
         10**6,
         "section",
         scratch_shapes=[pltpu.VMEM((2 * cells, width), F32)],
-    )(y_back, z_part, y_inverse, yf, z_inverse, zf)
+    )(near_y, *got_sums, z_part, y_inverse, yf, z_inverse, zf)
     pairs = [(0, 1), (1, 0)]
     recv = lax.ppermute(send, "core", pairs)
     z_buf, near = call(
@@ -609,7 +685,7 @@
         "inner",
         scratch_shapes=[pltpu.VMEM((local, width), F32), pltpu.VMEM((local, width), F32)],
         room=60,
-    )(inside, y_back, scalar_field, y_inverse, yf, z_inverse, zf, *weights)
+    )(inside, y_rows, scalar_field, y_inverse, yf, z_inverse, zf, *weights)
     own, sib = call_after(
         (inner_made,),
         functools.partial(unpack_kernel, planes),

time: 82.1 us -> 75.3 us (0.917)
  Pallas kernels: 39.1 us -> 34.6 us
  starting transfers between devices: 30 us -> 28.4 us
    all_to_all x2 -> x0, starting transfers between devices: 11.9 us -> none  [the longest x1 7.49 us: body(): y_in = lax.all_to_all(y_buf, 'row', 0, 0, tiled=True)]
    ppermute x0 -> x4, starting transfers between devices: none -> 9.68 us  [the longest x3 6.02 us: body(): lax.ppermute(total, 'row', [(i, (i + 2 * k + 2) % rows) for i in range(ro...]
    pallas_call x4 -> x3, Pallas kernels: 12.5 us -> 7.5 us  [the longest x1 5.17 us: body(): call(explicit_kernel, (sds(planes, cells, width), held(4 * planes, width)...]
    all_to_all x2 -> x0, waiting for transfers between devices: 4 us -> none  [the longest x1 2.29 us: body(): y_in = lax.all_to_all(y_buf, 'row', 0, 0, tiled=True)]
    ppermute x0 -> x4, waiting for transfers between devices: none -> 3.42 us  [the longest x1 3.42 us: body(): got_ends = lax.ppermute(ends, 'row', [(i, i ^ 1) for i in range(rows)])]
    all_to_all x1, starting transfers between devices: 8.32 us -> 9.21 us  [body(): z_in = lax.all_to_all(z_buf, 'chip', 0, 0, tiled=True)]
    pallas_call x2 -> x3, Pallas kernels: 1.21 us -> 1.74 us  [call_after(): call(ordered, out_shape, flops, nbytes, name, in_specs=specs, **kw)]
  transfers between devices with their start and end apart: 6 -> 8, of which waited for: 6 -> 5; matrix products, arithmetic and copies ran while one was open for 0% -> 0% of each run, Pallas kernels for 32% -> 29%
where the time goes in v3:
time: 75.3 us; the launch traced here: 74.9 us
  Pallas kernels  34.6 us (46%)
  starting transfers between devices  28.4 us (38%)
  waiting for transfers between devices  11.7 us (16%)
    all_to_all x1, starting transfers between devices, body(): z_in = lax.all_to_all(z_buf, 'chip', 0, 0, tiled=True)  9.21 us
    pallas_call x1, Pallas kernels, body(): call(inner_kernel, (sds(planes, cells, width), held(8, LANES)), 12 * loca...  9.16 us
    ppermute x3, starting transfers between devices, body(): lax.ppermute(total, 'row', [(i, (i + 2 * k + 2) % rows) for i in range(ro...  6.02 us
    pallas_call x1, Pallas kernels, body(): call(local_kernel, (sds(local, width), held(2 * cells, width)), 6 * 320 *...  5.85 us
    all_to_all x1, waiting for transfers between devices, body(): z_in = lax.all_to_all(z_buf, 'chip', 0, 0, tiled=True)  5.5 us
    pallas_call x1, Pallas kernels, body(): call(reduced_kernel, (half(16, 128, 256), half(16, 128, 256), half(32, wi...  5.48 us
    pallas_call x1, Pallas kernels, body(): call(explicit_kernel, (sds(planes, cells, width), held(4 * planes, width)...  5.17 us
    ppermute x1, starting transfers between devices, body(): got_ends = lax.ppermute(ends, 'row', [(i, i ^ 1) for i in range(rows)])  3.66 us
  transfers between devices with their start and end apart: 8, of which 5 were waited for; matrix products, arithmetic and copies ran while one was open for 0% of the time, Pallas kernels for 29%

profile of v3, /device:TPU:1, one launch (start us, length us, event | category | flops | bytes accessed | tf_op | source)
XLA Modules:
  0.0 74.9 jit_solution(18176044108559899538)
XLA Ops:
  0.0 0.0 copy-start.13
  0.0 5.2 %explicit.1 = (f32[8,32,2048]{2,1,0:T(8,128)}, f32[32,2048]{1,0:T(8,128)S(1)}) custom-call(f32[8,32,2048]{2,1,0:T(8,128)} %u_ref.1, f32[8,32,2048]{2,1,0:T(8,128)} %r_hbm.1, f32[1,2048]{1,0:T(1,128)} %bitcast.17, f32[2,128,128]{2,1,0:T(8,128)} %gy_ref.5, f32[1,256]{1,0:T(1,128)} %bitcast.11), custom_call_target="tpu_custom_call" | custom-call | flops 10485760 | bytes 6291456 | tf_op jit(solution)/shard_map/explicit/pallas_call | solution.py:573
  5.2 3.7 %collective-permute-start = (f32[32,2048]{1,0:T(8,128)S(1)}, f32[32,2048]{1,0:T(8,128)S(1)}, u32[]{:S(2)}, u32[]{:S(2)}) collective-permute-start(f32[32,2048]{1,0:T(8,128)S(1)} %get-tuple-element.29.refs_0_), channel_id=1, source_target_pairs={{0,32},{32,0},{64,96},{96,64},{128,160},{160,128},{192,224},{224,1... | collective-permute-start | bytes 786440 | tf_op jit(solution)/shard_map/ppermute | solution.py:597
  8.9 0.0 copy-done.2
  8.9 0.0 copy-done.10
  8.9 1.5 %coefs.1.refs_4_.refs_1_ = f32[64,128]{1,0:T(8,128)S(1)} custom-call(f32[2,128,128]{2,1,0:T(8,128)S(1)} %copy-done.2, f32[1,256]{1,0:T(1,128)S(1)} %bitcast.6), custom_call_target="tpu_custom_call" | custom-call | flops 100000000 | bytes 1000000 | tf_op jit(solution)/shard_map/coefs/pallas_call | solution.py:599
  10.4 3.4 %collective-permute-done.refs_1_ = f32[32,2048]{1,0:T(8,128)S(1)} collective-permute-done((f32[32,2048]{1,0:T(8,128)S(1)}, f32[32,2048]{1,0:T(8,128)S(1)}, u32[]{:S(2)}, u32[]{:S(2)}) %collective-permute-start) | collective-permute-done | bytes 262176 | tf_op jit(solution)/shard_map/ppermute | solution.py:597
  13.8 0.0 copy-done.5
  13.8 0.0 copy-done.13
  13.8 0.5 pair.1
  14.4 2.3 %collective-permute-start.1 = (f32[16,2048]{1,0:T(8,128)S(1)}, f32[16,2048]{1,0:T(8,128)S(1)}, u32[]{:S(2)}, u32[]{:S(2)}) collective-permute-start(f32[16,2048]{1,0:T(8,128)S(1)} %get-tuple-element.31), channel_id=1, source_target_pairs={{0,64},{32,96},{64,128},{96,160},{128,192},{160,224},{192,0},{224,... | collective-permute-start | bytes 393224 | tf_op jit(solution)/shard_map/ppermute | solution.py:653
  16.7 2.6 %collective-permute-start.2 = (f32[16,2048]{1,0:T(8,128)S(1)}, f32[16,2048]{1,0:T(8,128)S(1)}, u32[]{:S(2)}, u32[]{:S(2)}) collective-permute-start(f32[16,2048]{1,0:T(8,128)S(1)} %get-tuple-element.32), channel_id=1, source_target_pairs={{0,128},{32,160},{64,192},{96,224},{128,0},{160,32},{192,64},{224,... | collective-permute-start | bytes 393224 | tf_op jit(solution)/shard_map/ppermute | solution.py:653
  19.3 1.1 %collective-permute-start.3 = (f32[16,2048]{1,0:T(8,128)S(1)}, f32[16,2048]{1,0:T(8,128)S(1)}, u32[]{:S(2)}, u32[]{:S(2)}) collective-permute-start(f32[16,2048]{1,0:T(8,128)S(1)} %get-tuple-element.33), channel_id=1, source_target_pairs={{0,192},{32,224},{64,0},{96,32},{128,64},{160,96},{192,128},{224,1... | collective-permute-start | bytes 393224 | tf_op jit(solution)/shard_map/ppermute | solution.py:653
  20.4 5.8 %local.1 = (f32[256,2048]{1,0:T(8,128)}, f32[64,2048]{1,0:T(8,128)S(1)}) custom-call(f32[256,2048]{1,0:T(8,128)} %bitcast.16, f32[8,32,2048]{2,1,0:T(8,128)} %u_ref.1, f32[2,128,128]{2,1,0:T(8,128)} %gy_ref.5, f32[1,256]{1,0:T(1,128)} %bitcast.12, f32[2,128,128]{2,1,0:T(8,128)} %gz_ref.9, f32[1,256]{1,0:T(1,128)} %bitcast.4), custom_call_target="tpu_custom_call", output_to_operand_aliasing={{0}: (0, {})} | custom-call | flops 2013265920 | bytes 7340032 | tf_op jit(solution)/shard_map/local/pallas_call | solution.py:619
  26.3 0.0 collective-permute-done.1.r1_ref
  26.3 0.0 collective-permute-done.2.r2_ref
  26.3 0.0 collective-permute-done.3.r3_ref
  26.3 0.0 copy-done.3
  26.3 0.0 copy-done.6
  26.3 0.0 copy-done.11
  26.3 0.0 copy-done.14
  26.3 0.8 %section.1 = (f32[32,2048]{1,0:T(8,128)S(1)}, f32[32,2048]{1,0:T(8,128)S(1)}, f32[32,2048]{1,0:T(8,128)S(1)}) custom-call(f32[32,2048]{1,0:T(8,128)S(1)} %get-tuple-element.30.near_ref, f32[16,2048]{1,0:T(8,128)S(1)} %collective-permute-done.1.r1_ref, f32[16,2048]{1,0:T(8,128)S(1)} %collective-permute-done.2.r2_ref, ...), custom_call_target="tpu_custom_call" | custom-call | flops 10000000 | bytes 1000000 | tf_op jit(solution)/shard_map/section/pallas_call | solution.py:657
  27.1 0.0 copy-start.9
  27.1 2.5 %collective-permute-start.4 = (f32[32,2048]{1,0:T(8,128)S(1)}, f32[32,2048]{1,0:T(8,128)S(1)}, u32[]{:S(2)}, u32[]{:S(2)}) collective-permute-start(f32[32,2048]{1,0:T(8,128)S(1)} %get-tuple-element.42), channel_id=1, source_target_pairs={{0,1},{1,0},{2,3},{3,2},{4,5},{5,4},{6,7},{7,6},{8,9},{9,8},{10,11... | collective-permute-start | bytes 786440 | tf_op jit(solution)/shard_map/ppermute | solution.py:666
  29.6 1.2 %collective-permute-done.4.recv_ref = f32[32,2048]{1,0:T(8,128)S(1)} collective-permute-done((f32[32,2048]{1,0:T(8,128)S(1)}, f32[32,2048]{1,0:T(8,128)S(1)}, u32[]{:S(2)}, u32[]{:S(2)}) %collective-permute-start.4) | collective-permute-done | bytes 262176 | tf_op jit(solution)/shard_map/ppermute | solution.py:666
  30.8 1.2 %pack.1 = (f32[16,32,128]{2,1,0:T(8,128)}, f32[32,2048]{1,0:T(8,128)S(1)}) custom-call(f32[32,2048]{1,0:T(8,128)S(1)} %get-tuple-element.41.keep_ref, f32[32,2048]{1,0:T(8,128)S(1)} %collective-permute-done.4.recv_ref, f32[2,128,128]{2,1,0:T(8,128)S(1)} %copy-done.3, f32[1,256]{1,0:T(1,128)S(1)} %bitcast.8), custom_call_target="tpu_custom_call" | custom-call | flops 1000000 | bytes 1000000 | tf_op jit(solution)/shard_map/pack/pallas_call | solution.py:667
  32.0 9.2 %all-to-all-start = ((f32[16,32,128]{2,1,0:T(8,128)}), f32[16,32,128]{2,1,0:T(8,128)S(1)}, u32[]{:S(2)}, u32[]{:S(2)}) async-start(f32[16,32,128]{2,1,0:T(8,128)} %get-tuple-element.43), calls=%async_computation | async-start | bytes 524288 | tf_op jit(solution)/shard_map/all_to_all | solution.py:674
  41.2 5.5 %reduced.1 = (bf16[16,128,256]{2,1,0:T(8,128)(2,1)}, bf16[16,128,256]{2,1,0:T(8,128)(2,1)}, bf16[32,2048]{1,0:T(8,128)(2,1)}, bf16[32,2048]{1,0:T(8,128)(2,1)}, f32[8,128]{1,0:T(8,128)S(1)}) custom-call(f32[16,128,128]{2,1,0:T(8,128)} %g_ref.3, f32[1,2048]{1,0:T(1,128)} %bitcast.18), custom_call_target="tpu_custom_call" | custom-call | flops 1000000000 | bytes 2000000 | tf_op jit(solution)/shard_map/reduced/pallas_call | solution.py:603
  46.7 0.0 copy-done.9
  46.7 5.5 %all-to-all-done.refs_0_ = f32[16,32,128]{2,1,0:T(8,128)S(1)} async-done(((f32[16,32,128]{2,1,0:T(8,128)}), f32[16,32,128]{2,1,0:T(8,128)S(1)}, u32[]{:S(2)}, u32[]{:S(2)}) %all-to-all-start) | async-done | bytes 262176 | tf_op jit(solution)/shard_map/all_to_all | solution.py:674
  52.2 0.8 %scan_z.1 = f32[16,32,128]{2,1,0:T(8,128)} custom-call(f32[16,32,128]{2,1,0:T(8,128)S(1)} %all-to-all-done.refs_0_, f32[64,128]{1,0:T(8,128)S(1)} %coefs.1.refs_4_.refs_1_, f32[8,128]{1,0:T(8,128)S(1)} %get-tuple-element.44.refs_2_), custom_call_target="tpu_custom_call" | custom-call | flops 1000000 | bytes 1000000 | tf_op jit(solution)/shard_map/scan_z/pallas_call | solution.py:91
  53.0 3.5 %all-to-all-start.1 = ((f32[16,32,128]{2,1,0:T(8,128)}), f32[16,32,128]{2,1,0:T(8,128)S(1)}, u32[]{:S(2)}, u32[]{:S(2)}) async-start(f32[16,32,128]{2,1,0:T(8,128)} %scan_z.1), calls=%async_computation.1 | async-start | bytes 524288 | tf_op jit(solution)/shard_map/all_to_all | solution.py:679
  56.5 0.0 copy-start.4
  56.6 0.0 copy-start.12
  56.6 0.0 copy-start
  56.6 0.0 copy-start.1
  56.6 0.0 copy-start.7
  56.6 0.0 copy-start.8
  56.6 9.2 %inner.1 = (f32[8,32,2048]{2,1,0:T(8,128)}, f32[8,128]{1,0:T(8,128)S(1)}) custom-call(f32[256,2048]{1,0:T(8,128)} %get-tuple-element.28.l_ref, f32[32,2048]{1,0:T(8,128)} %copy-done.9, f32[8,32,2048]{2,1,0:T(8,128)} %u_ref.1, f32[2,128,128]{2,1,0:T(8,128)} %gy_ref.5, f32[1,256]{1,0:T(1,128)} %bitcast.13, f32[2,128,128]{2,1,0:T(8,128)} %gz_ref.9, ...), custom_call_target="tpu_custom_call" | custom-call | flops 1258291200 | bytes 8388608 | tf_op jit(solution)/shard_map/inner/pallas_call | solution.py:680
  65.8 0.4 all-to-all-done.1.refs_0_
  66.2 0.0 copy-done.4
  66.2 0.0 copy-done.12
  66.2 0.4 unpack.1
  66.6 3.5 %collective-permute-start.5 = (f32[32,2048]{1,0:T(8,128)S(1)}, f32[32,2048]{1,0:T(8,128)S(1)}, u32[]{:S(2)}, u32[]{:S(2)}) collective-permute-start(f32[32,2048]{1,0:T(8,128)S(1)} %get-tuple-element.48), channel_id=1, source_target_pairs={{0,1},{1,0},{2,3},{3,2},{4,5},{5,4},{6,7},{7,6},{8,9},{9,8},{10,11... | collective-permute-start | bytes 786440 | tf_op jit(solution)/shard_map/ppermute | solution.py:701
  70.1 1.2 %collective-permute-done.5.got_ref = f32[32,2048]{1,0:T(8,128)S(1)} collective-permute-done((f32[32,2048]{1,0:T(8,128)S(1)}, f32[32,2048]{1,0:T(8,128)S(1)}, u32[]{:S(2)}, u32[]{:S(2)}) %collective-permute-start.5) | collective-permute-done | bytes 262176 | tf_op jit(solution)/shard_map/ppermute | solution.py:701
  71.3 0.0 copy-done
  71.3 0.0 copy-done.1
  71.3 3.6 %final.1 = f32[8,32,2048]{2,1,0:T(8,128)} custom-call(f32[8,32,2048]{2,1,0:T(8,128)} %get-tuple-element.40.s_hbm, f32[32,2048]{1,0:T(8,128)S(1)} %get-tuple-element.47.own_ref, f32[32,2048]{1,0:T(8,128)S(1)} %collective-permute-done.5.got_ref, f32[2,128,128]{2,1,0:T(8,128)S(1)} %copy-done.4, f32[1,256]{1,0:T(1,128)S(1)} %bitcast.10, ...), custom_call_target="tpu_custom_call", output_to_operand_aliasing={{}: (0, {})} | custom-call | flops 6291456 | bytes 4194304 | tf_op jit(solution)/shard_map/final/pallas_call | solution.py:702
  (9 shorter events, 0.0 us)
Async XLA Ops:
  0.0 8.9 %copy-start.2 = (f32[2,128,128]{2,1,0:T(8,128)S(1)}, f32[2,128,128]{2,1,0:T(8,128)}, u32[]{:S(2)}) copy-start(f32[2,128,128]{2,1,0:T(8,128)} %gz_ref.9) | copy-start | bytes 393220
  0.0 8.9 %copy-start.10 = (f32[256]{0:T(256)S(1)}, f32[256]{0:T(256)}, u32[]{:S(2)}) copy-start(f32[256]{0:T(256)} %param.12) | copy-start | bytes 3076
  0.0 13.8 %copy-start.5 = (f32[2,128,128]{2,1,0:T(8,128)S(1)}, f32[2,128,128]{2,1,0:T(8,128)}, u32[]{:S(2)}) copy-start(f32[2,128,128]{2,1,0:T(8,128)} %gy_ref.5) | copy-start | bytes 393220
  0.0 13.8 %copy-start.13 = (f32[256]{0:T(256)S(1)}, f32[256]{0:T(256)}, u32[]{:S(2)}) copy-start(f32[256]{0:T(256)} %param.11) | copy-start | bytes 3076
  5.2 8.6 %collective-permute-start = (f32[32,2048]{1,0:T(8,128)S(1)}, f32[32,2048]{1,0:T(8,128)S(1)}, u32[]{:S(2)}, u32[]{:S(2)}) collective-permute-start(f32[32,2048]{1,0:T(8,128)S(1)} %get-tuple-element.29.refs_0_), channel_id=1, source_target_pairs={{0,32},{32,0},{64,96},{96,64},{128,160},{160,128},{192,224},{224,1... | collective-permute-start | bytes 786440 | tf_op jit(solution)/shard_map/ppermute | solution.py:597
  14.4 11.9 %collective-permute-start.1 = (f32[16,2048]{1,0:T(8,128)S(1)}, f32[16,2048]{1,0:T(8,128)S(1)}, u32[]{:S(2)}, u32[]{:S(2)}) collective-permute-start(f32[16,2048]{1,0:T(8,128)S(1)} %get-tuple-element.31), channel_id=1, source_target_pairs={{0,64},{32,96},{64,128},{96,160},{128,192},{160,224},{192,0},{224,... | collective-permute-start | bytes 393224 | tf_op jit(solution)/shard_map/ppermute | solution.py:653
  16.7 9.6 %collective-permute-start.2 = (f32[16,2048]{1,0:T(8,128)S(1)}, f32[16,2048]{1,0:T(8,128)S(1)}, u32[]{:S(2)}, u32[]{:S(2)}) collective-permute-start(f32[16,2048]{1,0:T(8,128)S(1)} %get-tuple-element.32), channel_id=1, source_target_pairs={{0,128},{32,160},{64,192},{96,224},{128,0},{160,32},{192,64},{224,... | collective-permute-start | bytes 393224 | tf_op jit(solution)/shard_map/ppermute | solution.py:653
  19.3 7.0 %collective-permute-start.3 = (f32[16,2048]{1,0:T(8,128)S(1)}, f32[16,2048]{1,0:T(8,128)S(1)}, u32[]{:S(2)}, u32[]{:S(2)}) collective-permute-start(f32[16,2048]{1,0:T(8,128)S(1)} %get-tuple-element.33), channel_id=1, source_target_pairs={{0,192},{32,224},{64,0},{96,32},{128,64},{160,96},{192,128},{224,1... | collective-permute-start | bytes 393224 | tf_op jit(solution)/shard_map/ppermute | solution.py:653
  20.4 5.9 %copy-start.3 = (f32[2,128,128]{2,1,0:T(8,128)S(1)}, f32[2,128,128]{2,1,0:T(8,128)}, u32[]{:S(2)}) copy-start(f32[2,128,128]{2,1,0:T(8,128)} %gz_ref.9) | copy-start | bytes 393220
  20.4 5.9 %copy-start.6 = (f32[2,128,128]{2,1,0:T(8,128)S(1)}, f32[2,128,128]{2,1,0:T(8,128)}, u32[]{:S(2)}) copy-start(f32[2,128,128]{2,1,0:T(8,128)} %gy_ref.5) | copy-start | bytes 393220
  20.4 5.9 %copy-start.11 = (f32[256]{0:T(256)S(1)}, f32[256]{0:T(256)}, u32[]{:S(2)}) copy-start(f32[256]{0:T(256)} %param.12) | copy-start | bytes 3076
  20.4 5.9 %copy-start.14 = (f32[256]{0:T(256)S(1)}, f32[256]{0:T(256)}, u32[]{:S(2)}) copy-start(f32[256]{0:T(256)} %param.11) | copy-start | bytes 3076
  27.1 19.6 %copy-start.9 = (f32[32,2048]{1,0:T(8,128)}, f32[32,2048]{1,0:T(8,128)S(1)}, u32[]{:S(2)}) copy-start(f32[32,2048]{1,0:T(8,128)S(1)} %get-tuple-element.35.y_ref) | copy-start | bytes 786436
  27.1 3.7 %collective-permute-start.4 = (f32[32,2048]{1,0:T(8,128)S(1)}, f32[32,2048]{1,0:T(8,128)S(1)}, u32[]{:S(2)}, u32[]{:S(2)}) collective-permute-start(f32[32,2048]{1,0:T(8,128)S(1)} %get-tuple-element.42), channel_id=1, source_target_pairs={{0,1},{1,0},{2,3},{3,2},{4,5},{5,4},{6,7},{7,6},{8,9},{9,8},{10,11... | collective-permute-start | bytes 786440 | tf_op jit(solution)/shard_map/ppermute | solution.py:666
  32.0 20.2 %all-to-all-start = ((f32[16,32,128]{2,1,0:T(8,128)}), f32[16,32,128]{2,1,0:T(8,128)S(1)}, u32[]{:S(2)}, u32[]{:S(2)}) async-start(f32[16,32,128]{2,1,0:T(8,128)} %get-tuple-element.43), calls=%async_computation | async-start | bytes 524288 | tf_op jit(solution)/shard_map/all_to_all | solution.py:674
  53.0 13.2 %all-to-all-start.1 = ((f32[16,32,128]{2,1,0:T(8,128)}), f32[16,32,128]{2,1,0:T(8,128)S(1)}, u32[]{:S(2)}, u32[]{:S(2)}) async-start(f32[16,32,128]{2,1,0:T(8,128)} %scan_z.1), calls=%async_computation.1 | async-start | bytes 524288 | tf_op jit(solution)/shard_map/all_to_all | solution.py:679
  56.5 9.6 %copy-start.4 = (f32[2,128,128]{2,1,0:T(8,128)S(1)}, f32[2,128,128]{2,1,0:T(8,128)}, u32[]{:S(2)}) copy-start(f32[2,128,128]{2,1,0:T(8,128)} %gz_ref.9) | copy-start | bytes 393220
  56.6 9.6 %copy-start.12 = (f32[256]{0:T(256)S(1)}, f32[256]{0:T(256)}, u32[]{:S(2)}) copy-start(f32[256]{0:T(256)} %param.12) | copy-start | bytes 3076
  56.6 14.7 %copy-start = (bf16[16,128,256]{2,1,0:T(8,128)(2,1)S(1)}, bf16[16,128,256]{2,1,0:T(8,128)(2,1)}, u32[]{:S(2)}) copy-start(bf16[16,128,256]{2,1,0:T(8,128)(2,1)} %get-tuple-element.36.wh_ref) | copy-start | bytes 3145732
  56.6 14.7 %copy-start.1 = (bf16[16,128,256]{2,1,0:T(8,128)(2,1)S(1)}, bf16[16,128,256]{2,1,0:T(8,128)(2,1)}, u32[]{:S(2)}) copy-start(bf16[16,128,256]{2,1,0:T(8,128)(2,1)} %get-tuple-element.37.wl_ref) | copy-start | bytes 3145732
  56.6 14.7 %copy-start.7 = (bf16[32,2048]{1,0:T(8,128)(2,1)S(1)}, bf16[32,2048]{1,0:T(8,128)(2,1)}, u32[]{:S(2)}) copy-start(bf16[32,2048]{1,0:T(8,128)(2,1)} %get-tuple-element.38.bh_ref) | copy-start | bytes 393220
  56.6 14.7 %copy-start.8 = (bf16[32,2048]{1,0:T(8,128)(2,1)S(1)}, bf16[32,2048]{1,0:T(8,128)(2,1)}, u32[]{:S(2)}) copy-start(bf16[32,2048]{1,0:T(8,128)(2,1)} %get-tuple-element.39.bl_ref) | copy-start | bytes 393220
  66.6 4.7 %collective-permute-start.5 = (f32[32,2048]{1,0:T(8,128)S(1)}, f32[32,2048]{1,0:T(8,128)S(1)}, u32[]{:S(2)}, u32[]{:S(2)}) collective-permute-start(f32[32,2048]{1,0:T(8,128)S(1)} %get-tuple-element.48), channel_id=1, source_target_pairs={{0,1},{1,0},{2,3},{3,2},{4,5},{5,4},{6,7},{7,6},{8,9},{9,8},{10,11... | collective-permute-start | bytes 786440 | tf_op jit(solution)/shard_map/ppermute | solution.py:701

commit v4 on v3

--- a/solution.py
+++ b/solution.py
@@ -207,7 +207,8 @@
 
 
 def pair_kernel(cells, rings, mine_ref, got_ref, gy_ref, yf_ref, *out_refs):
-    *send_refs, near_ref = out_refs
+    *send_refs, near_ref, mark_ref = out_refs
+    mark_ref[...] = jnp.zeros_like(mark_ref)
     r = lax.axis_index("row")
     pair = r // 2
     lower = r % 2 == 0
@@ -393,7 +394,7 @@
 
 def section_kernel(
     near_ref, r1_ref, r2_ref, r3_ref, zp_ref, gy_ref, yf_ref, gz_ref, zf_ref,
-    keep_ref, send_ref, rows_ref, all_ref
+    keep_ref, send_ref, rows_hbm, all_ref, rows_ref, sem
 ):
     rows, width = near_ref.shape
     cells = zp_ref.shape[0] // 2
@@ -428,9 +429,14 @@
         hi = near_ref[half:, at] + sum(c * g for c, g in zip(above, got))
         rows_ref[:half, at] = lo
         rows_ref[half:, at] = hi
+    copy = pltpu.make_async_copy(rows_ref, rows_hbm, sem)
+    copy.start()
+    for s in range(width // span):
+        at = slice(s * span, (s + 1) * span)
+        lo, hi = rows_ref[:planes, at], rows_ref[half : half + planes, at]
         for k, w in enumerate((last, first)):
-            low = jnp.sum(w * lo[:planes], axis=0, keepdims=True)
-            high = jnp.sum(w * hi[:planes], axis=0, keepdims=True)
+            low = jnp.sum(w * lo, axis=0, keepdims=True)
+            high = jnp.sum(w * hi, axis=0, keepdims=True)
             own = slice(k * cells, (k + 1) * cells)
             all_ref[own, at] = zp_ref[own, at] + from_first * low + from_last * high
     half = cells // 2
@@ -440,6 +446,7 @@
         sent = pl.multiple_of(k * cells + (1 - mine) * half, half)
         keep_ref[at, :] = all_ref[pl.ds(kept, half), :]
         send_ref[at, :] = all_ref[pl.ds(sent, half), :]
+    copy.wait()
 
 
 def chip_pair(keep_ref, recv_ref, rows, lanes):
@@ -506,11 +513,15 @@
     for z in range(planes):
         row = jnp.where(lane < planes, dz[z : z + 1, :], jnp.where(lane == planes + z, -2.0, 0.0))
         parts.append(from_first * row + from_last * pltpu.roll(row, 2 * planes, 1))
-    mix = jnp.concatenate(parts, axis=0)[:, :rows]
+    high, low = halves(jnp.concatenate(parts, axis=0)[:, :rows])
+    both = jnp.concatenate([high, low], axis=0)
     span = 256
     for s in range(width // span):
         at = slice(s * span, (s + 1) * span)
-        rows_ref[:, at] = l_ref[:, at] + dot(mix, y_ref[:, at])
+        y_high, y_low = halves(y_ref[:, at])
+        wide = jnp.dot(both, y_high, preferred_element_type=F32)
+        wide = wide[:local] + wide[local:] + jnp.dot(high, y_low, preferred_element_type=F32)
+        rows_ref[:, at] = l_ref[:, at] + wide
 
     def store(at, value):
         for z in range(planes):
@@ -596,9 +607,6 @@
     )(scalar_field, reaction, xf, y_inverse, yf)
     got_ends = lax.ppermute(ends, "row", [(i, i ^ 1) for i in range(rows)])
 
-    z_coef = call(
-        functools.partial(coef_kernel, chips), held(4 * chips, LANES), 10**8, 10**6, "coefs"
-    )(z_inverse, zf)
     half = lambda *s: jax.ShapeDtypeStruct(s, BF16)
     *weights, x_made = call(
         reduced_kernel,
@@ -637,10 +645,11 @@
         room=61.5,
     )(a.reshape(local, width), scalar_field, y_inverse, yf, z_inverse, zf)
 
-    *sums, near_y = call_after(
-        (z_coef,),
+    *sums, near_y, joined = call_after(
+        (z_part,),
         functools.partial(pair_kernel, cells, rows // 2),
-        tuple(sds(2 * planes, width) for _ in range(3)) + (sds(4 * planes, width),),
+        tuple(sds(2 * planes, width) for _ in range(3))
+        + (sds(4 * planes, width), held(8, LANES)),
         10**6,
         10**6,
         "pair",
@@ -654,14 +663,37 @@
         for k, total in enumerate(sums)
     ]
 
-    keep, send, y_rows = call(
+    z_coef = call_after(
+        (joined,),
+        functools.partial(coef_kernel, chips),
+        held(4 * chips, LANES),
+        10**8,
+        10**6,
+        "coefs",
+        z_inverse,
+        zf,
+    )
+    keep, send, y_rows = call_after(
+        (z_coef,),
         section_kernel,
-        (sds(cells, width), sds(cells, width), sds(4 * planes, width)),
+        (sds(cells, width), sds(cells, width), pltpu.HBM((4 * planes, width), F32)),
         10**7,
         10**6,
         "section",
-        scratch_shapes=[pltpu.VMEM((2 * cells, width), F32)],
-    )(near_y, *got_sums, z_part, y_inverse, yf, z_inverse, zf)
+        near_y,
+        *got_sums,
+        z_part,
+        y_inverse,
+        yf,
+        z_inverse,
+        zf,
+        out_specs=(near_by, near_by, far),
+        scratch_shapes=[
+            pltpu.VMEM((2 * cells, width), F32),
+            pltpu.VMEM((4 * planes, width), F32),
+            pltpu.SemaphoreType.DMA,
+        ],
+    )
     pairs = [(0, 1), (1, 0)]
     recv = lax.ppermute(send, "core", pairs)
     z_buf, near = call(

time: 75.3 us -> 73.8 us (0.980)
  starting transfers between devices: 28.4 us -> 27.4 us
    ppermute x1, waiting for transfers between devices: 3.42 us -> 0.01 us  [body(): got_ends = lax.ppermute(ends, 'row', [(i, i ^ 1) for i in range(rows)])]
    pallas_call x3 -> x5, Pallas kernels: 1.74 us -> 4.79 us  [call_after(): call(ordered, out_shape, flops, nbytes, name, in_specs=specs, **kw)]
    ppermute x3, waiting for transfers between devices: 0.01 us -> 2.36 us  [body(): lax.ppermute(total, 'row', [(i, (i + 2 * k + 2) % rows) for i in range(ro...]
    pallas_call x2 -> x0, Pallas kernels: 2.33 us -> none  [the longest x1 1.55 us: body(): call(functools.partial(coef_kernel, chips), held(4 * chips, LANES), 10 **...]
    ppermute x3, starting transfers between devices: 6.02 us -> 5.09 us  [body(): lax.ppermute(total, 'row', [(i, (i + 2 * k + 2) % rows) for i in range(ro...]
    pallas_call x1, Pallas kernels: 9.16 us -> 8.34 us  [body(): call(inner_kernel, (sds(planes, cells, width), held(8, LANES)), 12 * loca...]
    all_to_all x1, waiting for transfers between devices: 0.42 us -> 1.24 us  [body(): z_back = lax.all_to_all(z_out, 'chip', 0, 0, tiled=True)]
  transfers between devices with their start and end apart: 8 -> 8, of which waited for: 5 -> 6; matrix products, arithmetic and copies ran while one was open for 0% -> 0% of each run, Pallas kernels for 29% -> 29%
where the time goes in v4:
time: 73.8 us; the launch traced here: 73.5 us
  Pallas kernels  34.4 us (47%)
  starting transfers between devices  27.4 us (37%)
  waiting for transfers between devices  11.5 us (16%)
    all_to_all x1, starting transfers between devices, body(): z_in = lax.all_to_all(z_buf, 'chip', 0, 0, tiled=True)  9.22 us
    pallas_call x1, Pallas kernels, body(): call(inner_kernel, (sds(planes, cells, width), held(8, LANES)), 12 * loca...  8.34 us
    pallas_call x1, Pallas kernels, body(): call(local_kernel, (sds(local, width), held(2 * cells, width)), 6 * 320 *...  5.85 us
    all_to_all x1, waiting for transfers between devices, body(): z_in = lax.all_to_all(z_buf, 'chip', 0, 0, tiled=True)  5.53 us
    pallas_call x1, Pallas kernels, body(): call(reduced_kernel, (half(16, 128, 256), half(16, 128, 256), half(32, wi...  5.46 us
    pallas_call x1, Pallas kernels, body(): call(explicit_kernel, (sds(planes, cells, width), held(4 * planes, width)...  5.11 us
    ppermute x3, starting transfers between devices, body(): lax.ppermute(total, 'row', [(i, (i + 2 * k + 2) % rows) for i in range(ro...  5.09 us
    pallas_call x5, Pallas kernels, call_after(): call(ordered, out_shape, flops, nbytes, name, in_specs=specs, **kw)  4.79 us
  transfers between devices with their start and end apart: 8, of which 6 were waited for; matrix products, arithmetic and copies ran while one was open for 0% of the time, Pallas kernels for 29%

profile of v4, /device:TPU:1, one launch (start us, length us, event | category | flops | bytes accessed | tf_op | source)
XLA Modules:
  0.0 73.5 jit_solution(11380970988554581074)
XLA Ops:
  0.0 5.1 %explicit.1 = (f32[8,32,2048]{2,1,0:T(8,128)}, f32[32,2048]{1,0:T(8,128)S(1)}) custom-call(f32[8,32,2048]{2,1,0:T(8,128)} %u_ref.1, f32[8,32,2048]{2,1,0:T(8,128)} %r_hbm.1, f32[1,2048]{1,0:T(1,128)} %bitcast.17, f32[2,128,128]{2,1,0:T(8,128)} %gy_ref.3, f32[1,256]{1,0:T(1,128)} %bitcast.11), custom_call_target="tpu_custom_call" | custom-call | flops 10485760 | bytes 6291456 | tf_op jit(solution)/shard_map/explicit/pallas_call | solution.py:584
  5.1 3.7 %collective-permute-start = (f32[32,2048]{1,0:T(8,128)S(1)}, f32[32,2048]{1,0:T(8,128)S(1)}, u32[]{:S(2)}, u32[]{:S(2)}) collective-permute-start(f32[32,2048]{1,0:T(8,128)S(1)} %get-tuple-element.30.refs_0_), channel_id=1, source_target_pairs={{0,32},{32,0},{64,96},{96,64},{128,160},{160,128},{192,224},{224,1... | collective-permute-start | bytes 786440 | tf_op jit(solution)/shard_map/ppermute | solution.py:608
  8.8 0.0 copy-start.4
  8.8 0.0 copy-start.9
  8.8 0.0 copy-start.2
  8.8 0.0 copy-start.7
  8.8 5.9 %local.1 = (f32[256,2048]{1,0:T(8,128)}, f32[64,2048]{1,0:T(8,128)S(1)}) custom-call(f32[256,2048]{1,0:T(8,128)} %bitcast.16, f32[8,32,2048]{2,1,0:T(8,128)} %u_ref.1, f32[2,128,128]{2,1,0:T(8,128)} %gy_ref.3, f32[1,256]{1,0:T(1,128)} %bitcast.12, f32[2,128,128]{2,1,0:T(8,128)} %gz_ref.7, f32[1,256]{1,0:T(1,128)} %bitcast.4), custom_call_target="tpu_custom_call", output_to_operand_aliasing={{0}: (0, {})} | custom-call | flops 2013265920 | bytes 7340032 | tf_op jit(solution)/shard_map/local/pallas_call | solution.py:627
  14.7 0.0 collective-permute-done.refs_1_
  14.7 0.0 copy-done.4
  14.7 0.0 copy-done.9
  14.7 0.5 pair.1
  15.2 1.4 %collective-permute-start.1 = (f32[16,2048]{1,0:T(8,128)S(1)}, f32[16,2048]{1,0:T(8,128)S(1)}, u32[]{:S(2)}, u32[]{:S(2)}) collective-permute-start(f32[16,2048]{1,0:T(8,128)S(1)} %get-tuple-element.33), channel_id=1, source_target_pairs={{0,64},{32,96},{64,128},{96,160},{128,192},{160,224},{192,0},{224,... | collective-permute-start | bytes 393224 | tf_op jit(solution)/shard_map/ppermute | solution.py:662
  16.6 2.6 %collective-permute-start.2 = (f32[16,2048]{1,0:T(8,128)S(1)}, f32[16,2048]{1,0:T(8,128)S(1)}, u32[]{:S(2)}, u32[]{:S(2)}) collective-permute-start(f32[16,2048]{1,0:T(8,128)S(1)} %get-tuple-element.34), channel_id=1, source_target_pairs={{0,128},{32,160},{64,192},{96,224},{128,0},{160,32},{192,64},{224,... | collective-permute-start | bytes 393224 | tf_op jit(solution)/shard_map/ppermute | solution.py:662
  19.3 1.1 %collective-permute-start.3 = (f32[16,2048]{1,0:T(8,128)S(1)}, f32[16,2048]{1,0:T(8,128)S(1)}, u32[]{:S(2)}, u32[]{:S(2)}) collective-permute-start(f32[16,2048]{1,0:T(8,128)S(1)} %get-tuple-element.35), channel_id=1, source_target_pairs={{0,192},{32,224},{64,0},{96,32},{128,64},{160,96},{192,128},{224,1... | collective-permute-start | bytes 393224 | tf_op jit(solution)/shard_map/ppermute | solution.py:662
  20.3 0.0 copy-done.2
  20.3 0.0 copy-done.7
  20.3 1.5 %coefs.1.refs_9_.refs_1_ = f32[64,128]{1,0:T(8,128)S(1)} custom-call(f32[2,128,128]{2,1,0:T(8,128)S(1)} %copy-done.2, f32[1,256]{1,0:T(1,128)S(1)} %bitcast.6, f32[8,128]{1,0:T(8,128)S(1)} %get-tuple-element.36.refs_2_), custom_call_target="tpu_custom_call" | custom-call | flops 100000000 | bytes 1000000 | tf_op jit(solution)/shard_map/coefs/pallas_call | solution.py:91
  21.9 0.0 collective-permute-done.1.refs_1_
  21.9 1.9 %collective-permute-done.2.refs_2_ = f32[16,2048]{1,0:T(8,128)S(1)} collective-permute-done((f32[16,2048]{1,0:T(8,128)S(1)}, f32[16,2048]{1,0:T(8,128)S(1)}, u32[]{:S(2)}, u32[]{:S(2)}) %collective-permute-start.2) | collective-permute-done | bytes 131104 | tf_op jit(solution)/shard_map/ppermute | solution.py:662
  23.8 0.5 collective-permute-done.3.refs_3_
  24.3 1.5 %section.1 = (f32[32,2048]{1,0:T(8,128)S(1)}, f32[32,2048]{1,0:T(8,128)S(1)}, f32[32,2048]{1,0:T(8,128)}) custom-call(f32[32,2048]{1,0:T(8,128)S(1)} %get-tuple-element.32.refs_0_, f32[16,2048]{1,0:T(8,128)S(1)} %collective-permute-done.1.refs_1_, f32[16,2048]{1,0:T(8,128)S(1)} %collective-permute-done.2.refs_2_, ...), custom_call_target="tpu_custom_call" | custom-call | flops 10000000 | bytes 1000000 | tf_op jit(solution)/shard_map/section/pallas_call | solution.py:91
  25.8 2.4 %collective-permute-start.4 = (f32[32,2048]{1,0:T(8,128)S(1)}, f32[32,2048]{1,0:T(8,128)S(1)}, u32[]{:S(2)}, u32[]{:S(2)}) collective-permute-start(f32[32,2048]{1,0:T(8,128)S(1)} %get-tuple-element.44), channel_id=1, source_target_pairs={{0,1},{1,0},{2,3},{3,2},{4,5},{5,4},{6,7},{7,6},{8,9},{9,8},{10,11... | collective-permute-start | bytes 786440 | tf_op jit(solution)/shard_map/ppermute | solution.py:698
  28.2 1.2 %collective-permute-done.4.recv_ref = f32[32,2048]{1,0:T(8,128)S(1)} collective-permute-done((f32[32,2048]{1,0:T(8,128)S(1)}, f32[32,2048]{1,0:T(8,128)S(1)}, u32[]{:S(2)}, u32[]{:S(2)}) %collective-permute-start.4) | collective-permute-done | bytes 262176 | tf_op jit(solution)/shard_map/ppermute | solution.py:698
  29.3 1.2 %pack.1 = (f32[16,32,128]{2,1,0:T(8,128)}, f32[32,2048]{1,0:T(8,128)S(1)}) custom-call(f32[32,2048]{1,0:T(8,128)S(1)} %get-tuple-element.43.keep_ref, f32[32,2048]{1,0:T(8,128)S(1)} %collective-permute-done.4.recv_ref, f32[2,128,128]{2,1,0:T(8,128)S(1)} %copy-done.2, f32[1,256]{1,0:T(1,128)S(1)} %bitcast.8), custom_call_target="tpu_custom_call" | custom-call | flops 1000000 | bytes 1000000 | tf_op jit(solution)/shard_map/pack/pallas_call | solution.py:699
  30.6 9.2 %all-to-all-start = ((f32[16,32,128]{2,1,0:T(8,128)}), f32[16,32,128]{2,1,0:T(8,128)S(1)}, u32[]{:S(2)}, u32[]{:S(2)}) async-start(f32[16,32,128]{2,1,0:T(8,128)} %get-tuple-element.45), calls=%async_computation | async-start | bytes 524288 | tf_op jit(solution)/shard_map/all_to_all | solution.py:706
  39.8 5.5 %reduced.1 = (bf16[16,128,256]{2,1,0:T(8,128)(2,1)}, bf16[16,128,256]{2,1,0:T(8,128)(2,1)}, bf16[32,2048]{1,0:T(8,128)(2,1)}, bf16[32,2048]{1,0:T(8,128)(2,1)}, f32[8,128]{1,0:T(8,128)S(1)}) custom-call(f32[16,128,128]{2,1,0:T(8,128)} %g_ref.1, f32[1,2048]{1,0:T(1,128)} %bitcast.18), custom_call_target="tpu_custom_call" | custom-call | flops 1000000000 | bytes 2000000 | tf_op jit(solution)/shard_map/reduced/pallas_call | solution.py:611
  45.2 5.5 %all-to-all-done.refs_0_ = f32[16,32,128]{2,1,0:T(8,128)S(1)} async-done(((f32[16,32,128]{2,1,0:T(8,128)}), f32[16,32,128]{2,1,0:T(8,128)S(1)}, u32[]{:S(2)}, u32[]{:S(2)}) %all-to-all-start) | async-done | bytes 262176 | tf_op jit(solution)/shard_map/all_to_all | solution.py:706
  50.8 0.8 %scan_z.1 = f32[16,32,128]{2,1,0:T(8,128)} custom-call(f32[16,32,128]{2,1,0:T(8,128)S(1)} %all-to-all-done.refs_0_, f32[64,128]{1,0:T(8,128)S(1)} %coefs.1.refs_9_.refs_1_, f32[8,128]{1,0:T(8,128)S(1)} %get-tuple-element.46.refs_2_), custom_call_target="tpu_custom_call" | custom-call | flops 1000000 | bytes 1000000 | tf_op jit(solution)/shard_map/scan_z/pallas_call | solution.py:91
  51.5 3.5 %all-to-all-start.1 = ((f32[16,32,128]{2,1,0:T(8,128)}), f32[16,32,128]{2,1,0:T(8,128)S(1)}, u32[]{:S(2)}, u32[]{:S(2)}) async-start(f32[16,32,128]{2,1,0:T(8,128)} %scan_z.1), calls=%async_computation.1 | async-start | bytes 524288 | tf_op jit(solution)/shard_map/all_to_all | solution.py:711
  55.1 0.0 copy-start.3
  55.1 0.0 copy-start.8
  55.1 0.0 copy-start
  55.1 0.0 copy-start.1
  55.1 0.0 copy-start.5
  55.1 0.0 copy-start.6
  55.1 8.3 %inner.1 = (f32[8,32,2048]{2,1,0:T(8,128)}, f32[8,128]{1,0:T(8,128)S(1)}) custom-call(f32[256,2048]{1,0:T(8,128)} %get-tuple-element.29.l_ref, f32[32,2048]{1,0:T(8,128)} %get-tuple-element.37.y_ref, f32[8,32,2048]{2,1,0:T(8,128)} %u_ref.1, f32[2,128,128]{2,1,0:T(8,128)} %gy_ref.3, f32[1,256]{1,0:T(1,128)} %bitcast.13, f32[2,128,128]{2,1,0:T(8,128)} %gz_ref.7, ...), custom_call_target="tpu_custom_call" | custom-call | flops 1258291200 | bytes 8388608 | tf_op jit(solution)/shard_map/inner/pallas_call | solution.py:712
  63.5 1.2 %all-to-all-done.1.refs_0_ = f32[16,32,128]{2,1,0:T(8,128)S(1)} async-done(((f32[16,32,128]{2,1,0:T(8,128)}), f32[16,32,128]{2,1,0:T(8,128)S(1)}, u32[]{:S(2)}, u32[]{:S(2)}) %all-to-all-start.1) | async-done | bytes 262176 | tf_op jit(solution)/shard_map/all_to_all | solution.py:711
  64.7 0.0 copy-done.3
  64.7 0.0 copy-done.8
  64.7 0.4 unpack.1
  65.2 3.5 %collective-permute-start.5 = (f32[32,2048]{1,0:T(8,128)S(1)}, f32[32,2048]{1,0:T(8,128)S(1)}, u32[]{:S(2)}, u32[]{:S(2)}) collective-permute-start(f32[32,2048]{1,0:T(8,128)S(1)} %get-tuple-element.50), channel_id=1, source_target_pairs={{0,1},{1,0},{2,3},{3,2},{4,5},{5,4},{6,7},{7,6},{8,9},{9,8},{10,11... | collective-permute-start | bytes 786440 | tf_op jit(solution)/shard_map/ppermute | solution.py:733
  68.7 1.2 %collective-permute-done.5.got_ref = f32[32,2048]{1,0:T(8,128)S(1)} collective-permute-done((f32[32,2048]{1,0:T(8,128)S(1)}, f32[32,2048]{1,0:T(8,128)S(1)}, u32[]{:S(2)}, u32[]{:S(2)}) %collective-permute-start.5) | collective-permute-done | bytes 262176 | tf_op jit(solution)/shard_map/ppermute | solution.py:733
  69.8 0.0 copy-done
  69.8 0.0 copy-done.1
  69.8 0.0 copy-done.5
  69.8 0.0 copy-done.6
  69.8 3.6 %final.1 = f32[8,32,2048]{2,1,0:T(8,128)} custom-call(f32[8,32,2048]{2,1,0:T(8,128)} %get-tuple-element.42.s_hbm, f32[32,2048]{1,0:T(8,128)S(1)} %get-tuple-element.49.own_ref, f32[32,2048]{1,0:T(8,128)S(1)} %collective-permute-done.5.got_ref, f32[2,128,128]{2,1,0:T(8,128)S(1)} %copy-done.3, f32[1,256]{1,0:T(1,128)S(1)} %bitcast.10, ...), custom_call_target="tpu_custom_call", output_to_operand_aliasing={{}: (0, {})} | custom-call | flops 6291456 | bytes 4194304 | tf_op jit(solution)/shard_map/final/pallas_call | solution.py:734
Async XLA Ops:
  5.1 9.5 %collective-permute-start = (f32[32,2048]{1,0:T(8,128)S(1)}, f32[32,2048]{1,0:T(8,128)S(1)}, u32[]{:S(2)}, u32[]{:S(2)}) collective-permute-start(f32[32,2048]{1,0:T(8,128)S(1)} %get-tuple-element.30.refs_0_), channel_id=1, source_target_pairs={{0,32},{32,0},{64,96},{96,64},{128,160},{160,128},{192,224},{224,1... | collective-permute-start | bytes 786440 | tf_op jit(solution)/shard_map/ppermute | solution.py:608
  8.8 5.9 %copy-start.4 = (f32[2,128,128]{2,1,0:T(8,128)S(1)}, f32[2,128,128]{2,1,0:T(8,128)}, u32[]{:S(2)}) copy-start(f32[2,128,128]{2,1,0:T(8,128)} %gy_ref.3) | copy-start | bytes 393220
  8.8 5.9 %copy-start.9 = (f32[256]{0:T(256)S(1)}, f32[256]{0:T(256)}, u32[]{:S(2)}) copy-start(f32[256]{0:T(256)} %param.11) | copy-start | bytes 3076
  8.8 11.5 %copy-start.2 = (f32[2,128,128]{2,1,0:T(8,128)S(1)}, f32[2,128,128]{2,1,0:T(8,128)}, u32[]{:S(2)}) copy-start(f32[2,128,128]{2,1,0:T(8,128)} %gz_ref.7) | copy-start | bytes 393220
  8.8 11.5 %copy-start.7 = (f32[256]{0:T(256)S(1)}, f32[256]{0:T(256)}, u32[]{:S(2)}) copy-start(f32[256]{0:T(256)} %param.12) | copy-start | bytes 3076
  15.2 6.7 %collective-permute-start.1 = (f32[16,2048]{1,0:T(8,128)S(1)}, f32[16,2048]{1,0:T(8,128)S(1)}, u32[]{:S(2)}, u32[]{:S(2)}) collective-permute-start(f32[16,2048]{1,0:T(8,128)S(1)} %get-tuple-element.33), channel_id=1, source_target_pairs={{0,64},{32,96},{64,128},{96,160},{128,192},{160,224},{192,0},{224,... | collective-permute-start | bytes 393224 | tf_op jit(solution)/shard_map/ppermute | solution.py:662
  16.6 7.1 %collective-permute-start.2 = (f32[16,2048]{1,0:T(8,128)S(1)}, f32[16,2048]{1,0:T(8,128)S(1)}, u32[]{:S(2)}, u32[]{:S(2)}) collective-permute-start(f32[16,2048]{1,0:T(8,128)S(1)} %get-tuple-element.34), channel_id=1, source_target_pairs={{0,128},{32,160},{64,192},{96,224},{128,0},{160,32},{192,64},{224,... | collective-permute-start | bytes 393224 | tf_op jit(solution)/shard_map/ppermute | solution.py:662
  19.3 5.0 %collective-permute-start.3 = (f32[16,2048]{1,0:T(8,128)S(1)}, f32[16,2048]{1,0:T(8,128)S(1)}, u32[]{:S(2)}, u32[]{:S(2)}) collective-permute-start(f32[16,2048]{1,0:T(8,128)S(1)} %get-tuple-element.35), channel_id=1, source_target_pairs={{0,192},{32,224},{64,0},{96,32},{128,64},{160,96},{192,128},{224,1... | collective-permute-start | bytes 393224 | tf_op jit(solution)/shard_map/ppermute | solution.py:662
  25.8 3.6 %collective-permute-start.4 = (f32[32,2048]{1,0:T(8,128)S(1)}, f32[32,2048]{1,0:T(8,128)S(1)}, u32[]{:S(2)}, u32[]{:S(2)}) collective-permute-start(f32[32,2048]{1,0:T(8,128)S(1)} %get-tuple-element.44), channel_id=1, source_target_pairs={{0,1},{1,0},{2,3},{3,2},{4,5},{5,4},{6,7},{7,6},{8,9},{9,8},{10,11... | collective-permute-start | bytes 786440 | tf_op jit(solution)/shard_map/ppermute | solution.py:698
  30.6 20.2 %all-to-all-start = ((f32[16,32,128]{2,1,0:T(8,128)}), f32[16,32,128]{2,1,0:T(8,128)S(1)}, u32[]{:S(2)}, u32[]{:S(2)}) async-start(f32[16,32,128]{2,1,0:T(8,128)} %get-tuple-element.45), calls=%async_computation | async-start | bytes 524288 | tf_op jit(solution)/shard_map/all_to_all | solution.py:706
  51.5 13.2 %all-to-all-start.1 = ((f32[16,32,128]{2,1,0:T(8,128)}), f32[16,32,128]{2,1,0:T(8,128)S(1)}, u32[]{:S(2)}, u32[]{:S(2)}) async-start(f32[16,32,128]{2,1,0:T(8,128)} %scan_z.1), calls=%async_computation.1 | async-start | bytes 524288 | tf_op jit(solution)/shard_map/all_to_all | solution.py:711
  55.1 9.6 %copy-start.3 = (f32[2,128,128]{2,1,0:T(8,128)S(1)}, f32[2,128,128]{2,1,0:T(8,128)}, u32[]{:S(2)}) copy-start(f32[2,128,128]{2,1,0:T(8,128)} %gz_ref.7) | copy-start | bytes 393220
  55.1 9.6 %copy-start.8 = (f32[256]{0:T(256)S(1)}, f32[256]{0:T(256)}, u32[]{:S(2)}) copy-start(f32[256]{0:T(256)} %param.12) | copy-start | bytes 3076
  55.1 14.7 %copy-start = (bf16[16,128,256]{2,1,0:T(8,128)(2,1)S(1)}, bf16[16,128,256]{2,1,0:T(8,128)(2,1)}, u32[]{:S(2)}) copy-start(bf16[16,128,256]{2,1,0:T(8,128)(2,1)} %get-tuple-element.38.wh_ref) | copy-start | bytes 3145732
  55.1 14.7 %copy-start.1 = (bf16[16,128,256]{2,1,0:T(8,128)(2,1)S(1)}, bf16[16,128,256]{2,1,0:T(8,128)(2,1)}, u32[]{:S(2)}) copy-start(bf16[16,128,256]{2,1,0:T(8,128)(2,1)} %get-tuple-element.39.wl_ref) | copy-start | bytes 3145732
  55.1 14.7 %copy-start.5 = (bf16[32,2048]{1,0:T(8,128)(2,1)S(1)}, bf16[32,2048]{1,0:T(8,128)(2,1)}, u32[]{:S(2)}) copy-start(bf16[32,2048]{1,0:T(8,128)(2,1)} %get-tuple-element.40.bh_ref) | copy-start | bytes 393220
  55.1 14.7 %copy-start.6 = (bf16[32,2048]{1,0:T(8,128)(2,1)S(1)}, bf16[32,2048]{1,0:T(8,128)(2,1)}, u32[]{:S(2)}) copy-start(bf16[32,2048]{1,0:T(8,128)(2,1)} %get-tuple-element.41.bl_ref) | copy-start | bytes 393220
  65.2 4.7 %collective-permute-start.5 = (f32[32,2048]{1,0:T(8,128)S(1)}, f32[32,2048]{1,0:T(8,128)S(1)}, u32[]{:S(2)}, u32[]{:S(2)}) collective-permute-start(f32[32,2048]{1,0:T(8,128)S(1)} %get-tuple-element.50), channel_id=1, source_target_pairs={{0,1},{1,0},{2,3},{3,2},{4,5},{5,4},{6,7},{7,6},{8,9},{9,8},{10,11... | collective-permute-start | bytes 786440 | tf_op jit(solution)/shard_map/ppermute | solution.py:733

commit v5 on v4

--- a/solution.py
+++ b/solution.py
@@ -101,9 +101,6 @@
         pltpu.make_async_copy(yf_hbm, yf_ref, s_sem.at[1]),
         pltpu.make_async_copy(xf_hbm, xf_ref, s_sem.at[2]),
     ]
-    for copy in small:
-        copy.start()
-
     def fetch(z):
         return (
             pltpu.make_async_copy(u_hbm.at[z], u_ref.at[z], u_sem.at[z]),
@@ -113,7 +110,9 @@
     def give(z):
         return pltpu.make_async_copy(a_ref.at[z], a_hbm.at[z], a_sem.at[z])
 
-    for z in range(planes):
+    for copy in small[:2] + list(fetch(0)) + small[2:]:
+        copy.start()
+    for z in range(1, planes):
         for copy in fetch(z):
             copy.start()
     for copy in small:
@@ -698,7 +697,7 @@
     recv = lax.ppermute(send, "core", pairs)
     z_buf, near = call(
         functools.partial(pack_kernel, planes),
-        (sds(chips, cells, width // chips), sds(cells, width)),
+        (held(chips, cells, width // chips), sds(cells, width)),
         10**6,
         10**6,
         "pack",

time: 73.8 us -> 73.8 us (level)
  no operation moved by 1% of the time
where the time goes in v5:
time: 73.8 us; the launch traced here: 73.5 us
  Pallas kernels  34.4 us (47%)
  starting transfers between devices  27.4 us (37%)
  waiting for transfers between devices  11.5 us (16%)
    all_to_all x1, starting transfers between devices, body(): z_in = lax.all_to_all(z_buf, 'chip', 0, 0, tiled=True)  9.22 us
    pallas_call x1, Pallas kernels, body(): call(inner_kernel, (sds(planes, cells, width), held(8, LANES)), 12 * loca...  8.34 us
    pallas_call x1, Pallas kernels, body(): call(local_kernel, (sds(local, width), held(2 * cells, width)), 6 * 320 *...  5.85 us
    all_to_all x1, waiting for transfers between devices, body(): z_in = lax.all_to_all(z_buf, 'chip', 0, 0, tiled=True)  5.53 us
    pallas_call x1, Pallas kernels, body(): call(reduced_kernel, (half(16, 128, 256), half(16, 128, 256), half(32, wi...  5.46 us
    pallas_call x1, Pallas kernels, body(): call(explicit_kernel, (sds(planes, cells, width), held(4 * planes, width)...  5.11 us
    ppermute x3, starting transfers between devices, body(): lax.ppermute(total, 'row', [(i, (i + 2 * k + 2) % rows) for i in range(ro...  5.09 us
    pallas_call x5, Pallas kernels, call_after(): call(ordered, out_shape, flops, nbytes, name, in_specs=specs, **kw)  4.79 us
  transfers between devices with their start and end apart: 8, of which 6 were waited for; matrix products, arithmetic and copies ran while one was open for 0% of the time, Pallas kernels for 29%

profile of v5, /device:TPU:1, one launch (start us, length us, event | category | flops | bytes accessed | tf_op | source)
XLA Modules:
  0.0 73.5 jit_solution(11380970988554581074)
XLA Ops:
  0.0 5.1 %explicit.1 = (f32[8,32,2048]{2,1,0:T(8,128)}, f32[32,2048]{1,0:T(8,128)S(1)}) custom-call(f32[8,32,2048]{2,1,0:T(8,128)} %u_ref.1, f32[8,32,2048]{2,1,0:T(8,128)} %r_hbm.1, f32[1,2048]{1,0:T(1,128)} %bitcast.17, f32[2,128,128]{2,1,0:T(8,128)} %gy_ref.3, f32[1,256]{1,0:T(1,128)} %bitcast.11), custom_call_target="tpu_custom_call" | custom-call | flops 10485760 | bytes 6291456 | tf_op jit(solution)/shard_map/explicit/pallas_call | solution.py:583
  5.1 3.7 %collective-permute-start = (f32[32,2048]{1,0:T(8,128)S(1)}, f32[32,2048]{1,0:T(8,128)S(1)}, u32[]{:S(2)}, u32[]{:S(2)}) collective-permute-start(f32[32,2048]{1,0:T(8,128)S(1)} %get-tuple-element.30.refs_0_), channel_id=1, source_target_pairs={{0,32},{32,0},{64,96},{96,64},{128,160},{160,128},{192,224},{224,1... | collective-permute-start | bytes 786440 | tf_op jit(solution)/shard_map/ppermute | solution.py:607
  8.8 0.0 copy-start.4
  8.8 0.0 copy-start.9
  8.8 0.0 copy-start.2
  8.8 0.0 copy-start.7
  8.8 5.9 %local.1 = (f32[256,2048]{1,0:T(8,128)}, f32[64,2048]{1,0:T(8,128)S(1)}) custom-call(f32[256,2048]{1,0:T(8,128)} %bitcast.16, f32[8,32,2048]{2,1,0:T(8,128)} %u_ref.1, f32[2,128,128]{2,1,0:T(8,128)} %gy_ref.3, f32[1,256]{1,0:T(1,128)} %bitcast.12, f32[2,128,128]{2,1,0:T(8,128)} %gz_ref.7, f32[1,256]{1,0:T(1,128)} %bitcast.4), custom_call_target="tpu_custom_call", output_to_operand_aliasing={{0}: (0, {})} | custom-call | flops 2013265920 | bytes 7340032 | tf_op jit(solution)/shard_map/local/pallas_call | solution.py:626
  14.7 0.0 collective-permute-done.refs_1_
  14.7 0.0 copy-done.4
  14.7 0.0 copy-done.9
  14.7 0.5 pair.1
  15.2 1.4 %collective-permute-start.1 = (f32[16,2048]{1,0:T(8,128)S(1)}, f32[16,2048]{1,0:T(8,128)S(1)}, u32[]{:S(2)}, u32[]{:S(2)}) collective-permute-start(f32[16,2048]{1,0:T(8,128)S(1)} %get-tuple-element.33), channel_id=1, source_target_pairs={{0,64},{32,96},{64,128},{96,160},{128,192},{160,224},{192,0},{224,... | collective-permute-start | bytes 393224 | tf_op jit(solution)/shard_map/ppermute | solution.py:661
  16.6 2.6 %collective-permute-start.2 = (f32[16,2048]{1,0:T(8,128)S(1)}, f32[16,2048]{1,0:T(8,128)S(1)}, u32[]{:S(2)}, u32[]{:S(2)}) collective-permute-start(f32[16,2048]{1,0:T(8,128)S(1)} %get-tuple-element.34), channel_id=1, source_target_pairs={{0,128},{32,160},{64,192},{96,224},{128,0},{160,32},{192,64},{224,... | collective-permute-start | bytes 393224 | tf_op jit(solution)/shard_map/ppermute | solution.py:661
  19.3 1.1 %collective-permute-start.3 = (f32[16,2048]{1,0:T(8,128)S(1)}, f32[16,2048]{1,0:T(8,128)S(1)}, u32[]{:S(2)}, u32[]{:S(2)}) collective-permute-start(f32[16,2048]{1,0:T(8,128)S(1)} %get-tuple-element.35), channel_id=1, source_target_pairs={{0,192},{32,224},{64,0},{96,32},{128,64},{160,96},{192,128},{224,1... | collective-permute-start | bytes 393224 | tf_op jit(solution)/shard_map/ppermute | solution.py:661
  20.3 0.0 copy-done.2
  20.3 0.0 copy-done.7
  20.3 1.5 %coefs.1.refs_9_.refs_1_ = f32[64,128]{1,0:T(8,128)S(1)} custom-call(f32[2,128,128]{2,1,0:T(8,128)S(1)} %copy-done.2, f32[1,256]{1,0:T(1,128)S(1)} %bitcast.6, f32[8,128]{1,0:T(8,128)S(1)} %get-tuple-element.36.refs_2_), custom_call_target="tpu_custom_call" | custom-call | flops 100000000 | bytes 1000000 | tf_op jit(solution)/shard_map/coefs/pallas_call | solution.py:91
  21.9 0.0 collective-permute-done.1.refs_1_
  21.9 1.9 %collective-permute-done.2.refs_2_ = f32[16,2048]{1,0:T(8,128)S(1)} collective-permute-done((f32[16,2048]{1,0:T(8,128)S(1)}, f32[16,2048]{1,0:T(8,128)S(1)}, u32[]{:S(2)}, u32[]{:S(2)}) %collective-permute-start.2) | collective-permute-done | bytes 131104 | tf_op jit(solution)/shard_map/ppermute | solution.py:661
  23.8 0.5 collective-permute-done.3.refs_3_
  24.3 1.5 %section.1 = (f32[32,2048]{1,0:T(8,128)S(1)}, f32[32,2048]{1,0:T(8,128)S(1)}, f32[32,2048]{1,0:T(8,128)}) custom-call(f32[32,2048]{1,0:T(8,128)S(1)} %get-tuple-element.32.refs_0_, f32[16,2048]{1,0:T(8,128)S(1)} %collective-permute-done.1.refs_1_, f32[16,2048]{1,0:T(8,128)S(1)} %collective-permute-done.2.refs_2_, ...), custom_call_target="tpu_custom_call" | custom-call | flops 10000000 | bytes 1000000 | tf_op jit(solution)/shard_map/section/pallas_call | solution.py:91
  25.8 2.4 %collective-permute-start.4 = (f32[32,2048]{1,0:T(8,128)S(1)}, f32[32,2048]{1,0:T(8,128)S(1)}, u32[]{:S(2)}, u32[]{:S(2)}) collective-permute-start(f32[32,2048]{1,0:T(8,128)S(1)} %get-tuple-element.44), channel_id=1, source_target_pairs={{0,1},{1,0},{2,3},{3,2},{4,5},{5,4},{6,7},{7,6},{8,9},{9,8},{10,11... | collective-permute-start | bytes 786440 | tf_op jit(solution)/shard_map/ppermute | solution.py:697
  28.2 1.2 %collective-permute-done.4.recv_ref = f32[32,2048]{1,0:T(8,128)S(1)} collective-permute-done((f32[32,2048]{1,0:T(8,128)S(1)}, f32[32,2048]{1,0:T(8,128)S(1)}, u32[]{:S(2)}, u32[]{:S(2)}) %collective-permute-start.4) | collective-permute-done | bytes 262176 | tf_op jit(solution)/shard_map/ppermute | solution.py:697
  29.3 1.2 %pack.1 = (f32[16,32,128]{2,1,0:T(8,128)}, f32[32,2048]{1,0:T(8,128)S(1)}) custom-call(f32[32,2048]{1,0:T(8,128)S(1)} %get-tuple-element.43.keep_ref, f32[32,2048]{1,0:T(8,128)S(1)} %collective-permute-done.4.recv_ref, f32[2,128,128]{2,1,0:T(8,128)S(1)} %copy-done.2, f32[1,256]{1,0:T(1,128)S(1)} %bitcast.8), custom_call_target="tpu_custom_call" | custom-call | flops 1000000 | bytes 1000000 | tf_op jit(solution)/shard_map/pack/pallas_call | solution.py:698
  30.6 9.2 %all-to-all-start = ((f32[16,32,128]{2,1,0:T(8,128)}), f32[16,32,128]{2,1,0:T(8,128)S(1)}, u32[]{:S(2)}, u32[]{:S(2)}) async-start(f32[16,32,128]{2,1,0:T(8,128)} %get-tuple-element.45), calls=%async_computation | async-start | bytes 524288 | tf_op jit(solution)/shard_map/all_to_all | solution.py:705
  39.8 5.5 %reduced.1 = (bf16[16,128,256]{2,1,0:T(8,128)(2,1)}, bf16[16,128,256]{2,1,0:T(8,128)(2,1)}, bf16[32,2048]{1,0:T(8,128)(2,1)}, bf16[32,2048]{1,0:T(8,128)(2,1)}, f32[8,128]{1,0:T(8,128)S(1)}) custom-call(f32[16,128,128]{2,1,0:T(8,128)} %g_ref.1, f32[1,2048]{1,0:T(1,128)} %bitcast.18), custom_call_target="tpu_custom_call" | custom-call | flops 1000000000 | bytes 2000000 | tf_op jit(solution)/shard_map/reduced/pallas_call | solution.py:610
  45.2 5.5 %all-to-all-done.refs_0_ = f32[16,32,128]{2,1,0:T(8,128)S(1)} async-done(((f32[16,32,128]{2,1,0:T(8,128)}), f32[16,32,128]{2,1,0:T(8,128)S(1)}, u32[]{:S(2)}, u32[]{:S(2)}) %all-to-all-start) | async-done | bytes 262176 | tf_op jit(solution)/shard_map/all_to_all | solution.py:705
  50.8 0.8 %scan_z.1 = f32[16,32,128]{2,1,0:T(8,128)} custom-call(f32[16,32,128]{2,1,0:T(8,128)S(1)} %all-to-all-done.refs_0_, f32[64,128]{1,0:T(8,128)S(1)} %coefs.1.refs_9_.refs_1_, f32[8,128]{1,0:T(8,128)S(1)} %get-tuple-element.46.refs_2_), custom_call_target="tpu_custom_call" | custom-call | flops 1000000 | bytes 1000000 | tf_op jit(solution)/shard_map/scan_z/pallas_call | solution.py:91
  51.5 3.5 %all-to-all-start.1 = ((f32[16,32,128]{2,1,0:T(8,128)}), f32[16,32,128]{2,1,0:T(8,128)S(1)}, u32[]{:S(2)}, u32[]{:S(2)}) async-start(f32[16,32,128]{2,1,0:T(8,128)} %scan_z.1), calls=%async_computation.1 | async-start | bytes 524288 | tf_op jit(solution)/shard_map/all_to_all | solution.py:710
  55.1 0.0 copy-start.3
  55.1 0.0 copy-start.8
  55.1 0.0 copy-start
  55.1 0.0 copy-start.1
  55.1 0.0 copy-start.5
  55.1 0.0 copy-start.6
  55.1 8.3 %inner.1 = (f32[8,32,2048]{2,1,0:T(8,128)}, f32[8,128]{1,0:T(8,128)S(1)}) custom-call(f32[256,2048]{1,0:T(8,128)} %get-tuple-element.29.l_ref, f32[32,2048]{1,0:T(8,128)} %get-tuple-element.37.y_ref, f32[8,32,2048]{2,1,0:T(8,128)} %u_ref.1, f32[2,128,128]{2,1,0:T(8,128)} %gy_ref.3, f32[1,256]{1,0:T(1,128)} %bitcast.13, f32[2,128,128]{2,1,0:T(8,128)} %gz_ref.7, ...), custom_call_target="tpu_custom_call" | custom-call | flops 1258291200 | bytes 8388608 | tf_op jit(solution)/shard_map/inner/pallas_call | solution.py:711
  63.5 1.2 %all-to-all-done.1.refs_0_ = f32[16,32,128]{2,1,0:T(8,128)S(1)} async-done(((f32[16,32,128]{2,1,0:T(8,128)}), f32[16,32,128]{2,1,0:T(8,128)S(1)}, u32[]{:S(2)}, u32[]{:S(2)}) %all-to-all-start.1) | async-done | bytes 262176 | tf_op jit(solution)/shard_map/all_to_all | solution.py:710
  64.7 0.0 copy-done.3
  64.7 0.0 copy-done.8
  64.7 0.4 unpack.1
  65.2 3.5 %collective-permute-start.5 = (f32[32,2048]{1,0:T(8,128)S(1)}, f32[32,2048]{1,0:T(8,128)S(1)}, u32[]{:S(2)}, u32[]{:S(2)}) collective-permute-start(f32[32,2048]{1,0:T(8,128)S(1)} %get-tuple-element.50), channel_id=1, source_target_pairs={{0,1},{1,0},{2,3},{3,2},{4,5},{5,4},{6,7},{7,6},{8,9},{9,8},{10,11... | collective-permute-start | bytes 786440 | tf_op jit(solution)/shard_map/ppermute | solution.py:732
  68.7 1.2 %collective-permute-done.5.got_ref = f32[32,2048]{1,0:T(8,128)S(1)} collective-permute-done((f32[32,2048]{1,0:T(8,128)S(1)}, f32[32,2048]{1,0:T(8,128)S(1)}, u32[]{:S(2)}, u32[]{:S(2)}) %collective-permute-start.5) | collective-permute-done | bytes 262176 | tf_op jit(solution)/shard_map/ppermute | solution.py:732
  69.8 0.0 copy-done
  69.8 0.0 copy-done.1
  69.8 0.0 copy-done.5
  69.8 0.0 copy-done.6
  69.8 3.6 %final.1 = f32[8,32,2048]{2,1,0:T(8,128)} custom-call(f32[8,32,2048]{2,1,0:T(8,128)} %get-tuple-element.42.s_hbm, f32[32,2048]{1,0:T(8,128)S(1)} %get-tuple-element.49.own_ref, f32[32,2048]{1,0:T(8,128)S(1)} %collective-permute-done.5.got_ref, f32[2,128,128]{2,1,0:T(8,128)S(1)} %copy-done.3, f32[1,256]{1,0:T(1,128)S(1)} %bitcast.10, ...), custom_call_target="tpu_custom_call", output_to_operand_aliasing={{}: (0, {})} | custom-call | flops 6291456 | bytes 4194304 | tf_op jit(solution)/shard_map/final/pallas_call | solution.py:733
Async XLA Ops:
  5.1 9.5 %collective-permute-start = (f32[32,2048]{1,0:T(8,128)S(1)}, f32[32,2048]{1,0:T(8,128)S(1)}, u32[]{:S(2)}, u32[]{:S(2)}) collective-permute-start(f32[32,2048]{1,0:T(8,128)S(1)} %get-tuple-element.30.refs_0_), channel_id=1, source_target_pairs={{0,32},{32,0},{64,96},{96,64},{128,160},{160,128},{192,224},{224,1... | collective-permute-start | bytes 786440 | tf_op jit(solution)/shard_map/ppermute | solution.py:607
  8.8 5.9 %copy-start.4 = (f32[2,128,128]{2,1,0:T(8,128)S(1)}, f32[2,128,128]{2,1,0:T(8,128)}, u32[]{:S(2)}) copy-start(f32[2,128,128]{2,1,0:T(8,128)} %gy_ref.3) | copy-start | bytes 393220
  8.8 5.9 %copy-start.9 = (f32[256]{0:T(256)S(1)}, f32[256]{0:T(256)}, u32[]{:S(2)}) copy-start(f32[256]{0:T(256)} %param.11) | copy-start | bytes 3076
  8.8 11.5 %copy-start.2 = (f32[2,128,128]{2,1,0:T(8,128)S(1)}, f32[2,128,128]{2,1,0:T(8,128)}, u32[]{:S(2)}) copy-start(f32[2,128,128]{2,1,0:T(8,128)} %gz_ref.7) | copy-start | bytes 393220
  8.8 11.5 %copy-start.7 = (f32[256]{0:T(256)S(1)}, f32[256]{0:T(256)}, u32[]{:S(2)}) copy-start(f32[256]{0:T(256)} %param.12) | copy-start | bytes 3076
  15.2 6.7 %collective-permute-start.1 = (f32[16,2048]{1,0:T(8,128)S(1)}, f32[16,2048]{1,0:T(8,128)S(1)}, u32[]{:S(2)}, u32[]{:S(2)}) collective-permute-start(f32[16,2048]{1,0:T(8,128)S(1)} %get-tuple-element.33), channel_id=1, source_target_pairs={{0,64},{32,96},{64,128},{96,160},{128,192},{160,224},{192,0},{224,... | collective-permute-start | bytes 393224 | tf_op jit(solution)/shard_map/ppermute | solution.py:661
  16.6 7.1 %collective-permute-start.2 = (f32[16,2048]{1,0:T(8,128)S(1)}, f32[16,2048]{1,0:T(8,128)S(1)}, u32[]{:S(2)}, u32[]{:S(2)}) collective-permute-start(f32[16,2048]{1,0:T(8,128)S(1)} %get-tuple-element.34), channel_id=1, source_target_pairs={{0,128},{32,160},{64,192},{96,224},{128,0},{160,32},{192,64},{224,... | collective-permute-start | bytes 393224 | tf_op jit(solution)/shard_map/ppermute | solution.py:661
  19.3 5.0 %collective-permute-start.3 = (f32[16,2048]{1,0:T(8,128)S(1)}, f32[16,2048]{1,0:T(8,128)S(1)}, u32[]{:S(2)}, u32[]{:S(2)}) collective-permute-start(f32[16,2048]{1,0:T(8,128)S(1)} %get-tuple-element.35), channel_id=1, source_target_pairs={{0,192},{32,224},{64,0},{96,32},{128,64},{160,96},{192,128},{224,1... | collective-permute-start | bytes 393224 | tf_op jit(solution)/shard_map/ppermute | solution.py:661
  25.8 3.6 %collective-permute-start.4 = (f32[32,2048]{1,0:T(8,128)S(1)}, f32[32,2048]{1,0:T(8,128)S(1)}, u32[]{:S(2)}, u32[]{:S(2)}) collective-permute-start(f32[32,2048]{1,0:T(8,128)S(1)} %get-tuple-element.44), channel_id=1, source_target_pairs={{0,1},{1,0},{2,3},{3,2},{4,5},{5,4},{6,7},{7,6},{8,9},{9,8},{10,11... | collective-permute-start | bytes 786440 | tf_op jit(solution)/shard_map/ppermute | solution.py:697
  30.6 20.2 %all-to-all-start = ((f32[16,32,128]{2,1,0:T(8,128)}), f32[16,32,128]{2,1,0:T(8,128)S(1)}, u32[]{:S(2)}, u32[]{:S(2)}) async-start(f32[16,32,128]{2,1,0:T(8,128)} %get-tuple-element.45), calls=%async_computation | async-start | bytes 524288 | tf_op jit(solution)/shard_map/all_to_all | solution.py:705
  51.5 13.2 %all-to-all-start.1 = ((f32[16,32,128]{2,1,0:T(8,128)}), f32[16,32,128]{2,1,0:T(8,128)S(1)}, u32[]{:S(2)}, u32[]{:S(2)}) async-start(f32[16,32,128]{2,1,0:T(8,128)} %scan_z.1), calls=%async_computation.1 | async-start | bytes 524288 | tf_op jit(solution)/shard_map/all_to_all | solution.py:710
  55.1 9.6 %copy-start.3 = (f32[2,128,128]{2,1,0:T(8,128)S(1)}, f32[2,128,128]{2,1,0:T(8,128)}, u32[]{:S(2)}) copy-start(f32[2,128,128]{2,1,0:T(8,128)} %gz_ref.7) | copy-start | bytes 393220
  55.1 9.6 %copy-start.8 = (f32[256]{0:T(256)S(1)}, f32[256]{0:T(256)}, u32[]{:S(2)}) copy-start(f32[256]{0:T(256)} %param.12) | copy-start | bytes 3076
  55.1 14.7 %copy-start = (bf16[16,128,256]{2,1,0:T(8,128)(2,1)S(1)}, bf16[16,128,256]{2,1,0:T(8,128)(2,1)}, u32[]{:S(2)}) copy-start(bf16[16,128,256]{2,1,0:T(8,128)(2,1)} %get-tuple-element.38.wh_ref) | copy-start | bytes 3145732
  55.1 14.7 %copy-start.1 = (bf16[16,128,256]{2,1,0:T(8,128)(2,1)S(1)}, bf16[16,128,256]{2,1,0:T(8,128)(2,1)}, u32[]{:S(2)}) copy-start(bf16[16,128,256]{2,1,0:T(8,128)(2,1)} %get-tuple-element.39.wl_ref) | copy-start | bytes 3145732
  55.1 14.7 %copy-start.5 = (bf16[32,2048]{1,0:T(8,128)(2,1)S(1)}, bf16[32,2048]{1,0:T(8,128)(2,1)}, u32[]{:S(2)}) copy-start(bf16[32,2048]{1,0:T(8,128)(2,1)} %get-tuple-element.40.bh_ref) | copy-start | bytes 393220
  55.1 14.7 %copy-start.6 = (bf16[32,2048]{1,0:T(8,128)(2,1)S(1)}, bf16[32,2048]{1,0:T(8,128)(2,1)}, u32[]{:S(2)}) copy-start(bf16[32,2048]{1,0:T(8,128)(2,1)} %get-tuple-element.41.bl_ref) | copy-start | bytes 393220
  65.2 4.7 %collective-permute-start.5 = (f32[32,2048]{1,0:T(8,128)S(1)}, f32[32,2048]{1,0:T(8,128)S(1)}, u32[]{:S(2)}, u32[]{:S(2)}) collective-permute-start(f32[32,2048]{1,0:T(8,128)S(1)} %get-tuple-element.50), channel_id=1, source_target_pairs={{0,1},{1,0},{2,3},{3,2},{4,5},{5,4},{6,7},{7,6},{8,9},{9,8},{10,11... | collective-permute-start | bytes 786440 | tf_op jit(solution)/shard_map/ppermute | solution.py:732
